TPU v7x, 256 devices: a whole 4x4x8 slice. The times are simulated.
256 devices in a mesh: layout: 16 (over y, x), rep: 16 (over z, core).
Axes of the slice: x: 4, y: 4, z: 8, core: 2. Of those that a mesh axis runs over, the one named last changes fastest.
Arguments:
- amplitudes: bfloat16 [48, 1024, 8192], P('rep', 'layout'), may hold values from -6 to 6
- integrals: bfloat16 [48, 1024, 2048], P('rep', None, 'layout'), may hold values from -0.0390625 to 0.0390625
- amp_mask: int32 [4, 8], replicated, may hold values 0 or 1
- int_mask: int32 [8, 4], replicated, may hold values 0 or 1
- occ_row: float32 [16], replicated, may hold values from -1.5 to -0.2
- occ_col: float32 [4], replicated, may hold values from -1.5 to -0.2
- vir_energy: float32 [4, 128], replicated, may hold values from 0.2 to 2
Outputs:
- update: bfloat16 [8192, 2048], P('layout', 'rep')
All inputs are finite; a program needn't handle non-finite values.
Results may differ from a plain program's by a relative error of at most 0.001.
Values may be sent and summed in bfloat16 or wider, within the bound.
No kernel may reach another device: no remote copies, remote signals or barrier semaphores. Data moves between devices by JAX's collectives and lax.ppermute only.
A program may use at most 256 MiB of HBM per device.

v0:
```python
import jax
import jax.numpy as jnp
from jax import lax
from jax.sharding import PartitionSpec as P

VB = 128
IW = 16
JW = 4


def pick_rows(lookup, positions):
    matches = positions[:, None] == jnp.arange(lookup.shape[0])[None, :]
    return jnp.sum(
        jnp.where(matches[:, :, None], lookup[None], jnp.zeros_like(lookup[None])), axis=1
    )


def full_product(left_side, right_side):
    return jnp.einsum("kcr,kcn->rn", left_side, right_side, preferred_element_type=jnp.float32)


def energy_line(first_block, block_count, window, occupied, virtual):
    block_ids = first_block + jnp.arange(block_count)
    occ_part = pick_rows(occupied[:, None], block_ids % window)
    vir_part = pick_rows(virtual, block_ids // window)
    return (vir_part - occ_part).reshape(-1)


def local(amplitudes, integrals, amp_mask, int_mask, occ_row, occ_col, vir_energy):
    layout_index = lax.axis_index("layout")
    layout_count = lax.axis_size("layout")
    rep_index = lax.axis_index("rep")
    k_slab, inner_slab, row_total = amplitudes.shape
    inner_total = integrals.shape[1]
    col_slab = integrals.shape[2]
    rows_here = row_total // layout_count
    row_index = jnp.arange(row_total)
    inner_index = layout_index * inner_slab + jnp.arange(inner_slab)
    row_table = pick_rows(amp_mask, row_index // (IW * VB))
    amp_keep = pick_rows(row_table.T, inner_index // VB)
    masked_amp = amplitudes * amp_keep.astype(jnp.bfloat16)[None]
    col_index = layout_index * col_slab + jnp.arange(col_slab)
    inner_table = pick_rows(int_mask, jnp.arange(inner_total) // VB)
    int_keep = pick_rows(inner_table.T, col_index // (JW * VB)).T
    masked_int = integrals * int_keep.astype(jnp.bfloat16)[None]
    regrouped = lax.all_to_all(masked_amp, "layout", split_axis=2, concat_axis=1, tiled=True)
    partials = full_product(regrouped, lax.all_gather(masked_int, "layout", axis=2, tiled=True))
    cycle_sum = lax.psum_scatter(partials, "rep", scatter_dimension=1, tiled=True)
    cols_here = cycle_sum.shape[1]
    row_energy = energy_line(
        layout_index * (rows_here // VB), rows_here // VB, IW, occ_row, vir_energy
    )
    col_energy = energy_line(
        rep_index * (cols_here // VB), cols_here // VB, JW, occ_col, vir_energy
    )
    denominator = -(row_energy[:, None] + col_energy[None, :])
    return (cycle_sum / denominator).astype(jnp.bfloat16)


def solution(mesh):
    placed = (P("rep", "layout", None), P("rep", None, "layout"), P(), P(), P(), P(), P())
    return jax.shard_map(
        local, mesh=mesh, in_specs=placed, out_specs=P("layout", "rep"), check_vma=False
    )
```

profile of v0, /device:TPU:32, one launch (start us, length us, event | category | flops | bytes accessed | tf_op | source)
XLA Modules:
  0.0 230.3 jit_solution(12605301808773910582)
XLA Ops:
  6.5 0.0 copy-start
  6.5 0.0 all-gather.2.cloned.1.call-start
  6.6 0.9 select_reduce_fusion.3
  7.5 0.2 select_reduce_fusion.1
  7.8 0.8 copy.24
  8.6 2.1 broadcast_multiply_fusion.1
  10.8 0.0 all-gather.2.cloned.1.call-update
  10.8 0.0 copy-start.2
  10.8 0.0 reduce-scatter.2.cloned.1.call-start
  10.8 0.0 copy-done
  10.9 8.5 %copy.21 = bf16[3,64,8192]{1,0,2:T(4,128)(2,1)} copy(bf16[3,64,8192]{2,1,0:T(8,128)(2,1)S(1)} %copy-done) | data formatting | bytes 6291456 | tf_op args[0]
  19.4 0.0 copy-done.2
  19.4 0.2 select_reduce_fusion.2
  19.6 0.1 iota_compare_fusion.2
  19.7 6.4 %select_reduce_fusion = s32[64,8192]{1,0:T(8,128)S(1)} fusion(s32[8,8192]{1,0:T(8,128)S(1)} %bitcast.23, pred[64,8]{1,0:T(8,128)(4,1)S(1)} %iota_compare_fusion.2), kind=kLoop, calls=%fused_computation | loop fusion | flops 7864320 | bytes 2359808 | tf_op jit(solution)/shard_map/reduce_sum | solution.py:13
  26.1 0.1 convert_element_type.16
  26.2 1.1 copy.20
  27.3 10.6 %fusion.7 = bf16[8192,3,64]{2,1,0:T(4,128)(2,1)} fusion(bf16[3,64,8192]{1,0,2:T(4,128)(2,1)} %copy.21, bf16[64,8192]{0,1:T(8,128)(2,1)S(1)} %copy.20), kind=kLoop, calls=%fused_computation.51 | loop fusion | flops 1572864 | bytes 7340032
  37.9 11.9 %reshape.311 = bf16[16,2,49152]{2,1,0:T(2,128)(2,1)S(1)} reshape(bf16[8192,3,64]{2,1,0:T(4,128)(2,1)} %fusion.7) | data formatting | bytes 6291456
  49.8 63.6 %all_to_all.18 = bf16[16,2,49152]{2,1,0:T(2,128)(2,1)} all-to-all(bf16[16,2,49152]{2,1,0:T(2,128)(2,1)S(1)} %reshape.311), channel_id=1, replica_groups=mesh['layout'=16,'rep'=16] {'layout'}, dimensions={0} | all-to-all | bytes 6291456 | tf_op jit(solution)/shard_map/all_to_all | solution.py:46
  113.4 13.1 %reshape.312 = bf16[8192,3,64]{2,1,0:T(4,128)(2,1)} reshape(bf16[16,2,49152]{2,1,0:T(2,128)(2,1)} %all_to_all.18) | data formatting | bytes 6291456
  126.5 10.7 %copy.28 = bf16[3,64,16,512]{3,1,2,0:T(8,128)(2,1)S(1)} copy(bf16[3,64,16,512]{1,0,3,2:T(4,128)(2,1)} %bitcast.21) | data formatting | bytes 6291456 | tf_op jit(solution)/shard_map/all_to_all | solution.py:46
  137.2 13.3 %all-gather.2.cloned.1.call-done = bf16[3,1024,2048]{2,1,0:T(8,128)(2,1)} async-done(((bf16[3,1024,128]{2,1,0:T(8,128)(2,1)}), bf16[3,1024,2048]{2,1,0:T(8,128)(2,1)}) %all-gather.2.cloned.1.call-update) | async-done | bytes 12582928 | tf_op jit(solution)/shard_map/all_gather | solution.py:47
  150.6 11.0 %convolution_bitcast_fusion = f32[512,2048]{1,0:T(8,128)} fusion(bf16[3,1024,512]{2,1,0:T(8,128)(2,1)S(1)} %bitcast.22, bf16[3,1024,2048]{2,1,0:T(8,128)(2,1)} %all-gather.2.cloned.1.call-done), kind=kOutput, calls=%fused_computation.2 | convolution fusion | flops 6442450944 | bytes 19922944 | tf_op jit(solution)/shard_map/kcr,kcn->rn/dot_general | solution.py:19
  161.5 0.0 copy-start.3
  161.5 0.0 copy-start.4
  161.5 0.0 copy-start.1
  161.5 0.0 reduce-scatter.2.cloned.1.call-update
  161.6 0.6 copy-done.3
  162.2 0.6 fusion.6
  162.8 0.0 copy-done.4
  162.8 0.2 select_reduce_fusion.6
  163.0 0.0 copy-done.1
  163.0 0.1 select_reduce_fusion.5
  163.0 0.1 iota_compare_fusion.4
  163.1 0.1 select_reduce_fusion.4
  163.2 0.6 broadcast_subtract_fusion
  163.9 0.1 subtract_bitcast_fusion
  163.9 57.8 %reduce-scatter.2.cloned.1.call-done = f32[512,128]{1,0:T(8,128)} async-done(((f32[512,2048]{1,0:T(8,128)}), f32[512,128]{1,0:T(8,128)}) %reduce-scatter.2.cloned.1.call-update) | async-done | bytes 262160 | tf_op jit(solution)/shard_map/reduce_scatter | solution.py:48
  221.7 1.7 divide_convert_fusion
  (10 shorter events, 0.1 us)
Async XLA Ops:
  6.5 4.3 %copy-start = (bf16[3,64,8192]{2,1,0:T(8,128)(2,1)S(1)}, bf16[3,64,8192]{2,1,0:T(8,128)(2,1)}, u32[]{:S(2)}) copy-start(bf16[3,64,8192]{2,1,0:T(8,128)(2,1)} %param.7) | copy-start | bytes 9437188
  6.5 144.0 %all-gather.2.cloned.1.call-start = ((), (), s32[]{:S(2)}) async-start(), calls=%async_computation.2 | async-start | bytes 13369344 | tf_op jit(solution)/shard_map/all_gather | solution.py:47
  10.8 8.6 %copy-start.2 = (s32[4,8]{1,0:T(4,128)S(1)}, s32[4,8]{1,0:T(4,128)}, u32[]{:S(2)}) copy-start(s32[4,8]{1,0:T(4,128)} %param.9) | copy-start | bytes 388
  10.8 210.9 %reduce-scatter.2.cloned.1.call-start = ((), (), s32[]{:S(2)}) async-start(), calls=%async_computation.3 | async-start | bytes 4456448 | tf_op jit(solution)/shard_map/reduce_scatter | solution.py:48
  161.5 0.7 copy-start.3
  161.5 1.3 copy-start.4
  161.5 1.4 copy-start.1
Sparse Core Ops, SparseCore 0:
  10.9 139.6 all-gather.1
  161.7 59.9 reduce-scatter.1
where the time goes:
time: 235 us; the launch traced here: 230 us
  waiting for transfers between devices  71.1 us (30%)
  blocking collectives  63.6 us (27%)
  local copies, waits for them, and re-layouts  46.8 us (20%)
  other arithmetic  24.3 us (10%)
  between operations  13.6 us (6%)
  matrix products  11 us (5%)
    all_to_all x1, blocking collectives, local(): lax.all_to_all(masked_amp, 'layout', split_axis=2, concat_axis=1, tiled=T...  63.6 us
    reduce_scatter x1, waiting for transfers between devices, local(): lax.psum_scatter(partials, 'rep', scatter_dimension=1, tiled=True)  57.8 us
    unnamed x13, local copies, waits for them, and re-layouts  34.1 us
    all_gather x1, waiting for transfers between devices, local(): lax.all_gather(masked_int, 'layout', axis=2, tiled=True)  13.3 us
    dot_general x1, matrix products, full_product(): jnp.einsum('kcr,kcn->rn', left_side, right_side, preferred_element_type=j...  11 us
    all_to_all x1, local copies, waits for them, and re-layouts, local(): lax.all_to_all(masked_amp, 'layout', split_axis=2, concat_axis=1, tiled=T...  10.7 us
    unnamed x1, other arithmetic  10.6 us
    reduce_sum x8, other arithmetic, pick_rows(): jnp.sum(jnp.where(matches[:, :, None], lookup[None], jnp.zeros_like(looku...  8.68 us
  transfers between devices with their start and end apart: 2, of which 2 were waited for; matrix products, arithmetic and copies ran while one was open for 28% of the time, Pallas kernels for 0%

commit v1 on v0

v1 whole, which is shorter than its diff:
```python
import jax
import jax.numpy as jnp
from jax import lax
from jax.experimental import pallas as pl
from jax.experimental.pallas import tpu as pltpu
from jax.sharding import Mesh, PartitionSpec as P

AXES = ("y", "x", "z", "core")
NY, NX, NZ, NC = 4, 4, 8, 2
KD = 192
RB = 512
KT = 16 * KD
VMEM = pltpu.MemorySpace.VMEM
SMEM = pltpu.MemorySpace.SMEM


def pairs(to):
    out = []
    for y in range(NY):
        for x in range(NX):
            for z in range(NZ):
                for c in range(NC):
                    ty, tx, tz, tc = to(y, x, z, c)
                    src = ((y * NX + x) * NZ + z) * NC + c
                    dst = ((ty % NY * NX + tx % NX) * NZ + tz % NZ) * NC + tc % NC
                    out.append((src, dst))
    return out


UP = pairs(lambda y, x, z, c: (y + 1, x, z, c))
DOWN = pairs(lambda y, x, z, c: (y - 1, x, z, c))
OVER = pairs(lambda y, x, z, c: (y + 2, x, z, c))
PARTNER = pairs(lambda y, x, z, c: (y, 3 - x, z, c))
CROSS = pairs(lambda y, x, z, c: (y, x ^ 1, z, c))
ACROSS = pairs(lambda y, x, z, c: (y, x + 2, z, c))
SWAP = pairs(lambda y, x, z, c: (y, x, z, 1 - c))


def slab_of(y, x, z):
    turn = (z // 2 == 1) * 3 + (z // 2 == 2) * 1 + (z // 2 == 3) * 2
    return (y + turn) % 4, x ^ (z % 2)


def home(y, x, z, c):
    col_y, col_x = slab_of(y, x, z)
    return y, x if c == 0 else 3 - x, 2 * col_y + col_x // 2, col_x % 2


HOME = pairs(home)


def send(value, where):
    return lax.ppermute(value, AXES, where)


def prepare_kernel(place, amp_mask, int_mask, a, b, own, near, up, down, over, scratch):
    y, x = place[0], place[1]
    block_q = 2 * y + x // 2
    low = jnp.minimum(x, 3 - x)
    for to_y, first, second in (
        (y, own, None),
        (lax.rem(y + 1, 4), up.at[0], up.at[1]),
        (lax.rem(y + 3, 4), down.at[0], down.at[1]),
        (lax.rem(y + 2, 4), over.at[0], over.at[1]),
    ):
        keep = amp_mask[to_y, block_q].astype(jnp.float32).astype(jnp.bfloat16)
        for dst, lo in ((first, low), (second, 1 - low)):
            for half in range(2):
                to_x = lo if half == 0 else 3 - lo
                start = pl.multiple_of((to_y * 4 + to_x) * RB, RB)
                for k in range(3):
                    value = a[k, :, pl.ds(start, RB)] * keep
                    if dst is None:
                        near[pl.ds(128, 64), pl.ds((2 * k + half) * RB, RB)] = value
                    else:
                        dst[pl.ds(k * 64, 64), pl.ds(half * RB, RB)] = value
    for slab in range(16):
        keep = int_mask[slab // 2, y].astype(jnp.float32).astype(jnp.bfloat16)
        at = ((slab % 4) * 4 + slab // 4) * KD
        for k in range(3):
            scratch[pl.ds(at + k * 64, 64), :] = b[k, pl.ds(slab * 64, 64), :] * keep
    for j in range(KT // 128):
        near[pl.ds(0, 128), pl.ds(j * 128, 128)] = scratch[pl.ds(j * 128, 128), :].T


def prepare(place, amp_mask, int_mask, a, b):
    piece = jax.ShapeDtypeStruct((KD, 2 * RB), jnp.bfloat16)
    two = jax.ShapeDtypeStruct((2, KD, 2 * RB), jnp.bfloat16)
    near = jax.ShapeDtypeStruct((KD, KT), jnp.bfloat16)
    smem = pl.BlockSpec(memory_space=SMEM)
    vmem = pl.BlockSpec(memory_space=VMEM)
    return pl.pallas_call(
        prepare_kernel,
        out_shape=(piece, near, two, two, two),
        in_specs=[smem, smem, smem, vmem, vmem],
        out_specs=(vmem,) * 5,
        scratch_shapes=[pltpu.VMEM((KT, 128), jnp.bfloat16)],
        compiler_params=pltpu.CompilerParams(vmem_limit_bytes=24 << 20),
        cost_estimate=pl.CostEstimate(flops=0, bytes_accessed=8 << 20, transcendentals=0),
        name="prepare",
    )(place, amp_mask, int_mask, a, b)


def gather_kernel(near, from_near, down, up, over, early, own_rest, oth_rest, oth_all, b_here):
    del early
    for j, ref in enumerate((down, up, over)):
        own_rest[j] = ref[0]
        oth_rest[j] = ref[1]
        oth_all[j] = ref[1]
    for k in range(3):
        oth_all[3, pl.ds(k * 64, 64), :] = near[pl.ds(128, 64), pl.ds(k * 2 * RB, 2 * RB)]
    b_here[pl.ds(0, 128), :] = near[pl.ds(0, 128), :]
    b_here[pl.ds(128, 128), :] = from_near[...]


def gather(near, from_near, down, up, over, early):
    def shape(n):
        return jax.ShapeDtypeStruct((n, KD, 2 * RB), jnp.bfloat16)

    vmem = pl.BlockSpec(memory_space=VMEM)
    return pl.pallas_call(
        gather_kernel,
        out_shape=(shape(3), shape(3), shape(4), jax.ShapeDtypeStruct((256, KT), jnp.bfloat16)),
        grid=(1,),
        in_specs=[
            vmem,
            pl.BlockSpec((128, KT), lambda i: (0, 0)),
            vmem,
            vmem,
            vmem,
            pl.BlockSpec(memory_space=pl.ANY),
        ],
        out_specs=(vmem,) * 4,
        compiler_params=pltpu.CompilerParams(vmem_limit_bytes=24 << 20),
        cost_estimate=pl.CostEstimate(flops=0, bytes_accessed=10 << 20, transcendentals=0),
        name="gather",
    )(near, from_near, down, up, over, early)


def arrange_kernel(place, half, s0, s1, s2, s3, p0, p1, c0, c1, x1, out):
    y, x = place[0], place[1]

    def put(ref, from_x, from_y):
        at = pl.multiple_of((from_x * 4 + from_y) * KD, KD)
        out[pl.ds(at, KD), :] = ref[...]

    around = (lax.rem(y + 3, 4), lax.rem(y + 1, 4), lax.rem(y + 2, 4))
    put(s0, x, y)
    for ref, from_y in zip((s1, s2, s3), around):
        put(ref.at[0], x, from_y)
    far = lax.rem(x + 2, 4)
    near = x + 1 - 2 * lax.rem(x, 2)
    put(p0, 3 - x, y)
    at = pl.multiple_of((near * 4 + y) * KD, KD)
    for k in range(3):
        start = pl.multiple_of(k * 2 * RB + half[0] * RB + pl.program_id(0) * 256, 256)
        out[pl.ds(at + k * 64, 64), :] = c0[:, pl.ds(start, 256)]
    put(x1.at[3], far, y)
    for late, from_x in ((p1, 3 - x), (c1, near), (x1, far)):
        for j, from_y in enumerate(around):
            put(late.at[j], from_x, from_y)


def arrange(place, half, amps):
    wide = 256

    def lanes(lead=None):
        if lead is None:
            return pl.BlockSpec((KD, wide), lambda i, pr, hr: (0, 2 * hr[0] + i))
        return pl.BlockSpec((lead, KD, wide), lambda i, pr, hr: (0, 0, 2 * hr[0] + i))

    specs = [lanes()] + [lanes(1)] * 3
    specs += [lanes(), lanes(3), pl.BlockSpec((64, KT), lambda i, pr, hr: (2, 0)), lanes(3), lanes(4)]
    return pl.pallas_call(
        arrange_kernel,
        out_shape=jax.ShapeDtypeStruct((KT, RB), jnp.bfloat16),
        grid_spec=pltpu.PrefetchScalarGridSpec(
            num_scalar_prefetch=2,
            grid=(RB // wide,),
            in_specs=specs,
            out_specs=pl.BlockSpec((KT, wide), lambda i, pr, hr: (0, i)),
        ),
        compiler_params=pltpu.CompilerParams(vmem_limit_bytes=24 << 20),
        cost_estimate=pl.CostEstimate(flops=0, bytes_accessed=6 << 20, transcendentals=0),
        name="arrange",
    )(place, half, *amps)


def product(place, half, amps, ints):
    right = arrange(place, half, amps)
    return [jnp.dot(left, right, preferred_element_type=jnp.float32) for left in ints]


def local(amplitudes, integrals, amp_mask, int_mask, occ_row, occ_col, vir_energy):
    y, x, z, core = (lax.axis_index(name) for name in AXES)
    place = jnp.stack([y, x]).astype(jnp.int32)
    own, near, up, down, over = prepare(place, amp_mask, int_mask, amplitudes, integrals)

    from_down = send(up, UP)
    from_up = send(down, DOWN)
    from_over = send(over, OVER)
    from_near = send(near, CROSS)
    p0 = send(own, PARTNER)

    own_rest, oth_rest, oth_all, b_here = gather(
        near, from_near, from_down, from_up, from_over, p0
    )
    b_down = send(b_here, UP)
    b_up = send(b_here, DOWN)
    p1 = send(own_rest, PARTNER)
    c1 = send(oth_rest, CROSS)
    x1 = send(oth_all, ACROSS)
    b_far0 = send(b_down[:128], UP)
    b_far1 = send(b_up[128:], DOWN)

    amps = (own, from_down, from_up, from_over, p0, p1, from_near, c1, x1)
    ints = (b_here, b_down, b_up, b_far0, b_far1)
    keep_half = jnp.bitwise_xor(x // 2, core).astype(jnp.int32)
    given = jnp.concatenate(product(place, (1 - keep_half)[None], amps, ints))
    taken = send(given, SWAP)
    kept = jnp.concatenate(product(place, keep_half[None], amps, ints))
    cycle_sum = lax.psum_scatter(
        (kept + taken).reshape(8, 128, RB), "z", scatter_dimension=0, tiled=True
    )[0]

    row_x = jnp.where(core == 0, x, 3 - x)
    row_occ = lax.dynamic_slice(occ_row, (4 * row_x,), (4,))
    row_vir = lax.dynamic_slice(vir_energy, (y, 0), (1, 128))
    row_energy = (row_vir - row_occ[:, None]).reshape(-1)
    col_y, col_x = slab_of(y, x, z)
    col_occ = lax.dynamic_slice(occ_col, (col_x,), (1,))
    col_energy = lax.dynamic_slice(vir_energy, (col_y, 0), (1, 128))[0] - col_occ
    denominator = -(row_energy[:, None] + col_energy[None, :])
    return send((cycle_sum.T / denominator).astype(jnp.bfloat16), HOME)


def solution(mesh):
    grid = Mesh(mesh.devices.reshape(NY, NX, NZ, NC), AXES)
    layout, rep = ("y", "x"), ("z", "core")
    placed = (P(rep, layout, None), P(rep, None, layout), P(), P(), P(), P(), P())
    return jax.shard_map(
        local, mesh=grid, in_specs=placed, out_specs=P(layout, rep), check_vma=False
    )
```

time: 235 us -> 211 us (0.90)
  the two profiles are of different devices: /device:TPU:32 before, /device:TPU:58 now
where the time goes in v1:
time: 211 us; the launch traced here: 210 us
  waiting for transfers between devices  137 us (65%)
  starting transfers between devices  21.3 us (10%)
  matrix products  16.7 us (8%)
  between operations  13.7 us (6%)
  local copies, waits for them, and re-layouts  10.6 us (5%)
  Pallas kernels  9.06 us (4%)
  other arithmetic  2.37 us (1%)
    ppermute x14, waiting for transfers between devices, send(): return lax.ppermute(value, AXES, where)  95.2 us
    reduce_scatter x1, waiting for transfers between devices, local(): lax.psum_scatter((kept + taken).reshape(8, 128, RB), 'z', scatter_dimensi...  41.4 us
    ppermute x14, starting transfers between devices, send(): return lax.ppermute(value, AXES, where)  21.3 us
    dot_general x10, matrix products, product(): jnp.dot(left, right, preferred_element_type=jnp.float32)  16.7 us
    unnamed x22, local copies, waits for them, and re-layouts  5.7 us
    pallas_call x2, Pallas kernels, arrange(): pl.pallas_call(arrange_kernel, out_shape=jax.ShapeDtypeStruct((KT, RB), j...  5.06 us
  transfers between devices with their start and end apart: 15, of which 8 were waited for; matrix products, arithmetic and copies ran while one was open for 9% of the time, Pallas kernels for 2%

profile of v1, /device:TPU:58, one launch (start us, length us, event | category | flops | bytes accessed | tf_op | source)
XLA Modules:
  0.0 210.3 jit_solution(8658344975726508042)
XLA Ops:
  6.5 0.8 copy.8.int_mask
  7.4 1.9 copy-done.2
  9.3 1.1 copy-done.5
  10.4 0.7 copy-done.6
  11.1 1.2 prepare.1
  12.3 0.6 collective-permute-start
  12.9 0.2 collective-permute-start.1
  13.1 1.8 collective-permute-start.2
  14.9 1.2 collective-permute-start.3
  16.2 2.2 %collective-permute-start.4 = (bf16[192,1024]{1,0:T(8,128)(2,1)S(1)}, bf16[192,1024]{1,0:T(8,128)(2,1)S(1)}, u32[]{:S(2)}, u32[]{:S(2)}) collective-permute-start(bf16[192,1024]{1,0:T(8,128)(2,1)S(1)} %get-tuple-element.18.s0), channel_id=1, source_target_pairs={{0,48},{1,49},{2,50},{3,51},{4,52},{5,53},{6,54},{7,55},{8,56},{9,... | collective-permute-start | bytes 1179656 | tf_op jit(solution)/shard_map/ppermute | solution.py:53
  18.3 8.0 %collective-permute-done.4.early.p0 = bf16[192,1024]{1,0:T(8,128)(2,1)S(1)} collective-permute-done((bf16[192,1024]{1,0:T(8,128)(2,1)S(1)}, bf16[192,1024]{1,0:T(8,128)(2,1)S(1)}, u32[]{:S(2)}, u32[]{:S(2)}) %collective-permute-start.4) | collective-permute-done | bytes 393248 | tf_op jit(solution)/shard_map/ppermute | solution.py:53
  26.3 7.1 %collective-permute-done.1.down.s1 = bf16[2,192,1024]{2,1,0:T(8,128)(2,1)S(1)} collective-permute-done((bf16[2,192,1024]{2,1,0:T(8,128)(2,1)S(1)}, bf16[2,192,1024]{2,1,0:T(8,128)(2,1)S(1)}, u32[]{:S(2)}, u32[]{:S(2)}) %collective-permute-start.1) | collective-permute-done | bytes 786464 | tf_op jit(solution)/shard_map/ppermute | solution.py:53
  33.4 16.6 %collective-permute-done.2.up.s2 = bf16[2,192,1024]{2,1,0:T(8,128)(2,1)S(1)} collective-permute-done((bf16[2,192,1024]{2,1,0:T(8,128)(2,1)S(1)}, bf16[2,192,1024]{2,1,0:T(8,128)(2,1)S(1)}, u32[]{:S(2)}, u32[]{:S(2)}) %collective-permute-start.2) | collective-permute-done | bytes 786464 | tf_op jit(solution)/shard_map/ppermute | solution.py:53
  50.0 2.8 %gather.1 = (bf16[3,192,1024]{2,1,0:T(8,128)(2,1)}, bf16[3,192,1024]{2,1,0:T(8,128)(2,1)}, bf16[4,192,1024]{2,1,0:T(8,128)(2,1)}, bf16[256,3072]{1,0:T(8,128)(2,1)}) custom-call(bf16[192,3072]{1,0:T(8,128)(2,1)S(1)} %get-tuple-element.14.near, bf16[192,3072]{1,0:T(8,128)(2,1)S(1)} %collective-permute-done.from_near.c0, ...), custom_call_target="tpu_custom_call" | custom-call | bytes 10485760 | tf_op jit(solution)/shard_map/gather/pallas_call | solution.py:121
  52.8 3.2 %collective-permute-start.8 = (bf16[256,3072]{1,0:T(8,128)(2,1)}, bf16[256,3072]{1,0:T(8,128)(2,1)}, u32[]{:S(2)}, u32[]{:S(2)}) collective-permute-start(bf16[256,3072]{1,0:T(8,128)(2,1)} %get-tuple-element.19), channel_id=1, source_target_pairs={{0,64},{1,65},{2,66},{3,67},{4,68},{5,69},{6,70},{7,71},{8,72},{9,... | collective-permute-start | bytes 4718600 | tf_op jit(solution)/shard_map/ppermute | solution.py:53
  56.0 2.4 %collective-permute-start.7 = (bf16[4,192,1024]{2,1,0:T(8,128)(2,1)}, bf16[4,192,1024]{2,1,0:T(8,128)(2,1)}, u32[]{:S(2)}, u32[]{:S(2)}) collective-permute-start(bf16[4,192,1024]{2,1,0:T(8,128)(2,1)} %get-tuple-element.22), channel_id=1, source_target_pairs={{0,32},{1,33},{2,34},{3,35},{4,36},{5,37},{6,38},{7,39},{8,40},{9,... | collective-permute-start | bytes 4718600 | tf_op jit(solution)/shard_map/ppermute | solution.py:53
  58.5 0.5 collective-permute-start.5
  59.0 1.7 collective-permute-start.6
  60.7 28.0 %collective-permute-done.9 = bf16[256,3072]{1,0:T(8,128)(2,1)} collective-permute-done((bf16[256,3072]{1,0:T(8,128)(2,1)}, bf16[256,3072]{1,0:T(8,128)(2,1)}, u32[]{:S(2)}, u32[]{:S(2)}) %collective-permute-start.9) | collective-permute-done | bytes 1572896 | tf_op jit(solution)/shard_map/ppermute | solution.py:53
  88.8 1.2 slice.9
  89.9 0.1 collective-permute-start.11
  90.0 1.2 slice.8
  91.2 3.5 %collective-permute-start.10 = (bf16[128,3072]{1,0:T(8,128)(2,1)S(1)}, bf16[128,3072]{1,0:T(8,128)(2,1)S(1)}, u32[]{:S(2)}, u32[]{:S(2)}) collective-permute-start(bf16[128,3072]{1,0:T(8,128)(2,1)S(1)} %slice.8), channel_id=1, source_target_pairs={{0,64},{1,65},{2,66},{3,67},{4,68},{5,69},{6,70},{7,71},{8,72},{9,... | collective-permute-start | bytes 2359304 | tf_op jit(solution)/shard_map/ppermute | solution.py:53
  94.7 22.3 %collective-permute-done.5.p1 = bf16[3,192,1024]{2,1,0:T(8,128)(2,1)} collective-permute-done((bf16[3,192,1024]{2,1,0:T(8,128)(2,1)}, bf16[3,192,1024]{2,1,0:T(8,128)(2,1)}, u32[]{:S(2)}, u32[]{:S(2)}) %collective-permute-start.5) | collective-permute-done | bytes 1179680 | tf_op jit(solution)/shard_map/ppermute | solution.py:53
  117.0 0.7 collective-permute-done.6.c1
  117.8 2.5 %arrange.3 = bf16[3072,512]{1,0:T(8,128)(2,1)S(1)} custom-call(s32[2]{0:T(128)S(1)} %pad_add_fusion.place, s32[1]{0:T(128)} %bitcast.3.half, bf16[192,1024]{1,0:T(8,128)(2,1)S(1)} %copy-done.4, bf16[2,192,1024]{2,1,0:T(8,128)(2,1)S(1)} %collective-permute-done.1.down.s1, bf16[2,192,1024]{2,1,0:T(8,128)(2,1)S(1)} %collective-permute-done.2.up.s2, ...), custom_call_target="tpu_custom_call" | custom-call | bytes 6291456 | tf_op jit(solution)/shard_map/arrange/pallas_call | solution.py:174
  120.3 2.4 %convolution_dynamic-update-slice_fusion.2 = f32[1024,512]{1,0:T(8,128)S(1)} fusion(bf16[256,3072]{1,0:T(8,128)(2,1)} %get-tuple-element.19, bf16[3072,512]{1,0:T(8,128)(2,1)S(1)} %arrange.3), kind=kOutput, calls=%fused_computation.2 | convolution fusion | flops 805306368 | bytes 5242880 | tf_op jit(solution)/shard_map/dot_general | solution.py:191
  122.7 2.4 %convolution_dynamic-update-slice_fusion.1 = f32[1024,512]{1,0:T(8,128)S(1)} fusion(f32[1024,512]{1,0:T(8,128)S(1)} %convolution_dynamic-update-slice_fusion.2, bf16[256,3072]{1,0:T(8,128)(2,1)} %collective-permute-done.8, bf16[3072,512]{1,0:T(8,128)(2,1)S(1)} %arrange.3), kind=kOutput, calls=%fused_computation.1 | convolution fusion | flops 805306368 | bytes 5242880 | tf_op jit(solution)/shard_map/dot_general | solution.py:191
  125.1 2.4 %convolution_dynamic-update-slice_fusion = f32[1024,512]{1,0:T(8,128)S(1)} fusion(f32[1024,512]{1,0:T(8,128)S(1)} %convolution_dynamic-update-slice_fusion.1, bf16[256,3072]{1,0:T(8,128)(2,1)} %collective-permute-done.9, bf16[3072,512]{1,0:T(8,128)(2,1)S(1)} %arrange.3), kind=kOutput, calls=%fused_computation | convolution fusion | flops 805306368 | bytes 5242880 | tf_op jit(solution)/shard_map/dot_general | solution.py:191
  127.5 0.6 convolution_dynamic-update-slice_fusion.7
  128.1 0.6 convolution_dynamic-update-slice_fusion.6
  128.7 0.1 collective-permute-start.12
  128.8 2.5 %arrange.2 = bf16[3072,512]{1,0:T(8,128)(2,1)S(1)} custom-call(s32[2]{0:T(128)S(1)} %pad_add_fusion.place, s32[1]{0:T(128)} %bitcast.2.half, bf16[192,1024]{1,0:T(8,128)(2,1)S(1)} %copy-done.4, bf16[2,192,1024]{2,1,0:T(8,128)(2,1)S(1)} %collective-permute-done.1.down.s1, bf16[2,192,1024]{2,1,0:T(8,128)(2,1)S(1)} %collective-permute-done.2.up.s2, ...), custom_call_target="tpu_custom_call" | custom-call | bytes 6291456 | tf_op jit(solution)/shard_map/arrange/pallas_call | solution.py:174
  131.4 2.4 %convolution_dynamic-update-slice_fusion.5 = f32[1024,512]{1,0:T(8,128)S(1)} fusion(bf16[256,3072]{1,0:T(8,128)(2,1)} %get-tuple-element.19, bf16[3072,512]{1,0:T(8,128)(2,1)S(1)} %arrange.2), kind=kOutput, calls=%fused_computation.5 | convolution fusion | flops 805306368 | bytes 5242880 | tf_op jit(solution)/shard_map/dot_general | solution.py:191
  133.7 2.4 %convolution_dynamic-update-slice_fusion.4 = f32[1024,512]{1,0:T(8,128)S(1)} fusion(f32[1024,512]{1,0:T(8,128)S(1)} %convolution_dynamic-update-slice_fusion.5, bf16[256,3072]{1,0:T(8,128)(2,1)} %collective-permute-done.8, bf16[3072,512]{1,0:T(8,128)(2,1)S(1)} %arrange.2), kind=kOutput, calls=%fused_computation.4 | convolution fusion | flops 805306368 | bytes 5242880 | tf_op jit(solution)/shard_map/dot_general | solution.py:191
  136.1 2.4 %convolution_dynamic-update-slice_fusion.3 = f32[1024,512]{1,0:T(8,128)S(1)} fusion(f32[1024,512]{1,0:T(8,128)S(1)} %convolution_dynamic-update-slice_fusion.4, bf16[256,3072]{1,0:T(8,128)(2,1)} %collective-permute-done.9, bf16[3072,512]{1,0:T(8,128)(2,1)S(1)} %arrange.2), kind=kOutput, calls=%fused_computation.3 | convolution fusion | flops 805306368 | bytes 5242880 | tf_op jit(solution)/shard_map/dot_general | solution.py:191
  138.5 0.6 convolution_dynamic-update-slice_fusion.9
  139.1 0.6 convolution_dynamic-update-slice_fusion.8
  139.8 0.5 add.50
  140.3 1.8 copy.9
  142.2 0.6 copy-done.8
  142.7 0.6 dynamic_slice.15
  143.4 0.7 dynamic-slice_bitcast_fusion
  144.1 41.4 %reduce-scatter.2.cloned.1.call-done = f32[1,128,512]{1,2,0:T(8,128)} async-done(((f32[8,128,512]{1,2,0:T(8,128)}), f32[1,128,512]{1,2,0:T(8,128)}) %reduce-scatter.2.cloned.1.call-update) | async-done | bytes 262160 | tf_op jit(solution)/shard_map/reduce_scatter | solution.py:222
  185.5 1.1 fusion
  186.6 3.6 %collective-permute-start.13 = (bf16[512,128]{1,0:T(8,128)(2,1)S(1)}, bf16[512,128]{1,0:T(8,128)(2,1)S(1)}, u32[]{:S(2)}, u32[]{:S(2)}) collective-permute-start(bf16[512,128]{1,0:T(8,128)(2,1)S(1)} %fusion), channel_id=1, source_target_pairs={{0,0},{1,48},{2,1},{3,49},{4,12},{5,60},{6,13},{7,61},{8,4},{9,52}... | collective-permute-start | bytes 393224 | tf_op jit(solution)/shard_map/ppermute | solution.py:53
  190.3 12.5 %collective-permute-done.13 = bf16[512,128]{1,0:T(8,128)(2,1)S(1)} collective-permute-done((bf16[512,128]{1,0:T(8,128)(2,1)S(1)}, bf16[512,128]{1,0:T(8,128)(2,1)S(1)}, u32[]{:S(2)}, u32[]{:S(2)}) %collective-permute-start.13) | collective-permute-done | bytes 131104 | tf_op jit(solution)/shard_map/ppermute | solution.py:53
  202.8 0.7 copy.19
  (29 shorter events, 0.3 us)
Async XLA Ops:
  6.5 179.0 %reduce-scatter.2.cloned.1.call-start = ((), (), s32[]{:S(2)}) async-start(), calls=%async_computation.1 | async-start | bytes 2359296 | tf_op jit(solution)/shard_map/reduce_scatter | solution.py:222
  7.4 1.9 copy-start.2
  9.3 1.1 copy-start.5
  10.4 0.7 copy-start.6
  12.3 40.5 %copy-start.3 = (bf16[192,1024]{1,0:T(8,128)(2,1)}, bf16[192,1024]{1,0:T(8,128)(2,1)S(1)}, u32[]{:S(2)}) copy-start(bf16[192,1024]{1,0:T(8,128)(2,1)S(1)} %get-tuple-element.18.s0) | copy-start | bytes 1179652
  12.3 37.7 %collective-permute-start = (bf16[192,3072]{1,0:T(8,128)(2,1)S(1)}, bf16[192,3072]{1,0:T(8,128)(2,1)S(1)}, u32[]{:S(2)}, u32[]{:S(2)}) collective-permute-start(bf16[192,3072]{1,0:T(8,128)(2,1)S(1)} %get-tuple-element.14.near), channel_id=1, source_target_pairs={{0,16},{1,17},{2,18},{3,19},{4,20},{5,21},{6,22},{7,23},{8,24},{9,... | collective-permute-start | bytes 3538952 | tf_op jit(solution)/shard_map/ppermute | solution.py:53
  12.9 20.5 %collective-permute-start.1 = (bf16[2,192,1024]{2,1,0:T(8,128)(2,1)S(1)}, bf16[2,192,1024]{2,1,0:T(8,128)(2,1)S(1)}, u32[]{:S(2)}, u32[]{:S(2)}) collective-permute-start(bf16[2,192,1024]{2,1,0:T(8,128)(2,1)S(1)} %get-tuple-element.15), channel_id=1, source_target_pairs={{0,64},{1,65},{2,66},{3,67},{4,68},{5,69},{6,70},{7,71},{8,72},{9,... | collective-permute-start | bytes 2359304 | tf_op jit(solution)/shard_map/ppermute | solution.py:53
  13.1 36.8 %collective-permute-start.2 = (bf16[2,192,1024]{2,1,0:T(8,128)(2,1)S(1)}, bf16[2,192,1024]{2,1,0:T(8,128)(2,1)S(1)}, u32[]{:S(2)}, u32[]{:S(2)}) collective-permute-start(bf16[2,192,1024]{2,1,0:T(8,128)(2,1)S(1)} %get-tuple-element.16), channel_id=1, source_target_pairs={{0,192},{1,193},{2,194},{3,195},{4,196},{5,197},{6,198},{7,199},{8... | collective-permute-start | bytes 2359304 | tf_op jit(solution)/shard_map/ppermute | solution.py:53
  14.9 35.0 %collective-permute-start.3 = (bf16[2,192,1024]{2,1,0:T(8,128)(2,1)S(1)}, bf16[2,192,1024]{2,1,0:T(8,128)(2,1)S(1)}, u32[]{:S(2)}, u32[]{:S(2)}) collective-permute-start(bf16[2,192,1024]{2,1,0:T(8,128)(2,1)S(1)} %get-tuple-element.17), channel_id=1, source_target_pairs={{0,128},{1,129},{2,130},{3,131},{4,132},{5,133},{6,134},{7,135},{8... | collective-permute-start | bytes 2359304 | tf_op jit(solution)/shard_map/ppermute | solution.py:53
  16.2 10.1 %collective-permute-start.4 = (bf16[192,1024]{1,0:T(8,128)(2,1)S(1)}, bf16[192,1024]{1,0:T(8,128)(2,1)S(1)}, u32[]{:S(2)}, u32[]{:S(2)}) collective-permute-start(bf16[192,1024]{1,0:T(8,128)(2,1)S(1)} %get-tuple-element.18.s0), channel_id=1, source_target_pairs={{0,48},{1,49},{2,50},{3,51},{4,52},{5,53},{6,54},{7,55},{8,56},{9,... | collective-permute-start | bytes 1179656 | tf_op jit(solution)/shard_map/ppermute | solution.py:53
  26.3 26.5 %copy-start = (bf16[192,1024]{1,0:T(8,128)(2,1)}, bf16[192,1024]{1,0:T(8,128)(2,1)S(1)}, u32[]{:S(2)}) copy-start(bf16[192,1024]{1,0:T(8,128)(2,1)S(1)} %collective-permute-done.4.early.p0) | copy-start | bytes 1179652
  52.8 36.0 %collective-permute-start.9 = (bf16[256,3072]{1,0:T(8,128)(2,1)}, bf16[256,3072]{1,0:T(8,128)(2,1)}, u32[]{:S(2)}, u32[]{:S(2)}) collective-permute-start(bf16[256,3072]{1,0:T(8,128)(2,1)} %get-tuple-element.19), channel_id=1, source_target_pairs={{0,192},{1,193},{2,194},{3,195},{4,196},{5,197},{6,198},{7,199},{8... | collective-permute-start | bytes 4718600 | tf_op jit(solution)/shard_map/ppermute | solution.py:53
  52.8 37.2 %collective-permute-start.8 = (bf16[256,3072]{1,0:T(8,128)(2,1)}, bf16[256,3072]{1,0:T(8,128)(2,1)}, u32[]{:S(2)}, u32[]{:S(2)}) collective-permute-start(bf16[256,3072]{1,0:T(8,128)(2,1)} %get-tuple-element.19), channel_id=1, source_target_pairs={{0,64},{1,65},{2,66},{3,67},{4,68},{5,69},{6,70},{7,71},{8,72},{9,... | collective-permute-start | bytes 4718600 | tf_op jit(solution)/shard_map/ppermute | solution.py:53
  56.0 61.7 %collective-permute-start.7 = (bf16[4,192,1024]{2,1,0:T(8,128)(2,1)}, bf16[4,192,1024]{2,1,0:T(8,128)(2,1)}, u32[]{:S(2)}, u32[]{:S(2)}) collective-permute-start(bf16[4,192,1024]{2,1,0:T(8,128)(2,1)} %get-tuple-element.22), channel_id=1, source_target_pairs={{0,32},{1,33},{2,34},{3,35},{4,36},{5,37},{6,38},{7,39},{8,40},{9,... | collective-permute-start | bytes 4718600 | tf_op jit(solution)/shard_map/ppermute | solution.py:53
  58.5 58.6 %collective-permute-start.5 = (bf16[3,192,1024]{2,1,0:T(8,128)(2,1)}, bf16[3,192,1024]{2,1,0:T(8,128)(2,1)}, u32[]{:S(2)}, u32[]{:S(2)}) collective-permute-start(bf16[3,192,1024]{2,1,0:T(8,128)(2,1)} %get-tuple-element.20), channel_id=1, source_target_pairs={{0,48},{1,49},{2,50},{3,51},{4,52},{5,53},{6,54},{7,55},{8,56},{9,... | collective-permute-start | bytes 3538952 | tf_op jit(solution)/shard_map/ppermute | solution.py:53
  59.0 58.8 %collective-permute-start.6 = (bf16[3,192,1024]{2,1,0:T(8,128)(2,1)}, bf16[3,192,1024]{2,1,0:T(8,128)(2,1)}, u32[]{:S(2)}, u32[]{:S(2)}) collective-permute-start(bf16[3,192,1024]{2,1,0:T(8,128)(2,1)} %get-tuple-element.21), channel_id=1, source_target_pairs={{0,16},{1,17},{2,18},{3,19},{4,20},{5,21},{6,22},{7,23},{8,24},{9,... | collective-permute-start | bytes 3538952 | tf_op jit(solution)/shard_map/ppermute | solution.py:53
  60.7 57.0 %copy-start.1 = (bf16[192,1024]{1,0:T(8,128)(2,1)S(1)}, bf16[192,1024]{1,0:T(8,128)(2,1)}, u32[]{:S(2)}) copy-start(bf16[192,1024]{1,0:T(8,128)(2,1)} %copy-done) | copy-start | bytes 1179652
  60.7 57.0 %copy-start.4 = (bf16[192,1024]{1,0:T(8,128)(2,1)S(1)}, bf16[192,1024]{1,0:T(8,128)(2,1)}, u32[]{:S(2)}) copy-start(bf16[192,1024]{1,0:T(8,128)(2,1)} %copy-done.3) | copy-start | bytes 1179652
  89.9 38.1 %collective-permute-start.11 = (bf16[128,3072]{1,0:T(8,128)(2,1)S(1)}, bf16[128,3072]{1,0:T(8,128)(2,1)S(1)}, u32[]{:S(2)}, u32[]{:S(2)}) collective-permute-start(bf16[128,3072]{1,0:T(8,128)(2,1)S(1)} %slice.9), channel_id=1, source_target_pairs={{0,192},{1,193},{2,194},{3,195},{4,196},{5,197},{6,198},{7,199},{8... | collective-permute-start | bytes 2359304 | tf_op jit(solution)/shard_map/ppermute | solution.py:53
  91.2 36.2 %collective-permute-start.10 = (bf16[128,3072]{1,0:T(8,128)(2,1)S(1)}, bf16[128,3072]{1,0:T(8,128)(2,1)S(1)}, u32[]{:S(2)}, u32[]{:S(2)}) collective-permute-start(bf16[128,3072]{1,0:T(8,128)(2,1)S(1)} %slice.8), channel_id=1, source_target_pairs={{0,64},{1,65},{2,66},{3,67},{4,68},{5,69},{6,70},{7,71},{8,72},{9,... | collective-permute-start | bytes 2359304 | tf_op jit(solution)/shard_map/ppermute | solution.py:53
  128.7 11.0 %collective-permute-start.12 = (f32[1024,512]{1,0:T(8,128)S(1)}, f32[1024,512]{1,0:T(8,128)S(1)}, u32[]{:S(2)}, u32[]{:S(2)}) collective-permute-start(f32[1024,512]{1,0:T(8,128)S(1)} %convolution_dynamic-update-slice_fusion.6), channel_id=1, source_target_pairs={{0,1},{1,0},{2,3},{3,2},{4,5},{5,4},{6,7},{7,6},{8,9},{9,8},{10,11... | collective-permute-start | bytes 6291464 | tf_op jit(solution)/shard_map/ppermute | solution.py:53
  142.1 0.7 copy-start.8
  142.1 1.2 copy-start.9
  142.1 1.3 copy-start.7
  186.6 16.2 %collective-permute-start.13 = (bf16[512,128]{1,0:T(8,128)(2,1)S(1)}, bf16[512,128]{1,0:T(8,128)(2,1)S(1)}, u32[]{:S(2)}, u32[]{:S(2)}) collective-permute-start(bf16[512,128]{1,0:T(8,128)(2,1)S(1)} %fusion), channel_id=1, source_target_pairs={{0,0},{1,48},{2,1},{3,49},{4,12},{5,60},{6,13},{7,61},{8,4},{9,52}... | collective-permute-start | bytes 393224 | tf_op jit(solution)/shard_map/ppermute | solution.py:53
Sparse Core Ops, SparseCore 0:
  142.2 43.2 reduce-scatter.1

commit v2 on v1

--- a/solution.py
+++ b/solution.py
@@ -36,13 +36,12 @@
 SWAP = pairs(lambda y, x, z, c: (y, x, z, 1 - c))
 
 
-def slab_of(y, x, z):
-    turn = (z // 2 == 1) * 3 + (z // 2 == 2) * 1 + (z // 2 == 3) * 2
-    return (y + turn) % 4, x ^ (z % 2)
+def slab_of(x, z):
+    return z // 2, 2 * (x // 2) + z % 2
 
 
 def home(y, x, z, c):
-    col_y, col_x = slab_of(y, x, z)
+    col_y, col_x = slab_of(x, z)
     return y, x if c == 0 else 3 - x, 2 * col_y + col_x // 2, col_x % 2
 
 
@@ -53,12 +52,12 @@
     return lax.ppermute(value, AXES, where)
 
 
-def prepare_kernel(place, amp_mask, int_mask, a, b, own, near, up, down, over, scratch):
+def prepare_kernel(place, amp_mask, int_mask, a, b, own, oth, near, up, down, over, scratch):
     y, x = place[0], place[1]
     block_q = 2 * y + x // 2
     low = jnp.minimum(x, 3 - x)
     for to_y, first, second in (
-        (y, own, None),
+        (y, own, oth),
         (lax.rem(y + 1, 4), up.at[0], up.at[1]),
         (lax.rem(y + 3, 4), down.at[0], down.at[1]),
         (lax.rem(y + 2, 4), over.at[0], over.at[1]),
@@ -70,10 +69,9 @@
                 start = pl.multiple_of((to_y * 4 + to_x) * RB, RB)
                 for k in range(3):
                     value = a[k, :, pl.ds(start, RB)] * keep
-                    if dst is None:
+                    dst[pl.ds(k * 64, 64), pl.ds(half * RB, RB)] = value
+                    if dst is oth:
                         near[pl.ds(128, 64), pl.ds((2 * k + half) * RB, RB)] = value
-                    else:
-                        dst[pl.ds(k * 64, 64), pl.ds(half * RB, RB)] = value
     for slab in range(16):
         keep = int_mask[slab // 2, y].astype(jnp.float32).astype(jnp.bfloat16)
         at = ((slab % 4) * 4 + slab // 4) * KD
@@ -91,9 +89,9 @@
     vmem = pl.BlockSpec(memory_space=VMEM)
     return pl.pallas_call(
         prepare_kernel,
-        out_shape=(piece, near, two, two, two),
+        out_shape=(piece, piece, near, two, two, two),
         in_specs=[smem, smem, smem, vmem, vmem],
-        out_specs=(vmem,) * 5,
+        out_specs=(vmem,) * 6,
         scratch_shapes=[pltpu.VMEM((KT, 128), jnp.bfloat16)],
         compiler_params=pltpu.CompilerParams(vmem_limit_bytes=24 << 20),
         cost_estimate=pl.CostEstimate(flops=0, bytes_accessed=8 << 20, transcendentals=0),
@@ -101,43 +99,87 @@
     )(place, amp_mask, int_mask, a, b)
 
 
-def gather_kernel(near, from_near, down, up, over, early, own_rest, oth_rest, oth_all, b_here):
-    del early
+def gather_kernel(near, from_near, down, up, over, p0, x0, own_rest, oth_rest, b_here):
+    del p0, x0
     for j, ref in enumerate((down, up, over)):
         own_rest[j] = ref[0]
         oth_rest[j] = ref[1]
-        oth_all[j] = ref[1]
-    for k in range(3):
-        oth_all[3, pl.ds(k * 64, 64), :] = near[pl.ds(128, 64), pl.ds(k * 2 * RB, 2 * RB)]
-    b_here[pl.ds(0, 128), :] = near[pl.ds(0, 128), :]
+    b_here[pl.ds(0, 128), :] = near[...]
     b_here[pl.ds(128, 128), :] = from_near[...]
 
 
-def gather(near, from_near, down, up, over, early):
-    def shape(n):
-        return jax.ShapeDtypeStruct((n, KD, 2 * RB), jnp.bfloat16)
-
+def gather(*parts):
+    rest = jax.ShapeDtypeStruct((3, KD, 2 * RB), jnp.bfloat16)
     vmem = pl.BlockSpec(memory_space=VMEM)
+    slab = pl.BlockSpec((128, KT), lambda i: (0, 0))
+    anywhere = pl.BlockSpec(memory_space=pl.ANY)
     return pl.pallas_call(
         gather_kernel,
-        out_shape=(shape(3), shape(3), shape(4), jax.ShapeDtypeStruct((256, KT), jnp.bfloat16)),
+        out_shape=(rest, rest, jax.ShapeDtypeStruct((256, KT), jnp.bfloat16)),
         grid=(1,),
-        in_specs=[
-            vmem,
-            pl.BlockSpec((128, KT), lambda i: (0, 0)),
-            vmem,
-            vmem,
-            vmem,
-            pl.BlockSpec(memory_space=pl.ANY),
-        ],
-        out_specs=(vmem,) * 4,
-        compiler_params=pltpu.CompilerParams(vmem_limit_bytes=24 << 20),
-        cost_estimate=pl.CostEstimate(flops=0, bytes_accessed=10 << 20, transcendentals=0),
+        in_specs=[slab, slab, vmem, vmem, vmem, anywhere, anywhere],
+        out_specs=(vmem,) * 3,
+        compiler_params=pltpu.CompilerParams(vmem_limit_bytes=16 << 20),
+        cost_estimate=pl.CostEstimate(flops=0, bytes_accessed=8 << 20, transcendentals=0),
         name="gather",
-    )(near, from_near, down, up, over, early)
-
-
-def arrange_kernel(place, half, s0, s1, s2, s3, p0, p1, c0, c1, x1, out):
+    )(*parts)
+
+
+def six_kernel(place, here, down, up, out):
+    odd = lax.rem(place[1], 2)
+    for which, ref in enumerate((here, down, up)):
+
+        @pl.when(pl.program_id(0) == which)
+        def _(ref=ref):
+            out[pl.ds(pl.multiple_of(odd * 128, 128), 128), :] = ref[pl.ds(0, 128), :]
+            out[pl.ds(pl.multiple_of((1 - odd) * 128, 128), 128), :] = ref[pl.ds(128, 128), :]
+
+
+def six(place, *parts):
+    def spot(i, pr):
+        return (lax.rem(pr[0] + jnp.where(i == 0, 0, jnp.where(i == 1, 3, 1)), 4), 0)
+
+    return pl.pallas_call(
+        six_kernel,
+        out_shape=jax.ShapeDtypeStruct((1024, KT), jnp.bfloat16),
+        grid_spec=pltpu.PrefetchScalarGridSpec(
+            num_scalar_prefetch=1,
+            grid=(3,),
+            in_specs=[pl.BlockSpec((256, KT), lambda i, pr: (0, 0))] * 3,
+            out_specs=pl.BlockSpec((256, KT), spot),
+        ),
+        compiler_params=pltpu.CompilerParams(vmem_limit_bytes=16 << 20),
+        cost_estimate=pl.CostEstimate(flops=0, bytes_accessed=9 << 20, transcendentals=0),
+        name="six",
+    )(place, *parts)
+
+
+def eight_kernel(place, six_ref, far0, far1, out):
+    del six_ref
+    odd = lax.rem(place[1], 2)
+    out[pl.ds(pl.multiple_of(odd * 128, 128), 128), :] = far0[...]
+    out[pl.ds(pl.multiple_of((1 - odd) * 128, 128), 128), :] = far1[...]
+
+
+def eight(place, slabs, far0, far1):
+    slab = pl.BlockSpec((128, KT), lambda i, pr: (0, 0))
+    return pl.pallas_call(
+        eight_kernel,
+        out_shape=jax.ShapeDtypeStruct((1024, KT), jnp.bfloat16),
+        grid_spec=pltpu.PrefetchScalarGridSpec(
+            num_scalar_prefetch=1,
+            grid=(1,),
+            in_specs=[pl.BlockSpec(memory_space=pl.ANY), slab, slab],
+            out_specs=pl.BlockSpec((256, KT), lambda i, pr: (lax.rem(pr[0] + 2, 4), 0)),
+        ),
+        input_output_aliases={1: 0},
+        compiler_params=pltpu.CompilerParams(vmem_limit_bytes=16 << 20),
+        cost_estimate=pl.CostEstimate(flops=0, bytes_accessed=3 << 20, transcendentals=0),
+        name="eight",
+    )(place, slabs, far0, far1)
+
+
+def arrange_kernel(place, half, s0, s1, s2, s3, p0, p1, c0, c1, x0, x1, out):
     y, x = place[0], place[1]
 
     def put(ref, from_x, from_y):
@@ -155,7 +197,7 @@
     for k in range(3):
         start = pl.multiple_of(k * 2 * RB + half[0] * RB + pl.program_id(0) * 256, 256)
         out[pl.ds(at + k * 64, 64), :] = c0[:, pl.ds(start, 256)]
-    put(x1.at[3], far, y)
+    put(x0, far, y)
     for late, from_x in ((p1, 3 - x), (c1, near), (x1, far)):
         for j, from_y in enumerate(around):
             put(late.at[j], from_x, from_y)
@@ -170,7 +212,8 @@
         return pl.BlockSpec((lead, KD, wide), lambda i, pr, hr: (0, 0, 2 * hr[0] + i))
 
     specs = [lanes()] + [lanes(1)] * 3
-    specs += [lanes(), lanes(3), pl.BlockSpec((64, KT), lambda i, pr, hr: (2, 0)), lanes(3), lanes(4)]
+    specs += [lanes(), lanes(3), pl.BlockSpec((64, KT), lambda i, pr, hr: (2, 0)), lanes(3)]
+    specs += [lanes(), lanes(3)]
     return pl.pallas_call(
         arrange_kernel,
         out_shape=jax.ShapeDtypeStruct((KT, RB), jnp.bfloat16),
@@ -186,39 +229,50 @@
     )(place, half, *amps)
 
 
-def product(place, half, amps, ints):
-    right = arrange(place, half, amps)
-    return [jnp.dot(left, right, preferred_element_type=jnp.float32) for left in ints]
+def finish_kernel(total, row, col, out):
+    out[...] = (total[...] / -(row[...] + col[...])).T.astype(jnp.bfloat16)
+
+
+def finish(total, row, col):
+    return pl.pallas_call(
+        finish_kernel,
+        out_shape=jax.ShapeDtypeStruct((RB, 128), jnp.bfloat16),
+        in_specs=[pl.BlockSpec(memory_space=VMEM)] * 3,
+        out_specs=pl.BlockSpec(memory_space=VMEM),
+        compiler_params=pltpu.CompilerParams(vmem_limit_bytes=16 << 20),
+        name="finish",
+    )(total, row, col)
 
 
 def local(amplitudes, integrals, amp_mask, int_mask, occ_row, occ_col, vir_energy):
     y, x, z, core = (lax.axis_index(name) for name in AXES)
     place = jnp.stack([y, x]).astype(jnp.int32)
-    own, near, up, down, over = prepare(place, amp_mask, int_mask, amplitudes, integrals)
+    own, oth, near, up, down, over = prepare(place, amp_mask, int_mask, amplitudes, integrals)
 
     from_down = send(up, UP)
     from_up = send(down, DOWN)
     from_over = send(over, OVER)
     from_near = send(near, CROSS)
     p0 = send(own, PARTNER)
-
-    own_rest, oth_rest, oth_all, b_here = gather(
-        near, from_near, from_down, from_up, from_over, p0
-    )
+    x0 = send(oth, ACROSS)
+
+    own_rest, oth_rest, b_here = gather(near, from_near, from_down, from_up, from_over, p0, x0)
     b_down = send(b_here, UP)
     b_up = send(b_here, DOWN)
     p1 = send(own_rest, PARTNER)
     c1 = send(oth_rest, CROSS)
-    x1 = send(oth_all, ACROSS)
+    x1 = send(oth_rest, ACROSS)
     b_far0 = send(b_down[:128], UP)
     b_far1 = send(b_up[128:], DOWN)
-
-    amps = (own, from_down, from_up, from_over, p0, p1, from_near, c1, x1)
-    ints = (b_here, b_down, b_up, b_far0, b_far1)
+    slabs = eight(place, six(place, b_here, b_down, b_up), b_far0, b_far1)
+
+    amps = (own, from_down, from_up, from_over, p0, p1, from_near, c1, x0, x1)
     keep_half = jnp.bitwise_xor(x // 2, core).astype(jnp.int32)
-    given = jnp.concatenate(product(place, (1 - keep_half)[None], amps, ints))
+    give = arrange(place, (1 - keep_half)[None], amps)
+    given = jnp.dot(slabs, give, preferred_element_type=jnp.float32)
     taken = send(given, SWAP)
-    kept = jnp.concatenate(product(place, keep_half[None], amps, ints))
+    keep = arrange(place, keep_half[None], amps)
+    kept = jnp.dot(slabs, keep, preferred_element_type=jnp.float32)
     cycle_sum = lax.psum_scatter(
         (kept + taken).reshape(8, 128, RB), "z", scatter_dimension=0, tiled=True
     )[0]
@@ -226,12 +280,11 @@
     row_x = jnp.where(core == 0, x, 3 - x)
     row_occ = lax.dynamic_slice(occ_row, (4 * row_x,), (4,))
     row_vir = lax.dynamic_slice(vir_energy, (y, 0), (1, 128))
-    row_energy = (row_vir - row_occ[:, None]).reshape(-1)
-    col_y, col_x = slab_of(y, x, z)
+    row_energy = (row_vir - row_occ[:, None]).reshape(1, RB)
+    col_y, col_x = slab_of(x, z)
     col_occ = lax.dynamic_slice(occ_col, (col_x,), (1,))
-    col_energy = lax.dynamic_slice(vir_energy, (col_y, 0), (1, 128))[0] - col_occ
-    denominator = -(row_energy[:, None] + col_energy[None, :])
-    return send((cycle_sum.T / denominator).astype(jnp.bfloat16), HOME)
+    col_energy = (lax.dynamic_slice(vir_energy, (col_y, 0), (1, 128)) - col_occ).reshape(128, 1)
+    return send(finish(cycle_sum, row_energy, col_energy), HOME)
 
 
 def solution(mesh):

time: 211 us -> 193 us (0.915)
  the two profiles are of different devices: /device:TPU:58 before, /device:TPU:32 now
where the time goes in v2:
time: 193 us
  waiting for transfers between devices  121 us (63%)
  starting transfers between devices  23.4 us (12%)
  local copies, waits for them, and re-layouts  14.5 us (8%)
  between operations  13.6 us (7%)
  Pallas kernels  11.4 us (6%)
  matrix products  8.15 us (4%)
    ppermute x15, waiting for transfers between devices, send(): return lax.ppermute(value, AXES, where)  82.6 us
    reduce_scatter x1, waiting for transfers between devices, local(): lax.psum_scatter((kept + taken).reshape(8, 128, RB), 'z', scatter_dimensi...  38.5 us
    ppermute x15, starting transfers between devices, send(): return lax.ppermute(value, AXES, where)  23.4 us
    unnamed x40, local copies, waits for them, and re-layouts  11.8 us
    pallas_call x2, Pallas kernels, arrange(): pl.pallas_call(arrange_kernel, out_shape=jax.ShapeDtypeStruct((KT, RB), j...  5.3 us
    dot_general x1, matrix products, local(): kept = jnp.dot(slabs, keep, preferred_element_type=jnp.float32)  4.76 us
  transfers between devices with their start and end apart: 16, of which 8 were waited for; matrix products, arithmetic and copies ran while one was open for 2% of the time, Pallas kernels for 3%

profile of v2, /device:TPU:32, one launch (start us, length us, event | category | flops | bytes accessed | tf_op | source)
XLA Modules:
  0.0 193.0 jit_solution(2514517936617171098)
XLA Ops:
  6.5 0.8 copy.9.int_mask
  7.4 1.9 copy-done.8
  9.3 1.1 copy-done.13
  10.4 0.7 copy-done.15
  11.1 1.2 prepare.1
  12.3 1.6 collective-permute-start
  13.9 2.1 %collective-permute-start.4 = (bf16[192,1024]{1,0:T(8,128)(2,1)S(1)}, bf16[192,1024]{1,0:T(8,128)(2,1)S(1)}, u32[]{:S(2)}, u32[]{:S(2)}) collective-permute-start(bf16[192,1024]{1,0:T(8,128)(2,1)S(1)} %get-tuple-element.18.s0), channel_id=1, source_target_pairs={{0,48},{1,49},{2,50},{3,51},{4,52},{5,53},{6,54},{7,55},{8,56},{9,... | collective-permute-start | bytes 1179656 | tf_op jit(solution)/shard_map/ppermute | solution.py:52
  16.0 1.6 collective-permute-start.1
  17.5 1.7 collective-permute-start.2
  19.2 2.0 %collective-permute-start.3 = (bf16[2,192,1024]{2,1,0:T(8,128)(2,1)S(1)}, bf16[2,192,1024]{2,1,0:T(8,128)(2,1)S(1)}, u32[]{:S(2)}, u32[]{:S(2)}) collective-permute-start(bf16[2,192,1024]{2,1,0:T(8,128)(2,1)S(1)} %get-tuple-element.17), channel_id=1, source_target_pairs={{0,128},{1,129},{2,130},{3,131},{4,132},{5,133},{6,134},{7,135},{8... | collective-permute-start | bytes 2359304 | tf_op jit(solution)/shard_map/ppermute | solution.py:52
  21.2 4.5 %collective-permute-done.4.p0 = bf16[192,1024]{1,0:T(8,128)(2,1)S(1)} collective-permute-done((bf16[192,1024]{1,0:T(8,128)(2,1)S(1)}, bf16[192,1024]{1,0:T(8,128)(2,1)S(1)}, u32[]{:S(2)}, u32[]{:S(2)}) %collective-permute-start.4) | collective-permute-done | bytes 393248 | tf_op jit(solution)/shard_map/ppermute | solution.py:52
  25.7 1.5 collective-permute-start.5
  27.2 23.5 %collective-permute-done.5.x0 = bf16[192,1024]{1,0:T(8,128)(2,1)S(1)} collective-permute-done((bf16[192,1024]{1,0:T(8,128)(2,1)S(1)}, bf16[192,1024]{1,0:T(8,128)(2,1)S(1)}, u32[]{:S(2)}, u32[]{:S(2)}) %collective-permute-start.5) | collective-permute-done | bytes 393248 | tf_op jit(solution)/shard_map/ppermute | solution.py:52
  50.7 3.3 %collective-permute-done.3.over.s3 = bf16[2,192,1024]{2,1,0:T(8,128)(2,1)S(1)} collective-permute-done((bf16[2,192,1024]{2,1,0:T(8,128)(2,1)S(1)}, bf16[2,192,1024]{2,1,0:T(8,128)(2,1)S(1)}, u32[]{:S(2)}, u32[]{:S(2)}) %collective-permute-start.3) | collective-permute-done | bytes 786464 | tf_op jit(solution)/shard_map/ppermute | solution.py:52
  54.0 1.7 gather.1
  55.7 1.1 collective-permute-start.6
  56.9 2.1 %collective-permute-start.7 = (bf16[256,3072]{1,0:T(8,128)(2,1)S(1)}, bf16[256,3072]{1,0:T(8,128)(2,1)S(1)}, u32[]{:S(2)}, u32[]{:S(2)}) collective-permute-start(bf16[256,3072]{1,0:T(8,128)(2,1)S(1)} %get-tuple-element.20.here), channel_id=1, source_target_pairs={{0,192},{1,193},{2,194},{3,195},{4,196},{5,197},{6,198},{7,199},{8... | collective-permute-start | bytes 4718600 | tf_op jit(solution)/shard_map/ppermute | solution.py:52
  59.0 1.2 copy-done.11
  60.1 1.1 collective-permute-start.10
  61.3 3.6 %collective-permute-start.12 = (bf16[3,192,1024]{2,1,0:T(8,128)(2,1)}, bf16[3,192,1024]{2,1,0:T(8,128)(2,1)}, u32[]{:S(2)}, u32[]{:S(2)}) collective-permute-start(bf16[3,192,1024]{2,1,0:T(8,128)(2,1)} %get-tuple-element.22), channel_id=1, source_target_pairs={{0,32},{1,33},{2,34},{3,35},{4,36},{5,37},{6,38},{7,39},{8,40},{9,... | collective-permute-start | bytes 3538952 | tf_op jit(solution)/shard_map/ppermute | solution.py:52
  64.8 26.7 %collective-permute-done.6.down = bf16[256,3072]{1,0:T(8,128)(2,1)S(1)} collective-permute-done((bf16[256,3072]{1,0:T(8,128)(2,1)S(1)}, bf16[256,3072]{1,0:T(8,128)(2,1)S(1)}, u32[]{:S(2)}, u32[]{:S(2)}) %collective-permute-start.6) | collective-permute-done | bytes 1572896 | tf_op jit(solution)/shard_map/ppermute | solution.py:52
  91.6 1.0 slice.8
  92.6 0.1 collective-permute-start.8
  92.7 0.3 copy-done.4
  93.0 1.0 slice.9
  94.0 1.1 copy-done.6
  95.1 2.9 %collective-permute-start.9 = (bf16[128,3072]{1,0:T(8,128)(2,1)}, bf16[128,3072]{1,0:T(8,128)(2,1)}, u32[]{:S(2)}, u32[]{:S(2)}) collective-permute-start(bf16[128,3072]{1,0:T(8,128)(2,1)} %slice.9), channel_id=1, source_target_pairs={{0,192},{1,193},{2,194},{3,195},{4,196},{5,197},{6,198},{7,199},{8... | collective-permute-start | bytes 2359304 | tf_op jit(solution)/shard_map/ppermute | solution.py:52
  98.1 15.7 %collective-permute-done.12.x1 = bf16[3,192,1024]{2,1,0:T(8,128)(2,1)} collective-permute-done((bf16[3,192,1024]{2,1,0:T(8,128)(2,1)}, bf16[3,192,1024]{2,1,0:T(8,128)(2,1)}, u32[]{:S(2)}, u32[]{:S(2)}) %collective-permute-start.12) | collective-permute-done | bytes 1179680 | tf_op jit(solution)/shard_map/ppermute | solution.py:52
  113.8 1.0 copy-done.1
  114.8 1.0 copy-done.3
  115.8 1.0 copy-done.10
  116.8 2.8 %arrange.3 = bf16[3072,512]{1,0:T(8,128)(2,1)S(1)} custom-call(s32[2]{0:T(128)S(1)} %pad_add_fusion.place, s32[1]{0:T(128)} %bitcast.3.half, bf16[192,1024]{1,0:T(8,128)(2,1)S(1)} %copy-done.10, bf16[2,192,1024]{2,1,0:T(8,128)(2,1)S(1)} %collective-permute-done.1.down.s1, bf16[2,192,1024]{2,1,0:T(8,128)(2,1)S(1)} %collective-permute-done.2.up.s2, ...), custom_call_target="tpu_custom_call" | custom-call | bytes 6291456 | tf_op jit(solution)/shard_map/arrange/pallas_call | solution.py:217
  119.7 0.9 six.1.six_ref
  120.7 2.0 %eight.1 = bf16[1024,3072]{1,0:T(8,128)(2,1)S(1)} custom-call(s32[2]{0:T(128)S(1)} %pad_add_fusion.place, bf16[1024,3072]{1,0:T(8,128)(2,1)S(1)} %six.1.six_ref, bf16[128,3072]{1,0:T(8,128)(2,1)} %collective-permute-done.8.far0, bf16[128,3072]{1,0:T(8,128)(2,1)} %collective-permute-done.9.far1), custom_call_target="tpu_custom_call", output_to_operand_aliasing={{}: (1, {})} | custom-call | bytes 3145728 | tf_op jit(solution)/shard_map/eight/pallas_call | solution.py:166
  122.7 3.4 %fusion = f32[1024,512]{1,0:T(8,128)S(1)} fusion(bf16[1024,3072]{1,0:T(8,128)(2,1)S(1)} %eight.1, bf16[3072,512]{1,0:T(8,128)(2,1)S(1)} %arrange.3), kind=kOutput, calls=%fused_computation.5 | convolution fusion | flops 3221225472 | bytes 11534336 | tf_op jit(solution)/shard_map/dot_general | solution.py:272
  126.1 0.1 collective-permute-start.13
  126.2 2.5 %arrange.2 = bf16[3072,512]{1,0:T(8,128)(2,1)S(1)} custom-call(s32[2]{0:T(128)S(1)} %pad_add_fusion.place, s32[1]{0:T(128)} %bitcast.2.half, bf16[192,1024]{1,0:T(8,128)(2,1)S(1)} %copy-done.10, bf16[2,192,1024]{2,1,0:T(8,128)(2,1)S(1)} %collective-permute-done.1.down.s1, bf16[2,192,1024]{2,1,0:T(8,128)(2,1)S(1)} %collective-permute-done.2.up.s2, ...), custom_call_target="tpu_custom_call" | custom-call | bytes 6291456 | tf_op jit(solution)/shard_map/arrange/pallas_call | solution.py:217
  128.7 1.6 collective-permute-done.13
  130.3 4.8 %convolution_add_fusion = f32[1024,512]{1,0:T(8,128)} fusion(f32[1024,512]{1,0:T(8,128)S(1)} %collective-permute-done.13, bf16[1024,3072]{1,0:T(8,128)(2,1)S(1)} %eight.1, bf16[3072,512]{1,0:T(8,128)(2,1)S(1)} %arrange.2), kind=kOutput, calls=%fused_computation | convolution fusion | flops 3221749760 | bytes 13631488 | tf_op jit(solution)/shard_map/dot_general | solution.py:275
  135.2 0.6 dynamic_slice.15
  135.7 0.6 subtract_bitcast_fusion
  136.3 0.1 copy.10.col
  136.6 38.5 %reduce-scatter.2.cloned.1.call-done = f32[1,128,512]{2,1,0:T(8,128)} async-done(((f32[8,128,512]{2,1,0:T(8,128)}), f32[1,128,512]{2,1,0:T(8,128)}) %reduce-scatter.2.cloned.1.call-update) | async-done | bytes 262160 | tf_op jit(solution)/shard_map/reduce_scatter | solution.py:276
  175.1 0.9 copy-done.14
  176.0 0.2 finish.1
  176.2 1.9 collective-permute-start.14
  178.2 7.3 %collective-permute-done.14 = bf16[512,128]{1,0:T(8,128)(2,1)S(1)} collective-permute-done((bf16[512,128]{1,0:T(8,128)(2,1)S(1)}, bf16[512,128]{1,0:T(8,128)(2,1)S(1)}, u32[]{:S(2)}, u32[]{:S(2)}) %collective-permute-start.14) | collective-permute-done | bytes 131104 | tf_op jit(solution)/shard_map/ppermute | solution.py:52
  185.5 0.7 copy.13
  (42 shorter events, 0.4 us)
Async XLA Ops:
  6.5 168.6 %reduce-scatter.2.cloned.1.call-start = ((), (), s32[]{:S(2)}) async-start(), calls=%async_computation.1 | async-start | bytes 2359296 | tf_op jit(solution)/shard_map/reduce_scatter | solution.py:276
  7.4 1.9 copy-start.8
  9.3 1.1 copy-start.13
  10.4 0.7 copy-start.15
  12.3 80.3 %copy-start.9 = (bf16[192,1024]{1,0:T(8,128)(2,1)}, bf16[192,1024]{1,0:T(8,128)(2,1)S(1)}, u32[]{:S(2)}) copy-start(bf16[192,1024]{1,0:T(8,128)(2,1)S(1)} %get-tuple-element.18.s0) | copy-start | bytes 1179652
  12.3 41.7 %collective-permute-start = (bf16[192,3072]{1,0:T(8,128)(2,1)S(1)}, bf16[192,3072]{1,0:T(8,128)(2,1)S(1)}, u32[]{:S(2)}, u32[]{:S(2)}) collective-permute-start(bf16[192,3072]{1,0:T(8,128)(2,1)S(1)} %get-tuple-element.14.near), channel_id=1, source_target_pairs={{0,16},{1,17},{2,18},{3,19},{4,20},{5,21},{6,22},{7,23},{8,24},{9,... | collective-permute-start | bytes 3538952 | tf_op jit(solution)/shard_map/ppermute | solution.py:52
  13.9 11.8 %collective-permute-start.4 = (bf16[192,1024]{1,0:T(8,128)(2,1)S(1)}, bf16[192,1024]{1,0:T(8,128)(2,1)S(1)}, u32[]{:S(2)}, u32[]{:S(2)}) collective-permute-start(bf16[192,1024]{1,0:T(8,128)(2,1)S(1)} %get-tuple-element.18.s0), channel_id=1, source_target_pairs={{0,48},{1,49},{2,50},{3,51},{4,52},{5,53},{6,54},{7,55},{8,56},{9,... | collective-permute-start | bytes 1179656 | tf_op jit(solution)/shard_map/ppermute | solution.py:52
  16.0 34.8 %collective-permute-start.1 = (bf16[2,192,1024]{2,1,0:T(8,128)(2,1)S(1)}, bf16[2,192,1024]{2,1,0:T(8,128)(2,1)S(1)}, u32[]{:S(2)}, u32[]{:S(2)}) collective-permute-start(bf16[2,192,1024]{2,1,0:T(8,128)(2,1)S(1)} %get-tuple-element.15), channel_id=1, source_target_pairs={{0,64},{1,65},{2,66},{3,67},{4,68},{5,69},{6,70},{7,71},{8,72},{9,... | collective-permute-start | bytes 2359304 | tf_op jit(solution)/shard_map/ppermute | solution.py:52
  17.5 33.2 %collective-permute-start.2 = (bf16[2,192,1024]{2,1,0:T(8,128)(2,1)S(1)}, bf16[2,192,1024]{2,1,0:T(8,128)(2,1)S(1)}, u32[]{:S(2)}, u32[]{:S(2)}) collective-permute-start(bf16[2,192,1024]{2,1,0:T(8,128)(2,1)S(1)} %get-tuple-element.16), channel_id=1, source_target_pairs={{0,192},{1,193},{2,194},{3,195},{4,196},{5,197},{6,198},{7,199},{8... | collective-permute-start | bytes 2359304 | tf_op jit(solution)/shard_map/ppermute | solution.py:52
  19.2 34.8 %collective-permute-start.3 = (bf16[2,192,1024]{2,1,0:T(8,128)(2,1)S(1)}, bf16[2,192,1024]{2,1,0:T(8,128)(2,1)S(1)}, u32[]{:S(2)}, u32[]{:S(2)}) collective-permute-start(bf16[2,192,1024]{2,1,0:T(8,128)(2,1)S(1)} %get-tuple-element.17), channel_id=1, source_target_pairs={{0,128},{1,129},{2,130},{3,131},{4,132},{5,133},{6,134},{7,135},{8... | collective-permute-start | bytes 2359304 | tf_op jit(solution)/shard_map/ppermute | solution.py:52
  25.7 66.9 %copy-start = (bf16[192,1024]{1,0:T(8,128)(2,1)}, bf16[192,1024]{1,0:T(8,128)(2,1)S(1)}, u32[]{:S(2)}) copy-start(bf16[192,1024]{1,0:T(8,128)(2,1)S(1)} %collective-permute-done.4.p0) | copy-start | bytes 1179652
  25.7 25.1 %collective-permute-start.5 = (bf16[192,1024]{1,0:T(8,128)(2,1)S(1)}, bf16[192,1024]{1,0:T(8,128)(2,1)S(1)}, u32[]{:S(2)}, u32[]{:S(2)}) collective-permute-start(bf16[192,1024]{1,0:T(8,128)(2,1)S(1)} %get-tuple-element.19), channel_id=1, source_target_pairs={{0,32},{1,33},{2,34},{3,35},{4,36},{5,37},{6,38},{7,39},{8,40},{9,... | collective-permute-start | bytes 1179656 | tf_op jit(solution)/shard_map/ppermute | solution.py:52
  50.7 41.9 %copy-start.2 = (bf16[192,1024]{1,0:T(8,128)(2,1)}, bf16[192,1024]{1,0:T(8,128)(2,1)S(1)}, u32[]{:S(2)}) copy-start(bf16[192,1024]{1,0:T(8,128)(2,1)S(1)} %collective-permute-done.5.x0) | copy-start | bytes 1179652
  55.7 35.9 %collective-permute-start.6 = (bf16[256,3072]{1,0:T(8,128)(2,1)S(1)}, bf16[256,3072]{1,0:T(8,128)(2,1)S(1)}, u32[]{:S(2)}, u32[]{:S(2)}) collective-permute-start(bf16[256,3072]{1,0:T(8,128)(2,1)S(1)} %get-tuple-element.20.here), channel_id=1, source_target_pairs={{0,64},{1,65},{2,66},{3,67},{4,68},{5,69},{6,70},{7,71},{8,72},{9,... | collective-permute-start | bytes 4718600 | tf_op jit(solution)/shard_map/ppermute | solution.py:52
  56.9 36.1 %collective-permute-start.7 = (bf16[256,3072]{1,0:T(8,128)(2,1)S(1)}, bf16[256,3072]{1,0:T(8,128)(2,1)S(1)}, u32[]{:S(2)}, u32[]{:S(2)}) collective-permute-start(bf16[256,3072]{1,0:T(8,128)(2,1)S(1)} %get-tuple-element.20.here), channel_id=1, source_target_pairs={{0,192},{1,193},{2,194},{3,195},{4,196},{5,197},{6,198},{7,199},{8... | collective-permute-start | bytes 4718600 | tf_op jit(solution)/shard_map/ppermute | solution.py:52
  59.0 1.2 copy-start.11
  60.1 37.9 %collective-permute-start.10 = (bf16[3,192,1024]{2,1,0:T(8,128)(2,1)}, bf16[3,192,1024]{2,1,0:T(8,128)(2,1)}, u32[]{:S(2)}, u32[]{:S(2)}) collective-permute-start(bf16[3,192,1024]{2,1,0:T(8,128)(2,1)} %get-tuple-element.21), channel_id=1, source_target_pairs={{0,48},{1,49},{2,50},{3,51},{4,52},{5,53},{6,54},{7,55},{8,56},{9,... | collective-permute-start | bytes 3538952 | tf_op jit(solution)/shard_map/ppermute | solution.py:52
  61.3 36.8 %collective-permute-start.11 = (bf16[3,192,1024]{2,1,0:T(8,128)(2,1)}, bf16[3,192,1024]{2,1,0:T(8,128)(2,1)}, u32[]{:S(2)}, u32[]{:S(2)}) collective-permute-start(bf16[3,192,1024]{2,1,0:T(8,128)(2,1)} %get-tuple-element.22), channel_id=1, source_target_pairs={{0,16},{1,17},{2,18},{3,19},{4,20},{5,21},{6,22},{7,23},{8,24},{9,... | collective-permute-start | bytes 3538952 | tf_op jit(solution)/shard_map/ppermute | solution.py:52
  61.3 52.5 %collective-permute-start.12 = (bf16[3,192,1024]{2,1,0:T(8,128)(2,1)}, bf16[3,192,1024]{2,1,0:T(8,128)(2,1)}, u32[]{:S(2)}, u32[]{:S(2)}) collective-permute-start(bf16[3,192,1024]{2,1,0:T(8,128)(2,1)} %get-tuple-element.22), channel_id=1, source_target_pairs={{0,32},{1,33},{2,34},{3,35},{4,36},{5,37},{6,38},{7,39},{8,40},{9,... | collective-permute-start | bytes 3538952 | tf_op jit(solution)/shard_map/ppermute | solution.py:52
  91.6 1.4 copy-start.4
  92.6 28.1 %collective-permute-start.8 = (bf16[128,3072]{1,0:T(8,128)(2,1)}, bf16[128,3072]{1,0:T(8,128)(2,1)}, u32[]{:S(2)}, u32[]{:S(2)}) collective-permute-start(bf16[128,3072]{1,0:T(8,128)(2,1)} %slice.8), channel_id=1, source_target_pairs={{0,64},{1,65},{2,66},{3,67},{4,68},{5,69},{6,70},{7,71},{8,72},{9,... | collective-permute-start | bytes 2359304 | tf_op jit(solution)/shard_map/ppermute | solution.py:52
  94.0 1.1 copy-start.6
  95.1 25.5 %collective-permute-start.9 = (bf16[128,3072]{1,0:T(8,128)(2,1)}, bf16[128,3072]{1,0:T(8,128)(2,1)}, u32[]{:S(2)}, u32[]{:S(2)}) collective-permute-start(bf16[128,3072]{1,0:T(8,128)(2,1)} %slice.9), channel_id=1, source_target_pairs={{0,192},{1,193},{2,194},{3,195},{4,196},{5,197},{6,198},{7,199},{8... | collective-permute-start | bytes 2359304 | tf_op jit(solution)/shard_map/ppermute | solution.py:52
  113.8 1.0 copy-start.1
  114.8 1.0 copy-start.3
  115.8 1.0 copy-start.10
  116.8 2.8 %copy-start.5 = (bf16[256,3072]{1,0:T(8,128)(2,1)S(1)}, bf16[256,3072]{1,0:T(8,128)(2,1)}, u32[]{:S(2)}) copy-start(bf16[256,3072]{1,0:T(8,128)(2,1)} %copy-done.4) | copy-start | bytes 4718596
  116.8 2.8 %copy-start.7 = (bf16[256,3072]{1,0:T(8,128)(2,1)S(1)}, bf16[256,3072]{1,0:T(8,128)(2,1)}, u32[]{:S(2)}) copy-start(bf16[256,3072]{1,0:T(8,128)(2,1)} %copy-done.6) | copy-start | bytes 4718596
  116.8 2.9 %copy-start.12 = (bf16[256,3072]{1,0:T(8,128)(2,1)S(1)}, bf16[256,3072]{1,0:T(8,128)(2,1)}, u32[]{:S(2)}) copy-start(bf16[256,3072]{1,0:T(8,128)(2,1)} %copy-done.11) | copy-start | bytes 4718596
  126.1 4.2 %collective-permute-start.13 = (f32[1024,512]{1,0:T(8,128)S(1)}, f32[1024,512]{1,0:T(8,128)S(1)}, u32[]{:S(2)}, u32[]{:S(2)}) collective-permute-start(f32[1024,512]{1,0:T(8,128)S(1)} %fusion), channel_id=1, source_target_pairs={{0,1},{1,0},{2,3},{3,2},{4,5},{5,4},{6,7},{7,6},{8,9},{9,8},{10,11... | collective-permute-start | bytes 6291464 | tf_op jit(solution)/shard_map/ppermute | solution.py:52
  128.7 6.5 %copy-start.17 = (f32[4]{0:T(128)S(1)}, f32[4]{0:T(128)}, u32[]{:S(2)}) copy-start(f32[4]{0:T(128)} %param.12) | copy-start | bytes 52
  128.7 7.0 %copy-start.16 = (f32[4,128]{1,0:T(4,128)S(1)}, f32[4,128]{1,0:T(4,128)}, u32[]{:S(2)}) copy-start(f32[4,128]{1,0:T(4,128)} %param.13) | copy-start | bytes 6148
  128.7 7.7 %copy-start.18 = (f32[16]{0:T(128)S(1)}, f32[16]{0:T(128)}, u32[]{:S(2)}) copy-start(f32[16]{0:T(128)} %param.11) | copy-start | bytes 196
  175.1 0.9 copy-start.14
  176.2 9.2 %collective-permute-start.14 = (bf16[512,128]{1,0:T(8,128)(2,1)S(1)}, bf16[512,128]{1,0:T(8,128)(2,1)S(1)}, u32[]{:S(2)}, u32[]{:S(2)}) collective-permute-start(bf16[512,128]{1,0:T(8,128)(2,1)S(1)} %finish.1), channel_id=1, source_target_pairs={{0,0},{1,48},{2,1},{3,49},{4,4},{5,52},{6,5},{7,53},{8,8},{9,56},{... | collective-permute-start | bytes 393224 | tf_op jit(solution)/shard_map/ppermute | solution.py:52
Sparse Core Ops, SparseCore 0:
  135.2 39.7 reduce-scatter.1

commit v3 on v2

v3 whole, which is shorter than its diff:
```python
import jax
import jax.numpy as jnp
from jax import lax
from jax.experimental import pallas as pl
from jax.experimental.pallas import tpu as pltpu
from jax.sharding import Mesh, PartitionSpec as P

AXES = ("y", "x", "z", "core")
NY, NX, NZ, NC = 4, 4, 8, 2
KD = 192
RB = 512
KT = 16 * KD
VMEM = pltpu.MemorySpace.VMEM


def pairs(to):
    out = []
    for y in range(NY):
        for x in range(NX):
            for z in range(NZ):
                for c in range(NC):
                    ty, tx, tz, tc = to(y, x, z, c)
                    src = ((y * NX + x) * NZ + z) * NC + c
                    dst = ((ty % NY * NX + tx % NX) * NZ + tz % NZ) * NC + tc % NC
                    out.append((src, dst))
    return out


UP = pairs(lambda y, x, z, c: (y + 1, x, z, c))
DOWN = pairs(lambda y, x, z, c: (y - 1, x, z, c))
OVER = pairs(lambda y, x, z, c: (y + 2, x, z, c))
PARTNER = pairs(lambda y, x, z, c: (y, 3 - x, z, c))
CROSS = pairs(lambda y, x, z, c: (y, x ^ 1, z, c))
ACROSS = pairs(lambda y, x, z, c: (y, x + 2, z, c))
AHEAD = pairs(lambda y, x, z, c: (y, x, z + 1, c))
BEHIND = pairs(lambda y, x, z, c: (y, x, z - 1, c))
SWAP = pairs(lambda y, x, z, c: (y, x, z, 1 - c))


def slab_of(x, z):
    return z // 2, 2 * (x // 2) + z % 2


def home(y, x, z, c):
    col_y, col_x = slab_of(x, z)
    return y, x if c == 0 else 3 - x, 2 * col_y + col_x // 2, col_x % 2


HOME = pairs(home)


def send(value, where):
    return lax.ppermute(value, AXES, where)


def prepare_kernel(
    place, amp_mask, int_mask, a_any, b_any, own, oth, near, up, down, over, a, b, scratch, sems
):
    y, x = place[0], place[1]
    block_q = 2 * y + x // 2
    low = jnp.minimum(x, 3 - x)
    turns = (y, lax.rem(y + 1, 4), lax.rem(y + 3, 4), lax.rem(y + 2, 4))
    moves = [pltpu.make_async_copy(b_any, b, sems.at[4])]
    for j, to_y in enumerate(turns):
        lanes = pl.ds(pl.multiple_of(to_y * 4 * RB, 4 * RB), 4 * RB)
        moves.append(pltpu.make_async_copy(a_any.at[:, :, lanes], a.at[j], sems.at[j]))
    for move in moves:
        move.start()
    moves[0].wait()
    for slab in range(16):
        keep = int_mask[y, slab // 2].astype(jnp.float32).astype(jnp.bfloat16)
        at = ((slab % 4) * 4 + slab // 4) * KD
        for k in range(3):
            scratch[pl.ds(at + k * 64, 64), :] = b[k, pl.ds(slab * 64, 64), :] * keep
    for j in range(KT // 128):
        near[pl.ds(0, 128), pl.ds(j * 128, 128)] = scratch[pl.ds(j * 128, 128), :].T
    for j, (first, second) in enumerate(
        ((own, oth), (up.at[0], up.at[1]), (down.at[0], down.at[1]), (over.at[0], over.at[1]))
    ):
        moves[1 + j].wait()
        keep = amp_mask[turns[j], block_q].astype(jnp.float32).astype(jnp.bfloat16)
        for dst, lo in ((first, low), (second, 1 - low)):
            for half in range(2):
                to_x = lo if half == 0 else 3 - lo
                start = pl.multiple_of(to_x * RB, RB)
                for k in range(3):
                    value = a[j, k, :, pl.ds(start, RB)] * keep
                    dst[pl.ds(k * 64, 64), pl.ds(half * RB, RB)] = value
                    if dst is oth:
                        near[pl.ds(128, 64), pl.ds((2 * k + half) * RB, RB)] = value


def prepare(place, amp_mask, int_mask, a, b):
    piece = jax.ShapeDtypeStruct((KD, 2 * RB), jnp.bfloat16)
    two = jax.ShapeDtypeStruct((2, KD, 2 * RB), jnp.bfloat16)
    near = jax.ShapeDtypeStruct((KD, KT), jnp.bfloat16)
    anywhere = pl.BlockSpec(memory_space=pl.ANY)
    vmem = pl.BlockSpec(memory_space=VMEM)
    return pl.pallas_call(
        prepare_kernel,
        out_shape=(piece, piece, near, two, two, two),
        grid_spec=pltpu.PrefetchScalarGridSpec(
            num_scalar_prefetch=3,
            grid=(1,),
            in_specs=[anywhere, anywhere],
            out_specs=(vmem,) * 6,
            scratch_shapes=[
                pltpu.VMEM((4, 3, 64, 4 * RB), jnp.bfloat16),
                pltpu.VMEM((3, 1024, 128), jnp.bfloat16),
                pltpu.VMEM((KT, 128), jnp.bfloat16),
                pltpu.SemaphoreType.DMA((5,)),
            ],
        ),
        compiler_params=pltpu.CompilerParams(vmem_limit_bytes=58 << 20),
        cost_estimate=pl.CostEstimate(flops=0, bytes_accessed=8 << 20, transcendentals=0),
        name="prepare",
    )(place, amp_mask, int_mask.T, a, b)


def follow_kernel(value, after, out):
    del after
    out[...] = value[...]


def follow(value, after):
    vmem = pl.BlockSpec(memory_space=VMEM)
    return pl.pallas_call(
        follow_kernel,
        out_shape=jax.ShapeDtypeStruct(value.shape, value.dtype),
        in_specs=[vmem, pl.BlockSpec(memory_space=pl.ANY)],
        out_specs=vmem,
        compiler_params=pltpu.CompilerParams(vmem_limit_bytes=4 << 20),
        cost_estimate=pl.CostEstimate(flops=0, bytes_accessed=1 << 20, transcendentals=0),
        name="follow",
    )(value, after)


def gather_kernel(near, from_near, down, up, over, p0, x0, own_rest, oth_rest, b_here):
    del p0, x0
    for j, ref in enumerate((down, up, over)):
        own_rest[j] = ref[0]
        oth_rest[j] = ref[1]
    b_here[pl.ds(0, 128), :] = near[...]
    b_here[pl.ds(128, 128), :] = from_near[...]


def gather(*parts):
    rest = jax.ShapeDtypeStruct((3, KD, 2 * RB), jnp.bfloat16)
    vmem = pl.BlockSpec(memory_space=VMEM)
    slab = pl.BlockSpec((128, KT), lambda i: (0, 0))
    anywhere = pl.BlockSpec(memory_space=pl.ANY)
    return pl.pallas_call(
        gather_kernel,
        out_shape=(rest, rest, jax.ShapeDtypeStruct((256, KT), jnp.bfloat16)),
        grid=(1,),
        in_specs=[slab, slab, vmem, vmem, vmem, anywhere, anywhere],
        out_specs=(vmem,) * 3,
        compiler_params=pltpu.CompilerParams(vmem_limit_bytes=16 << 20),
        cost_estimate=pl.CostEstimate(flops=0, bytes_accessed=8 << 20, transcendentals=0),
        name="gather",
    )(*parts)


def run(moves, sems):
    copies = [pltpu.make_async_copy(src, dst, sems.at[i]) for i, (src, dst) in enumerate(moves)]
    for copy in copies:
        copy.start()
    for copy in copies:
        copy.wait()


def join_kernel(place, here, down, up, far0, far1, out, sems):
    y, odd, z = place[0], lax.rem(place[1], 2), place[2]
    moves = []
    for turn, first, second in ((0, here, here), (3, down, down), (1, up, up), (2, far0, far1)):
        at = lax.rem(y + turn, 4) * 2
        skip = 0 if first is far0 else 128
        for bit, src in ((odd, first.at[pl.ds(0, 128), :]), (1 - odd, second.at[pl.ds(skip, 128), :])):
            ahead = lax.rem(at + bit - z + 8, 8)
            spot = jnp.where(ahead == 0, 7, jnp.where(ahead < 5, 7 - 2 * ahead, 2 * ahead - 8))
            spot = jnp.maximum(spot, 0)
            moves.append((src, out.at[pl.ds(pl.multiple_of(spot * 128, 128), 128), :]))
    run(moves, sems)


def join(place, *parts):
    return pl.pallas_call(
        join_kernel,
        out_shape=jax.ShapeDtypeStruct((1024, KT), jnp.bfloat16),
        grid_spec=pltpu.PrefetchScalarGridSpec(
            num_scalar_prefetch=1,
            grid=(1,),
            in_specs=[pl.BlockSpec(memory_space=pl.ANY)] * 5,
            out_specs=pl.BlockSpec(memory_space=VMEM),
            scratch_shapes=[pltpu.SemaphoreType.DMA((8,))],
        ),
        compiler_params=pltpu.CompilerParams(vmem_limit_bytes=16 << 20),
        cost_estimate=pl.CostEstimate(flops=0, bytes_accessed=6 << 20, transcendentals=0),
        name="join",
    )(place, *parts)


def arrange_kernel(place, half, s0, s1, s2, s3, p0, p1, c0, c1, x0, x1, out, sems):
    y, x = place[0], place[1]
    first = pl.multiple_of(half[0] * RB, RB)
    lanes = pl.ds(first, RB)
    moves = []

    def put(ref, from_x, from_y):
        at = pl.multiple_of((from_x * 4 + from_y) * KD, KD)
        moves.append((ref.at[:, lanes], out.at[pl.ds(at, KD), :]))

    around = (lax.rem(y + 3, 4), lax.rem(y + 1, 4), lax.rem(y + 2, 4))
    put(s0, x, y)
    for ref, from_y in zip((s1, s2, s3), around):
        put(ref.at[0], x, from_y)
    far = lax.rem(x + 2, 4)
    near = x + 1 - 2 * lax.rem(x, 2)
    put(p0, 3 - x, y)
    at = pl.multiple_of((near * 4 + y) * KD, KD)
    for k in range(3):
        source = pl.ds(pl.multiple_of(k * 2 * RB + first, RB), RB)
        moves.append((c0.at[pl.ds(128, 64), source], out.at[pl.ds(at + k * 64, 64), :]))
    put(x0, far, y)
    for late, from_x in ((p1, 3 - x), (c1, near), (x1, far)):
        for j, from_y in enumerate(around):
            put(late.at[j], from_x, from_y)
    run(moves, sems)


def arrange(place, half, amps):
    return pl.pallas_call(
        arrange_kernel,
        out_shape=jax.ShapeDtypeStruct((KT, RB), jnp.bfloat16),
        grid_spec=pltpu.PrefetchScalarGridSpec(
            num_scalar_prefetch=2,
            grid=(1,),
            in_specs=[pl.BlockSpec(memory_space=pl.ANY)] * 10,
            out_specs=pl.BlockSpec(memory_space=VMEM),
            scratch_shapes=[pltpu.SemaphoreType.DMA((18,))],
        ),
        compiler_params=pltpu.CompilerParams(vmem_limit_bytes=16 << 20),
        cost_estimate=pl.CostEstimate(flops=0, bytes_accessed=6 << 20, transcendentals=0),
        name="arrange",
    )(place, half, *amps)


def finish_kernel(total, row, col, out):
    out[...] = (total[...] / -(row[...] + col[...])).T.astype(jnp.bfloat16)


def finish(total, row, col):
    return pl.pallas_call(
        finish_kernel,
        out_shape=jax.ShapeDtypeStruct((RB, 128), jnp.bfloat16),
        in_specs=[pl.BlockSpec(memory_space=VMEM)] * 3,
        out_specs=pl.BlockSpec(memory_space=VMEM),
        compiler_params=pltpu.CompilerParams(vmem_limit_bytes=16 << 20),
        name="finish",
    )(total, row, col)


def local(amplitudes, integrals, amp_mask, int_mask, occ_row, occ_col, vir_energy):
    y, x, z, core = (lax.axis_index(name) for name in AXES)
    place = jnp.stack([y, x, z]).astype(jnp.int32)
    own, oth, near, up, down, over = prepare(place, amp_mask, int_mask, amplitudes, integrals)

    from_down = send(up, UP)
    from_up = send(down, DOWN)
    from_over = send(over, OVER)
    from_near = send(near, CROSS)
    p0 = send(own, PARTNER)
    x0 = send(follow(oth, p0), ACROSS)

    own_rest, oth_rest, b_here = gather(near, from_near, from_down, from_up, from_over, p0, x0)
    b_down = send(b_here, UP)
    b_up = send(b_here, DOWN)
    p1 = send(own_rest, PARTNER)
    c1 = send(oth_rest, CROSS)
    x1 = send(oth_rest, ACROSS)
    b_far0 = send(b_down[:128], UP)
    b_far1 = send(b_up[128:], DOWN)
    slabs = join(place, b_here, b_down, b_up, b_far0, b_far1)

    amps = (own, from_down, from_up, from_over, p0, p1, from_near, c1, x0, x1)
    keep_half = jnp.bitwise_xor(x // 2, core).astype(jnp.int32)
    give = arrange(place, (1 - keep_half)[None], amps)
    given = jnp.dot(slabs, give, preferred_element_type=jnp.float32)
    taken = send(given, SWAP)
    keep = arrange(place, keep_half[None], amps)

    def partial(spot):
        rows = slice(spot * 128, spot * 128 + 128)
        return jnp.dot(slabs[rows], keep, preferred_element_type=jnp.float32) + taken[rows]

    farthest = partial(0)
    ahead, behind = farthest[:64], farthest[64:]
    for step in range(3):
        ahead, behind = send(ahead, AHEAD), send(behind, BEHIND)
        if step == 0:
            ahead = jnp.pad(ahead, ((0, 64), (0, 0)))
            behind = jnp.pad(behind, ((64, 0), (0, 0)))
        ahead = partial(1 + 2 * step) + ahead
        behind = partial(2 + 2 * step) + behind
    cycle_sum = partial(7) + send(ahead, AHEAD) + send(behind, BEHIND)

    row_x = jnp.where(core == 0, x, 3 - x)
    row_occ = lax.dynamic_slice(occ_row, (4 * row_x,), (4,))
    row_vir = lax.dynamic_slice(vir_energy, (y, 0), (1, 128))
    row_energy = (row_vir - row_occ[:, None]).reshape(1, RB)
    col_y, col_x = slab_of(x, z)
    col_occ = lax.dynamic_slice(occ_col, (col_x,), (1,))
    col_energy = (lax.dynamic_slice(vir_energy, (col_y, 0), (1, 128)) - col_occ).reshape(128, 1)
    return send(finish(cycle_sum, row_energy, col_energy), HOME)


def solution(mesh):
    grid = Mesh(mesh.devices.reshape(NY, NX, NZ, NC), AXES)
    layout, rep = ("y", "x"), ("z", "core")
    placed = (P(rep, layout, None), P(rep, None, layout), P(), P(), P(), P(), P())
    return jax.shard_map(
        local, mesh=grid, in_specs=placed, out_specs=P(layout, rep), check_vma=False
    )
```

time: 193 us -> 177 us (0.917)
  waiting for transfers between devices: 121 us -> 99.2 us
  between operations: 13.6 us -> 0.35 us
  starting transfers between devices: 23.4 us -> 34 us
  matrix products: 8.15 us -> 13.3 us
  Pallas kernels: 11.4 us -> 14.6 us
    reduce_scatter x1 -> x0, waiting for transfers between devices: 38.5 us -> none  [local(): lax.psum_scatter((kept + taken).reshape(8, 128, RB), 'z', scatter_dimensi...]
    ppermute x15 -> x23, waiting for transfers between devices: 82.6 us -> 99.2 us  [send(): return lax.ppermute(value, AXES, where)]
    ppermute x15 -> x23, starting transfers between devices: 23.4 us -> 34 us  [send(): return lax.ppermute(value, AXES, where)]
    dot_general x1 -> x8, matrix products: 4.76 us -> 9.9 us  [partial(): jnp.dot(slabs[rows], keep, preferred_element_type=jnp.float32) + taken[rows]]
    pallas_call x1, Pallas kernels: 1.21 us -> 4.92 us  [prepare(): pl.pallas_call(prepare_kernel, out_shape=(piece, piece, near, two, two, t...]
    unnamed x40 -> x65, local copies, waits for them, and re-layouts: 11.8 us -> 10.5 us
  transfers between devices with their start and end apart: 16 -> 23, of which waited for: 8 -> 15; matrix products, arithmetic and copies ran while one was open for 2% -> 6% of each run, Pallas kernels for 3% -> 3%
where the time goes in v3:
time: 177 us; the launch traced here: 176 us
  waiting for transfers between devices  99.2 us (56%)
  starting transfers between devices  34 us (19%)
  Pallas kernels  14.6 us (8%)
  local copies, waits for them, and re-layouts  13.3 us (8%)
  matrix products  13.3 us (8%)
    ppermute x23, waiting for transfers between devices, send(): return lax.ppermute(value, AXES, where)  99.2 us
    ppermute x23, starting transfers between devices, send(): return lax.ppermute(value, AXES, where)  34 us
    unnamed x65, local copies, waits for them, and re-layouts  10.5 us
    dot_general x8, matrix products, partial(): jnp.dot(slabs[rows], keep, preferred_element_type=jnp.float32) + taken[rows]  9.9 us
    pallas_call x2, Pallas kernels, arrange(): pl.pallas_call(arrange_kernel, out_shape=jax.ShapeDtypeStruct((KT, RB), j...  5.32 us
    pallas_call x1, Pallas kernels, prepare(): pl.pallas_call(prepare_kernel, out_shape=(piece, piece, near, two, two, t...  4.92 us
  transfers between devices with their start and end apart: 23, of which 15 were waited for; matrix products, arithmetic and copies ran while one was open for 6% of the time, Pallas kernels for 3%

profile of v3, /device:TPU:32, one launch (start us, length us, event | category | flops | bytes accessed | tf_op | source)
XLA Modules:
  0.0 176.1 jit_solution(3264321006379951475)
XLA Ops:
  0.6 4.9 %prepare.1 = (bf16[192,1024]{1,0:T(8,128)(2,1)}, bf16[192,1024]{1,0:T(8,128)(2,1)}, bf16[192,3072]{1,0:T(8,128)(2,1)}, bf16[2,192,1024]{2,1,0:T(8,128)(2,1)}, bf...) custom-call(s32[3]{0:T(128)} %pad_add_fusion.place, s32[4,8]{1,0:T(4,128)} %amp_mask.1, s32[4,8]{1,0:T(4,128)} %bitcast.23, ...), custom_call_target="tpu_custom_call" | custom-call | bytes 8388608 | tf_op jit(solution)/shard_map/prepare/pallas_call | solution.py:99
  5.5 1.6 collective-permute-start
  7.1 2.1 %collective-permute-start.4 = (bf16[192,1024]{1,0:T(8,128)(2,1)}, bf16[192,1024]{1,0:T(8,128)(2,1)S(1)}, u32[]{:S(2)}, u32[]{:S(2)}) collective-permute-start(bf16[192,1024]{1,0:T(8,128)(2,1)} %get-tuple-element.18.s0), channel_id=1, source_target_pairs={{0,48},{1,49},{2,50},{3,51},{4,52},{5,53},{6,54},{7,55},{8,56},{9,... | collective-permute-start | bytes 1179656 | tf_op jit(solution)/shard_map/ppermute | solution.py:53
  9.2 1.6 collective-permute-start.1
  10.8 1.7 collective-permute-start.2
  12.5 2.0 %collective-permute-start.3 = (bf16[2,192,1024]{2,1,0:T(8,128)(2,1)}, bf16[2,192,1024]{2,1,0:T(8,128)(2,1)S(1)}, u32[]{:S(2)}, u32[]{:S(2)}) collective-permute-start(bf16[2,192,1024]{2,1,0:T(8,128)(2,1)} %get-tuple-element.17), channel_id=1, source_target_pairs={{0,128},{1,129},{2,130},{3,131},{4,132},{5,133},{6,134},{7,135},{8... | collective-permute-start | bytes 2359304 | tf_op jit(solution)/shard_map/ppermute | solution.py:53
  14.4 4.7 %collective-permute-done.4.after.p0 = bf16[192,1024]{1,0:T(8,128)(2,1)S(1)} collective-permute-done((bf16[192,1024]{1,0:T(8,128)(2,1)}, bf16[192,1024]{1,0:T(8,128)(2,1)S(1)}, u32[]{:S(2)}, u32[]{:S(2)}) %collective-permute-start.4) | collective-permute-done | bytes 393248 | tf_op jit(solution)/shard_map/ppermute | solution.py:53
  19.1 1.1 copy-done.25
  20.3 1.6 collective-permute-start.5
  21.9 22.3 %collective-permute-done.5.x0 = bf16[192,1024]{1,0:T(8,128)(2,1)S(1)} collective-permute-done((bf16[192,1024]{1,0:T(8,128)(2,1)S(1)}, bf16[192,1024]{1,0:T(8,128)(2,1)S(1)}, u32[]{:S(2)}, u32[]{:S(2)}) %collective-permute-start.5) | collective-permute-done | bytes 393248 | tf_op jit(solution)/shard_map/ppermute | solution.py:53
  44.2 3.3 %collective-permute-done.3.over.s3 = bf16[2,192,1024]{2,1,0:T(8,128)(2,1)S(1)} collective-permute-done((bf16[2,192,1024]{2,1,0:T(8,128)(2,1)}, bf16[2,192,1024]{2,1,0:T(8,128)(2,1)S(1)}, u32[]{:S(2)}, u32[]{:S(2)}) %collective-permute-start.3) | collective-permute-done | bytes 786464 | tf_op jit(solution)/shard_map/ppermute | solution.py:53
  47.5 1.6 copy-done.24
  49.0 1.8 %gather.1 = (bf16[3,192,1024]{2,1,0:T(8,128)(2,1)}, bf16[3,192,1024]{2,1,0:T(8,128)(2,1)}, bf16[256,3072]{1,0:T(8,128)(2,1)S(1)}) custom-call(bf16[192,3072]{1,0:T(8,128)(2,1)S(1)} %copy-done.24, bf16[192,3072]{1,0:T(8,128)(2,1)S(1)} %collective-permute-done.from_near.c0, bf16[2,192,1024]{2,1,0:T(8,128)(2,1)S(1)} %collective-permute-done.1.down.s1, ...), custom_call_target="tpu_custom_call" | custom-call | bytes 8388608 | tf_op jit(solution)/shard_map/gather/pallas_call | solution.py:152
  50.8 2.1 %collective-permute-start.7 = (bf16[256,3072]{1,0:T(8,128)(2,1)S(1)}, bf16[256,3072]{1,0:T(8,128)(2,1)S(1)}, u32[]{:S(2)}, u32[]{:S(2)}) collective-permute-start(bf16[256,3072]{1,0:T(8,128)(2,1)S(1)} %get-tuple-element.20.here), channel_id=1, source_target_pairs={{0,192},{1,193},{2,194},{3,195},{4,196},{5,197},{6,198},{7,199},{8... | collective-permute-start | bytes 4718600 | tf_op jit(solution)/shard_map/ppermute | solution.py:53
  52.9 1.1 copy-done.22
  54.0 1.1 collective-permute-start.10
  55.2 1.5 collective-permute-start.12
  56.7 1.4 collective-permute-start.11
  58.1 27.3 %collective-permute-done.7.up = bf16[256,3072]{1,0:T(8,128)(2,1)S(1)} collective-permute-done((bf16[256,3072]{1,0:T(8,128)(2,1)S(1)}, bf16[256,3072]{1,0:T(8,128)(2,1)S(1)}, u32[]{:S(2)}, u32[]{:S(2)}) %collective-permute-start.7) | collective-permute-done | bytes 1572896 | tf_op jit(solution)/shard_map/ppermute | solution.py:53
  85.5 1.0 slice.81
  86.5 2.5 %collective-permute-start.9 = (bf16[128,3072]{1,0:T(8,128)(2,1)}, bf16[128,3072]{1,0:T(8,128)(2,1)}, u32[]{:S(2)}, u32[]{:S(2)}) collective-permute-start(bf16[128,3072]{1,0:T(8,128)(2,1)} %slice.81), channel_id=1, source_target_pairs={{0,192},{1,193},{2,194},{3,195},{4,196},{5,197},{6,198},{7,199},{8... | collective-permute-start | bytes 2359304 | tf_op jit(solution)/shard_map/ppermute | solution.py:53
  89.0 0.9 slice.80
  90.0 1.1 copy-done.18
  91.1 15.4 %collective-permute-done.10.p1 = bf16[3,192,1024]{2,1,0:T(8,128)(2,1)} collective-permute-done((bf16[3,192,1024]{2,1,0:T(8,128)(2,1)}, bf16[3,192,1024]{2,1,0:T(8,128)(2,1)}, u32[]{:S(2)}, u32[]{:S(2)}) %collective-permute-start.10) | collective-permute-done | bytes 1179680 | tf_op jit(solution)/shard_map/ppermute | solution.py:53
  107.1 1.0 copy-done.11
  108.1 1.0 copy-done.14
  109.1 1.0 copy-done.20
  110.1 2.8 %arrange.3 = bf16[3072,512]{1,0:T(8,128)(2,1)S(1)} custom-call(s32[3]{0:T(128)S(1)} %copy-done.26, s32[1]{0:T(128)} %bitcast.5.half, bf16[192,1024]{1,0:T(8,128)(2,1)S(1)} %copy-done.20, bf16[2,192,1024]{2,1,0:T(8,128)(2,1)S(1)} %collective-permute-done.1.down.s1, bf16[2,192,1024]{2,1,0:T(8,128)(2,1)S(1)} %collective-permute-done.2.up.s2, ...), custom_call_target="tpu_custom_call" | custom-call | bytes 6291456 | tf_op jit(solution)/shard_map/arrange/pallas_call | solution.py:232
  113.1 2.4 %join.1 = bf16[1024,3072]{1,0:T(8,128)(2,1)S(1)} custom-call(s32[3]{0:T(128)S(1)} %copy-done.26, bf16[256,3072]{1,0:T(8,128)(2,1)S(1)} %copy-done.23, bf16[256,3072]{1,0:T(8,128)(2,1)S(1)} %copy-done.19, bf16[256,3072]{1,0:T(8,128)(2,1)S(1)} %copy-done.17, bf16[128,3072]{1,0:T(8,128)(2,1)} %collective-permute-done.8.far0, ...), custom_call_target="tpu_custom_call" | custom-call | bytes 6291456 | tf_op jit(solution)/shard_map/join/pallas_call | solution.py:187
  115.5 3.4 %fusion.17 = f32[1024,512]{1,0:T(8,128)S(1)} fusion(bf16[1024,3072]{1,0:T(8,128)(2,1)S(1)} %join.1, bf16[3072,512]{1,0:T(8,128)(2,1)S(1)} %arrange.3), kind=kOutput, calls=%fused_computation.29 | convolution fusion | flops 3221225472 | bytes 11534336 | tf_op jit(solution)/shard_map/dot_general | solution.py:288
  120.0 2.5 %arrange.2 = bf16[3072,512]{1,0:T(8,128)(2,1)S(1)} custom-call(s32[3]{0:T(128)S(1)} %copy-done.26, s32[1]{0:T(128)} %bitcast.4.half, bf16[192,1024]{1,0:T(8,128)(2,1)S(1)} %copy-done.21, bf16[2,192,1024]{2,1,0:T(8,128)(2,1)S(1)} %copy-done.5, bf16[2,192,1024]{2,1,0:T(8,128)(2,1)S(1)} %copy-done.7, bf16[2,192,1024]{2,1,0:T(8,128)(2,1)S(1)} %copy-done.9, ...), custom_call_target="tpu_custom_call" | custom-call | bytes 6291456 | tf_op jit(solution)/shard_map/arrange/pallas_call | solution.py:232
  125.3 1.9 %collective-permute-start.14 = (f32[64,512]{1,0:T(8,128)S(1)}, f32[64,512]{1,0:T(8,128)S(1)}, u32[]{:S(2)}, u32[]{:S(2)}) collective-permute-start(f32[64,512]{1,0:T(8,128)S(1)} %get-tuple-element.23), channel_id=1, source_target_pairs={{0,2},{1,3},{2,4},{3,5},{4,6},{5,7},{6,8},{7,9},{8,10},{9,11},{10,... | collective-permute-start | bytes 393224 | tf_op jit(solution)/shard_map/ppermute | solution.py:53
  127.3 3.1 %collective-permute-done.18 = f32[64,512]{1,0:T(8,128)S(1)} collective-permute-done((f32[64,512]{1,0:T(8,128)S(1)}, f32[64,512]{1,0:T(8,128)S(1)}, u32[]{:S(2)}, u32[]{:S(2)}) %collective-permute-start.18) | collective-permute-done | bytes 131104 | tf_op jit(solution)/shard_map/ppermute | solution.py:53
  130.4 1.9 %fusion.7 = f32[128,512]{1,0:T(8,128)S(1)} fusion(bf16[3072,512]{1,0:T(8,128)(2,1)S(1)} %arrange.2, bf16[1024,3072]{1,0:T(8,128)(2,1)} %copy-done, f32[1024,512]{1,0:T(8,128)} %copy-done.27, f32[64,512]{1,0:T(8,128)S(1)} %collective-permute-done.18), kind=kOutput, calls=%fused_computation.15 | convolution fusion | flops 402784256 | bytes 4587520 | tf_op jit(solution)/shard_map/dot_general | solution.py:294
  132.3 3.4 %collective-permute-start.19 = (f32[128,512]{1,0:T(8,128)S(1)}, f32[128,512]{1,0:T(8,128)S(1)}, u32[]{:S(2)}, u32[]{:S(2)}) collective-permute-start(f32[128,512]{1,0:T(8,128)S(1)} %fusion.7), channel_id=1, source_target_pairs={{0,14},{1,15},{2,0},{3,1},{4,2},{5,3},{6,4},{7,5},{8,6},{9,7},{10,... | collective-permute-start | bytes 786440 | tf_op jit(solution)/shard_map/ppermute | solution.py:53
  135.7 1.7 fusion.4
  137.5 3.2 %collective-permute-done.19 = f32[128,512]{1,0:T(8,128)S(1)} collective-permute-done((f32[128,512]{1,0:T(8,128)S(1)}, f32[128,512]{1,0:T(8,128)S(1)}, u32[]{:S(2)}, u32[]{:S(2)}) %collective-permute-start.19) | collective-permute-done | bytes 262176 | tf_op jit(solution)/shard_map/ppermute | solution.py:53
  141.3 3.8 %collective-permute-start.20 = (f32[128,512]{1,0:T(8,128)S(1)}, f32[128,512]{1,0:T(8,128)S(1)}, u32[]{:S(2)}, u32[]{:S(2)}) collective-permute-start(f32[128,512]{1,0:T(8,128)S(1)} %fusion.6), channel_id=1, source_target_pairs={{0,14},{1,15},{2,0},{3,1},{4,2},{5,3},{6,4},{7,5},{8,6},{9,7},{10,... | collective-permute-start | bytes 786440 | tf_op jit(solution)/shard_map/ppermute | solution.py:53
  145.1 1.6 collective-permute-done.15
  147.4 2.1 %collective-permute-done.20 = f32[128,512]{1,0:T(8,128)S(1)} collective-permute-done((f32[128,512]{1,0:T(8,128)S(1)}, f32[128,512]{1,0:T(8,128)S(1)}, u32[]{:S(2)}, u32[]{:S(2)}) %collective-permute-start.20) | collective-permute-done | bytes 262176 | tf_op jit(solution)/shard_map/ppermute | solution.py:53
  149.5 1.3 fusion.5
  150.8 3.4 %collective-permute-start.21 = (f32[128,512]{1,0:T(8,128)}, f32[128,512]{1,0:T(8,128)S(1)}, u32[]{:S(2)}, u32[]{:S(2)}) collective-permute-start(f32[128,512]{1,0:T(8,128)} %fusion.5), channel_id=1, source_target_pairs={{0,14},{1,15},{2,0},{3,1},{4,2},{5,3},{6,4},{7,5},{8,6},{9,7},{10,... | collective-permute-start | bytes 786440 | tf_op jit(solution)/shard_map/ppermute | solution.py:53
  154.9 1.3 fusion.2
  157.1 1.3 collective-permute-done.21
  158.4 5.4 %collective-permute-done.17 = f32[128,512]{1,0:T(8,128)} collective-permute-done((f32[128,512]{1,0:T(8,128)}, f32[128,512]{1,0:T(8,128)}, u32[]{:S(2)}, u32[]{:S(2)}) %collective-permute-start.17) | collective-permute-done | bytes 262176 | tf_op jit(solution)/shard_map/ppermute | solution.py:53
  163.8 1.9 %fusion.1.total = f32[128,512]{1,0:T(8,128)S(1)} fusion(f32[128,512]{1,0:T(8,128)S(1)} %collective-permute-done.21, f32[128,512]{1,0:T(8,128)} %collective-permute-done.17, bf16[3072,512]{1,0:T(8,128)(2,1)S(1)} %arrange.2, bf16[1024,3072]{1,0:T(8,128)(2,1)} %copy-done, f32[1024,512]{1,0:T(8,128)} %copy-done.27), kind=kOutput, calls=%fused_computation.9 | convolution fusion | flops 402849792 | bytes 4980736 | tf_op jit(solution)/shard_map/dot_general | solution.py:294
  165.9 1.9 %collective-permute-start.22 = (bf16[512,128]{1,0:T(8,128)(2,1)S(1)}, bf16[512,128]{1,0:T(8,128)(2,1)S(1)}, u32[]{:S(2)}, u32[]{:S(2)}) collective-permute-start(bf16[512,128]{1,0:T(8,128)(2,1)S(1)} %finish.1), channel_id=1, source_target_pairs={{0,0},{1,48},{2,1},{3,49},{4,4},{5,52},{6,5},{7,53},{8,8},{9,56},{... | collective-permute-start | bytes 393224 | tf_op jit(solution)/shard_map/ppermute | solution.py:53
  167.8 7.6 %collective-permute-done.22 = bf16[512,128]{1,0:T(8,128)(2,1)S(1)} collective-permute-done((bf16[512,128]{1,0:T(8,128)(2,1)S(1)}, bf16[512,128]{1,0:T(8,128)(2,1)S(1)}, u32[]{:S(2)}, u32[]{:S(2)}) %collective-permute-start.22) | collective-permute-done | bytes 131104 | tf_op jit(solution)/shard_map/ppermute | solution.py:53
  (88 shorter events, 9.1 us)
Async XLA Ops:
  5.5 41.9 %collective-permute-start = (bf16[192,3072]{1,0:T(8,128)(2,1)}, bf16[192,3072]{1,0:T(8,128)(2,1)S(1)}, u32[]{:S(2)}, u32[]{:S(2)}) collective-permute-start(bf16[192,3072]{1,0:T(8,128)(2,1)} %get-tuple-element.14.near), channel_id=1, source_target_pairs={{0,16},{1,17},{2,18},{3,19},{4,20},{5,21},{6,22},{7,23},{8,24},{9,... | collective-permute-start | bytes 3538952 | tf_op jit(solution)/shard_map/ppermute | solution.py:53
  7.1 12.0 %collective-permute-start.4 = (bf16[192,1024]{1,0:T(8,128)(2,1)}, bf16[192,1024]{1,0:T(8,128)(2,1)S(1)}, u32[]{:S(2)}, u32[]{:S(2)}) collective-permute-start(bf16[192,1024]{1,0:T(8,128)(2,1)} %get-tuple-element.18.s0), channel_id=1, source_target_pairs={{0,48},{1,49},{2,50},{3,51},{4,52},{5,53},{6,54},{7,55},{8,56},{9,... | collective-permute-start | bytes 1179656 | tf_op jit(solution)/shard_map/ppermute | solution.py:53
  9.2 35.0 %collective-permute-start.1 = (bf16[2,192,1024]{2,1,0:T(8,128)(2,1)}, bf16[2,192,1024]{2,1,0:T(8,128)(2,1)S(1)}, u32[]{:S(2)}, u32[]{:S(2)}) collective-permute-start(bf16[2,192,1024]{2,1,0:T(8,128)(2,1)} %get-tuple-element.15), channel_id=1, source_target_pairs={{0,64},{1,65},{2,66},{3,67},{4,68},{5,69},{6,70},{7,71},{8,72},{9,... | collective-permute-start | bytes 2359304 | tf_op jit(solution)/shard_map/ppermute | solution.py:53
  10.8 33.4 %collective-permute-start.2 = (bf16[2,192,1024]{2,1,0:T(8,128)(2,1)}, bf16[2,192,1024]{2,1,0:T(8,128)(2,1)S(1)}, u32[]{:S(2)}, u32[]{:S(2)}) collective-permute-start(bf16[2,192,1024]{2,1,0:T(8,128)(2,1)} %get-tuple-element.16), channel_id=1, source_target_pairs={{0,192},{1,193},{2,194},{3,195},{4,196},{5,197},{6,198},{7,199},{8... | collective-permute-start | bytes 2359304 | tf_op jit(solution)/shard_map/ppermute | solution.py:53
  12.5 35.0 %collective-permute-start.3 = (bf16[2,192,1024]{2,1,0:T(8,128)(2,1)}, bf16[2,192,1024]{2,1,0:T(8,128)(2,1)S(1)}, u32[]{:S(2)}, u32[]{:S(2)}) collective-permute-start(bf16[2,192,1024]{2,1,0:T(8,128)(2,1)} %get-tuple-element.17), channel_id=1, source_target_pairs={{0,128},{1,129},{2,130},{3,131},{4,132},{5,133},{6,134},{7,135},{8... | collective-permute-start | bytes 2359304 | tf_op jit(solution)/shard_map/ppermute | solution.py:53
  19.1 31.7 %copy-start.10 = (bf16[192,1024]{1,0:T(8,128)(2,1)}, bf16[192,1024]{1,0:T(8,128)(2,1)S(1)}, u32[]{:S(2)}) copy-start(bf16[192,1024]{1,0:T(8,128)(2,1)S(1)} %collective-permute-done.4.after.p0) | copy-start | bytes 1179652
  20.3 86.8 %copy-start.26 = (s32[3]{0:T(128)S(1)}, s32[3]{0:T(128)}, u32[]{:S(2)}) copy-start(s32[3]{0:T(128)} %pad_add_fusion.place) | copy-start | bytes 40
  20.3 23.9 %collective-permute-start.5 = (bf16[192,1024]{1,0:T(8,128)(2,1)S(1)}, bf16[192,1024]{1,0:T(8,128)(2,1)S(1)}, u32[]{:S(2)}, u32[]{:S(2)}) collective-permute-start(bf16[192,1024]{1,0:T(8,128)(2,1)S(1)} %follow.1), channel_id=1, source_target_pairs={{0,32},{1,33},{2,34},{3,35},{4,36},{5,37},{6,38},{7,39},{8,40},{9,... | collective-permute-start | bytes 1179656 | tf_op jit(solution)/shard_map/ppermute | solution.py:53
  44.2 42.3 %copy-start.13 = (bf16[192,1024]{1,0:T(8,128)(2,1)}, bf16[192,1024]{1,0:T(8,128)(2,1)S(1)}, u32[]{:S(2)}) copy-start(bf16[192,1024]{1,0:T(8,128)(2,1)S(1)} %collective-permute-done.5.x0) | copy-start | bytes 1179652
  44.2 62.9 %copy-start.4 = (bf16[2,192,1024]{2,1,0:T(8,128)(2,1)}, bf16[2,192,1024]{2,1,0:T(8,128)(2,1)S(1)}, u32[]{:S(2)}) copy-start(bf16[2,192,1024]{2,1,0:T(8,128)(2,1)S(1)} %collective-permute-done.1.down.s1) | copy-start | bytes 2359300
  44.2 62.9 %copy-start.6 = (bf16[2,192,1024]{2,1,0:T(8,128)(2,1)}, bf16[2,192,1024]{2,1,0:T(8,128)(2,1)S(1)}, u32[]{:S(2)}) copy-start(bf16[2,192,1024]{2,1,0:T(8,128)(2,1)S(1)} %collective-permute-done.2.up.s2) | copy-start | bytes 2359300
  47.5 59.6 %copy-start.8 = (bf16[2,192,1024]{2,1,0:T(8,128)(2,1)}, bf16[2,192,1024]{2,1,0:T(8,128)(2,1)S(1)}, u32[]{:S(2)}) copy-start(bf16[2,192,1024]{2,1,0:T(8,128)(2,1)S(1)} %collective-permute-done.3.over.s3) | copy-start | bytes 2359300
  47.5 1.6 copy-start.24
  49.0 58.1 %copy-start.2 = (bf16[192,3072]{1,0:T(8,128)(2,1)}, bf16[192,3072]{1,0:T(8,128)(2,1)S(1)}, u32[]{:S(2)}) copy-start(bf16[192,3072]{1,0:T(8,128)(2,1)S(1)} %collective-permute-done.from_near.c0) | copy-start | bytes 3538948
  50.8 34.6 %collective-permute-start.7 = (bf16[256,3072]{1,0:T(8,128)(2,1)S(1)}, bf16[256,3072]{1,0:T(8,128)(2,1)S(1)}, u32[]{:S(2)}, u32[]{:S(2)}) collective-permute-start(bf16[256,3072]{1,0:T(8,128)(2,1)S(1)} %get-tuple-element.20.here), channel_id=1, source_target_pairs={{0,192},{1,193},{2,194},{3,195},{4,196},{5,197},{6,198},{7,199},{8... | collective-permute-start | bytes 4718600 | tf_op jit(solution)/shard_map/ppermute | solution.py:53
  52.9 36.1 %collective-permute-start.6 = (bf16[256,3072]{1,0:T(8,128)(2,1)S(1)}, bf16[256,3072]{1,0:T(8,128)(2,1)S(1)}, u32[]{:S(2)}, u32[]{:S(2)}) collective-permute-start(bf16[256,3072]{1,0:T(8,128)(2,1)S(1)} %get-tuple-element.20.here), channel_id=1, source_target_pairs={{0,64},{1,65},{2,66},{3,67},{4,68},{5,69},{6,70},{7,71},{8,72},{9,... | collective-permute-start | bytes 4718600 | tf_op jit(solution)/shard_map/ppermute | solution.py:53
  54.0 52.4 %collective-permute-start.10 = (bf16[3,192,1024]{2,1,0:T(8,128)(2,1)}, bf16[3,192,1024]{2,1,0:T(8,128)(2,1)}, u32[]{:S(2)}, u32[]{:S(2)}) collective-permute-start(bf16[3,192,1024]{2,1,0:T(8,128)(2,1)} %get-tuple-element.21), channel_id=1, source_target_pairs={{0,48},{1,49},{2,50},{3,51},{4,52},{5,53},{6,54},{7,55},{8,56},{9,... | collective-permute-start | bytes 3538952 | tf_op jit(solution)/shard_map/ppermute | solution.py:53
  55.2 51.3 %collective-permute-start.12 = (bf16[3,192,1024]{2,1,0:T(8,128)(2,1)}, bf16[3,192,1024]{2,1,0:T(8,128)(2,1)}, u32[]{:S(2)}, u32[]{:S(2)}) collective-permute-start(bf16[3,192,1024]{2,1,0:T(8,128)(2,1)} %get-tuple-element.22), channel_id=1, source_target_pairs={{0,32},{1,33},{2,34},{3,35},{4,36},{5,37},{6,38},{7,39},{8,40},{9,... | collective-permute-start | bytes 3538952 | tf_op jit(solution)/shard_map/ppermute | solution.py:53
  56.7 50.4 %collective-permute-start.11 = (bf16[3,192,1024]{2,1,0:T(8,128)(2,1)}, bf16[3,192,1024]{2,1,0:T(8,128)(2,1)}, u32[]{:S(2)}, u32[]{:S(2)}) collective-permute-start(bf16[3,192,1024]{2,1,0:T(8,128)(2,1)} %get-tuple-element.22), channel_id=1, source_target_pairs={{0,16},{1,17},{2,18},{3,19},{4,20},{5,21},{6,22},{7,23},{8,24},{9,... | collective-permute-start | bytes 3538952 | tf_op jit(solution)/shard_map/ppermute | solution.py:53
  85.5 3.5 %copy-start.16 = (bf16[256,3072]{1,0:T(8,128)(2,1)}, bf16[256,3072]{1,0:T(8,128)(2,1)S(1)}, u32[]{:S(2)}) copy-start(bf16[256,3072]{1,0:T(8,128)(2,1)S(1)} %collective-permute-done.7.up) | copy-start | bytes 4718596
  86.5 26.4 %collective-permute-start.9 = (bf16[128,3072]{1,0:T(8,128)(2,1)}, bf16[128,3072]{1,0:T(8,128)(2,1)}, u32[]{:S(2)}, u32[]{:S(2)}) collective-permute-start(bf16[128,3072]{1,0:T(8,128)(2,1)} %slice.81), channel_id=1, source_target_pairs={{0,192},{1,193},{2,194},{3,195},{4,196},{5,197},{6,198},{7,199},{8... | collective-permute-start | bytes 2359304 | tf_op jit(solution)/shard_map/ppermute | solution.py:53
  91.1 21.9 %collective-permute-start.8 = (bf16[128,3072]{1,0:T(8,128)(2,1)}, bf16[128,3072]{1,0:T(8,128)(2,1)}, u32[]{:S(2)}, u32[]{:S(2)}) collective-permute-start(bf16[128,3072]{1,0:T(8,128)(2,1)} %slice.80), channel_id=1, source_target_pairs={{0,64},{1,65},{2,66},{3,67},{4,68},{5,69},{6,70},{7,71},{8,72},{9,... | collective-permute-start | bytes 2359304 | tf_op jit(solution)/shard_map/ppermute | solution.py:53
  110.1 2.9 %copy-start.17 = (bf16[256,3072]{1,0:T(8,128)(2,1)S(1)}, bf16[256,3072]{1,0:T(8,128)(2,1)}, u32[]{:S(2)}) copy-start(bf16[256,3072]{1,0:T(8,128)(2,1)} %copy-done.16) | copy-start | bytes 4718596
  110.1 2.9 %copy-start.19 = (bf16[256,3072]{1,0:T(8,128)(2,1)S(1)}, bf16[256,3072]{1,0:T(8,128)(2,1)}, u32[]{:S(2)}) copy-start(bf16[256,3072]{1,0:T(8,128)(2,1)} %copy-done.18) | copy-start | bytes 4718596
  110.1 3.0 %copy-start.23 = (bf16[256,3072]{1,0:T(8,128)(2,1)S(1)}, bf16[256,3072]{1,0:T(8,128)(2,1)}, u32[]{:S(2)}) copy-start(bf16[256,3072]{1,0:T(8,128)(2,1)} %copy-done.22) | copy-start | bytes 4718596
  115.5 7.7 %copy-start = (bf16[1024,3072]{1,0:T(8,128)(2,1)}, bf16[1024,3072]{1,0:T(8,128)(2,1)S(1)}, u32[]{:S(2)}) copy-start(bf16[1024,3072]{1,0:T(8,128)(2,1)S(1)} %join.1) | copy-start | bytes 18874372
  115.5 3.6 %copy-start.3 = (bf16[192,3072]{1,0:T(8,128)(2,1)S(1)}, bf16[192,3072]{1,0:T(8,128)(2,1)}, u32[]{:S(2)}) copy-start(bf16[192,3072]{1,0:T(8,128)(2,1)} %copy-done.2) | copy-start | bytes 3538948
  115.5 3.6 %copy-start.5 = (bf16[2,192,1024]{2,1,0:T(8,128)(2,1)S(1)}, bf16[2,192,1024]{2,1,0:T(8,128)(2,1)}, u32[]{:S(2)}) copy-start(bf16[2,192,1024]{2,1,0:T(8,128)(2,1)} %copy-done.4) | copy-start | bytes 2359300
  115.5 3.8 %copy-start.7 = (bf16[2,192,1024]{2,1,0:T(8,128)(2,1)S(1)}, bf16[2,192,1024]{2,1,0:T(8,128)(2,1)}, u32[]{:S(2)}) copy-start(bf16[2,192,1024]{2,1,0:T(8,128)(2,1)} %copy-done.6) | copy-start | bytes 2359300
  115.5 4.2 %copy-start.9 = (bf16[2,192,1024]{2,1,0:T(8,128)(2,1)S(1)}, bf16[2,192,1024]{2,1,0:T(8,128)(2,1)}, u32[]{:S(2)}) copy-start(bf16[2,192,1024]{2,1,0:T(8,128)(2,1)} %copy-done.8) | copy-start | bytes 2359300
  115.5 4.3 %copy-start.12 = (bf16[192,1024]{1,0:T(8,128)(2,1)S(1)}, bf16[192,1024]{1,0:T(8,128)(2,1)}, u32[]{:S(2)}) copy-start(bf16[192,1024]{1,0:T(8,128)(2,1)} %copy-done.10) | copy-start | bytes 1179652
  115.5 4.4 %copy-start.15 = (bf16[192,1024]{1,0:T(8,128)(2,1)S(1)}, bf16[192,1024]{1,0:T(8,128)(2,1)}, u32[]{:S(2)}) copy-start(bf16[192,1024]{1,0:T(8,128)(2,1)} %copy-done.13) | copy-start | bytes 1179652
  115.5 4.5 %copy-start.21 = (bf16[192,1024]{1,0:T(8,128)(2,1)S(1)}, bf16[192,1024]{1,0:T(8,128)(2,1)}, u32[]{:S(2)}) copy-start(bf16[192,1024]{1,0:T(8,128)(2,1)} %get-tuple-element.18.s0) | copy-start | bytes 1179652
  118.9 4.2 %collective-permute-start.13 = (f32[1024,512]{1,0:T(8,128)S(1)}, f32[1024,512]{1,0:T(8,128)S(1)}, u32[]{:S(2)}, u32[]{:S(2)}) collective-permute-start(f32[1024,512]{1,0:T(8,128)S(1)} %fusion.17), channel_id=1, source_target_pairs={{0,1},{1,0},{2,3},{3,2},{4,5},{5,4},{6,7},{7,6},{8,9},{9,8},{10,11... | collective-permute-start | bytes 6291464 | tf_op jit(solution)/shard_map/ppermute | solution.py:53
  122.5 2.2 %copy-start.30 = (f32[4]{0:T(128)S(1)}, f32[4]{0:T(128)}, u32[]{:S(2)}) copy-start(f32[4]{0:T(128)} %param.12) | copy-start | bytes 52
  124.6 5.8 %collective-permute-start.18 = (f32[64,512]{1,0:T(8,128)S(1)}, f32[64,512]{1,0:T(8,128)S(1)}, u32[]{:S(2)}, u32[]{:S(2)}) collective-permute-start(f32[64,512]{1,0:T(8,128)S(1)} %get-tuple-element.24), channel_id=1, source_target_pairs={{0,14},{1,15},{2,0},{3,1},{4,2},{5,3},{6,4},{7,5},{8,6},{9,7},{10,... | collective-permute-start | bytes 393224 | tf_op jit(solution)/shard_map/ppermute | solution.py:53
  124.8 10.9 %copy-start.28 = (f32[1024,512]{1,0:T(8,128)S(1)}, f32[1024,512]{1,0:T(8,128)}, u32[]{:S(2)}) copy-start(f32[1024,512]{1,0:T(8,128)} %copy-done.27) | copy-start | bytes 6291460
  125.3 10.3 %collective-permute-start.14 = (f32[64,512]{1,0:T(8,128)S(1)}, f32[64,512]{1,0:T(8,128)S(1)}, u32[]{:S(2)}, u32[]{:S(2)}) collective-permute-start(f32[64,512]{1,0:T(8,128)S(1)} %get-tuple-element.23), channel_id=1, source_target_pairs={{0,2},{1,3},{2,4},{3,5},{4,6},{5,7},{6,8},{7,9},{8,10},{9,11},{10,... | collective-permute-start | bytes 393224 | tf_op jit(solution)/shard_map/ppermute | solution.py:53
  130.4 10.4 %copy-start.1 = (bf16[1024,3072]{1,0:T(8,128)(2,1)S(1)}, bf16[1024,3072]{1,0:T(8,128)(2,1)}, u32[]{:S(2)}) copy-start(bf16[1024,3072]{1,0:T(8,128)(2,1)} %copy-done) | copy-start | bytes 18874372
  132.3 8.4 %collective-permute-start.19 = (f32[128,512]{1,0:T(8,128)S(1)}, f32[128,512]{1,0:T(8,128)S(1)}, u32[]{:S(2)}, u32[]{:S(2)}) collective-permute-start(f32[128,512]{1,0:T(8,128)S(1)} %fusion.7), channel_id=1, source_target_pairs={{0,14},{1,15},{2,0},{3,1},{4,2},{5,3},{6,4},{7,5},{8,6},{9,7},{10,... | collective-permute-start | bytes 786440 | tf_op jit(solution)/shard_map/ppermute | solution.py:53
  137.4 9.3 %collective-permute-start.15 = (f32[128,512]{1,0:T(8,128)S(1)}, f32[128,512]{1,0:T(8,128)S(1)}, u32[]{:S(2)}, u32[]{:S(2)}) collective-permute-start(f32[128,512]{1,0:T(8,128)S(1)} %fusion.4), channel_id=1, source_target_pairs={{0,2},{1,3},{2,4},{3,5},{4,6},{5,7},{6,8},{7,9},{8,10},{9,11},{10,... | collective-permute-start | bytes 786440 | tf_op jit(solution)/shard_map/ppermute | solution.py:53
  141.3 8.1 %collective-permute-start.20 = (f32[128,512]{1,0:T(8,128)S(1)}, f32[128,512]{1,0:T(8,128)S(1)}, u32[]{:S(2)}, u32[]{:S(2)}) collective-permute-start(f32[128,512]{1,0:T(8,128)S(1)} %fusion.6), channel_id=1, source_target_pairs={{0,14},{1,15},{2,0},{3,1},{4,2},{5,3},{6,4},{7,5},{8,6},{9,7},{10,... | collective-permute-start | bytes 786440 | tf_op jit(solution)/shard_map/ppermute | solution.py:53
  147.3 7.6 %collective-permute-start.16 = (f32[128,512]{1,0:T(8,128)S(1)}, f32[128,512]{1,0:T(8,128)S(1)}, u32[]{:S(2)}, u32[]{:S(2)}) collective-permute-start(f32[128,512]{1,0:T(8,128)S(1)} %fusion.3), channel_id=1, source_target_pairs={{0,2},{1,3},{2,4},{3,5},{4,6},{5,7},{6,8},{7,9},{8,10},{9,11},{10,... | collective-permute-start | bytes 786440 | tf_op jit(solution)/shard_map/ppermute | solution.py:53
  150.8 5.4 %copy-start.29 = (f32[4,128]{1,0:T(4,128)S(1)}, f32[4,128]{1,0:T(4,128)}, u32[]{:S(2)}) copy-start(f32[4,128]{1,0:T(4,128)} %param.13) | copy-start | bytes 6148
  150.8 6.2 %copy-start.31 = (f32[16]{0:T(128)S(1)}, f32[16]{0:T(128)}, u32[]{:S(2)}) copy-start(f32[16]{0:T(128)} %param.11) | copy-start | bytes 196
  150.8 7.6 %collective-permute-start.21 = (f32[128,512]{1,0:T(8,128)}, f32[128,512]{1,0:T(8,128)S(1)}, u32[]{:S(2)}, u32[]{:S(2)}) collective-permute-start(f32[128,512]{1,0:T(8,128)} %fusion.5), channel_id=1, source_target_pairs={{0,14},{1,15},{2,0},{3,1},{4,2},{5,3},{6,4},{7,5},{8,6},{9,7},{10,... | collective-permute-start | bytes 786440 | tf_op jit(solution)/shard_map/ppermute | solution.py:53
  156.2 7.7 %collective-permute-start.17 = (f32[128,512]{1,0:T(8,128)}, f32[128,512]{1,0:T(8,128)}, u32[]{:S(2)}, u32[]{:S(2)}) collective-permute-start(f32[128,512]{1,0:T(8,128)} %fusion.2), channel_id=1, source_target_pairs={{0,2},{1,3},{2,4},{3,5},{4,6},{5,7},{6,8},{7,9},{8,10},{9,11},{10,... | collective-permute-start | bytes 786440 | tf_op jit(solution)/shard_map/ppermute | solution.py:53
  165.9 9.5 %collective-permute-start.22 = (bf16[512,128]{1,0:T(8,128)(2,1)S(1)}, bf16[512,128]{1,0:T(8,128)(2,1)S(1)}, u32[]{:S(2)}, u32[]{:S(2)}) collective-permute-start(bf16[512,128]{1,0:T(8,128)(2,1)S(1)} %finish.1), channel_id=1, source_target_pairs={{0,0},{1,48},{2,1},{3,49},{4,4},{5,52},{6,5},{7,53},{8,8},{9,56},{... | collective-permute-start | bytes 393224 | tf_op jit(solution)/shard_map/ppermute | solution.py:53
  (7 other events, 7.8 us)

commit v4 on v3

--- a/solution.py
+++ b/solution.py
@@ -111,7 +111,7 @@
                 pltpu.SemaphoreType.DMA((5,)),
             ],
         ),
-        compiler_params=pltpu.CompilerParams(vmem_limit_bytes=58 << 20),
+        compiler_params=pltpu.CompilerParams(vmem_limit_bytes=55 << 20),
         cost_estimate=pl.CostEstimate(flops=0, bytes_accessed=8 << 20, transcendentals=0),
         name="prepare",
     )(place, amp_mask, int_mask.T, a, b)
@@ -135,28 +135,33 @@
     )(value, after)
 
 
-def gather_kernel(near, from_near, down, up, over, p0, x0, own_rest, oth_rest, b_here):
-    del p0, x0
+def gather_kernel(
+    near, from_near, down, up, over, own, p0, x0, own_rest, oth_rest, b_here, early
+):
     for j, ref in enumerate((down, up, over)):
         own_rest[j] = ref[0]
         oth_rest[j] = ref[1]
     b_here[pl.ds(0, 128), :] = near[...]
-    b_here[pl.ds(128, 128), :] = from_near[...]
+    b_here[pl.ds(128, 128), :] = from_near[pl.ds(0, 128), :]
+    for j, ref in ((0, own), (1, p0), (3, x0)):
+        early[j] = ref[...]
+    for k in range(3):
+        early[2, pl.ds(k * 64, 64), :] = from_near[pl.ds(128, 64), pl.ds(k * 2 * RB, 2 * RB)]
 
 
 def gather(*parts):
-    rest = jax.ShapeDtypeStruct((3, KD, 2 * RB), jnp.bfloat16)
+    def stack(n):
+        return jax.ShapeDtypeStruct((n, KD, 2 * RB), jnp.bfloat16)
+
     vmem = pl.BlockSpec(memory_space=VMEM)
-    slab = pl.BlockSpec((128, KT), lambda i: (0, 0))
-    anywhere = pl.BlockSpec(memory_space=pl.ANY)
     return pl.pallas_call(
         gather_kernel,
-        out_shape=(rest, rest, jax.ShapeDtypeStruct((256, KT), jnp.bfloat16)),
+        out_shape=(stack(3), stack(3), jax.ShapeDtypeStruct((256, KT), jnp.bfloat16), stack(4)),
         grid=(1,),
-        in_specs=[slab, slab, vmem, vmem, vmem, anywhere, anywhere],
-        out_specs=(vmem,) * 3,
-        compiler_params=pltpu.CompilerParams(vmem_limit_bytes=16 << 20),
-        cost_estimate=pl.CostEstimate(flops=0, bytes_accessed=8 << 20, transcendentals=0),
+        in_specs=[pl.BlockSpec((128, KT), lambda i: (0, 0))] + [vmem] * 7,
+        out_specs=(vmem,) * 4,
+        compiler_params=pltpu.CompilerParams(vmem_limit_bytes=20 << 20),
+        cost_estimate=pl.CostEstimate(flops=0, bytes_accessed=10 << 20, transcendentals=0),
         name="gather",
     )(*parts)
 
@@ -200,31 +205,16 @@
     )(place, *parts)
 
 
-def arrange_kernel(place, half, s0, s1, s2, s3, p0, p1, c0, c1, x0, x1, out, sems):
+def arrange_kernel(place, half, early, own_rest, p1, c1, x1, out, sems):
     y, x = place[0], place[1]
-    first = pl.multiple_of(half[0] * RB, RB)
-    lanes = pl.ds(first, RB)
+    lanes = pl.ds(pl.multiple_of(half[0] * RB, RB), RB)
+    around = (lax.rem(y + 3, 4), lax.rem(y + 1, 4), lax.rem(y + 2, 4))
+    sources = (x, 3 - x, x + 1 - 2 * lax.rem(x, 2), lax.rem(x + 2, 4))
     moves = []
-
-    def put(ref, from_x, from_y):
-        at = pl.multiple_of((from_x * 4 + from_y) * KD, KD)
-        moves.append((ref.at[:, lanes], out.at[pl.ds(at, KD), :]))
-
-    around = (lax.rem(y + 3, 4), lax.rem(y + 1, 4), lax.rem(y + 2, 4))
-    put(s0, x, y)
-    for ref, from_y in zip((s1, s2, s3), around):
-        put(ref.at[0], x, from_y)
-    far = lax.rem(x + 2, 4)
-    near = x + 1 - 2 * lax.rem(x, 2)
-    put(p0, 3 - x, y)
-    at = pl.multiple_of((near * 4 + y) * KD, KD)
-    for k in range(3):
-        source = pl.ds(pl.multiple_of(k * 2 * RB + first, RB), RB)
-        moves.append((c0.at[pl.ds(128, 64), source], out.at[pl.ds(at + k * 64, 64), :]))
-    put(x0, far, y)
-    for late, from_x in ((p1, 3 - x), (c1, near), (x1, far)):
-        for j, from_y in enumerate(around):
-            put(late.at[j], from_x, from_y)
+    for j, (rest, from_x) in enumerate(zip((own_rest, p1, c1, x1), sources)):
+        for ref, from_y in ((early.at[j], y), *((rest.at[i], at) for i, at in enumerate(around))):
+            at = pl.multiple_of((from_x * 4 + from_y) * KD, KD)
+            moves.append((ref.at[:, lanes], out.at[pl.ds(at, KD), :]))
     run(moves, sems)
 
 
@@ -235,9 +225,9 @@
         grid_spec=pltpu.PrefetchScalarGridSpec(
             num_scalar_prefetch=2,
             grid=(1,),
-            in_specs=[pl.BlockSpec(memory_space=pl.ANY)] * 10,
+            in_specs=[pl.BlockSpec(memory_space=pl.ANY)] * 5,
             out_specs=pl.BlockSpec(memory_space=VMEM),
-            scratch_shapes=[pltpu.SemaphoreType.DMA((18,))],
+            scratch_shapes=[pltpu.SemaphoreType.DMA((16,))],
         ),
         compiler_params=pltpu.CompilerParams(vmem_limit_bytes=16 << 20),
         cost_estimate=pl.CostEstimate(flops=0, bytes_accessed=6 << 20, transcendentals=0),
@@ -272,7 +262,9 @@
     p0 = send(own, PARTNER)
     x0 = send(follow(oth, p0), ACROSS)
 
-    own_rest, oth_rest, b_here = gather(near, from_near, from_down, from_up, from_over, p0, x0)
+    own_rest, oth_rest, b_here, early = gather(
+        near, from_near, from_down, from_up, from_over, own, p0, x0
+    )
     b_down = send(b_here, UP)
     b_up = send(b_here, DOWN)
     p1 = send(own_rest, PARTNER)
@@ -282,7 +274,7 @@
     b_far1 = send(b_up[128:], DOWN)
     slabs = join(place, b_here, b_down, b_up, b_far0, b_far1)
 
-    amps = (own, from_down, from_up, from_over, p0, p1, from_near, c1, x0, x1)
+    amps = (early, own_rest, p1, c1, x1)
     keep_half = jnp.bitwise_xor(x // 2, core).astype(jnp.int32)
     give = arrange(place, (1 - keep_half)[None], amps)
     given = jnp.dot(slabs, give, preferred_element_type=jnp.float32)

time: 177 us -> 173 us (0.977)
  local copies, waits for them, and re-layouts: 13.3 us -> 11.2 us
    unnamed x65 -> x43, local copies, waits for them, and re-layouts: 10.5 us -> 8.52 us
  transfers between devices with their start and end apart: 23 -> 23, of which waited for: 15 -> 16; matrix products, arithmetic and copies ran while one was open for 6% -> 6% of each run, Pallas kernels for 3% -> 3%
where the time goes in v4:
time: 173 us
  waiting for transfers between devices  99.2 us (57%)
  starting transfers between devices  34 us (20%)
  Pallas kernels  13.8 us (8%)
  matrix products  13.3 us (8%)
  local copies, waits for them, and re-layouts  11.2 us (6%)
    ppermute x23, waiting for transfers between devices, send(): return lax.ppermute(value, AXES, where)  99.2 us
    ppermute x23, starting transfers between devices, send(): return lax.ppermute(value, AXES, where)  34 us
    dot_general x8, matrix products, partial(): jnp.dot(slabs[rows], keep, preferred_element_type=jnp.float32) + taken[rows]  9.87 us
    unnamed x43, local copies, waits for them, and re-layouts  8.52 us
    pallas_call x2, Pallas kernels, arrange(): pl.pallas_call(arrange_kernel, out_shape=jax.ShapeDtypeStruct((KT, RB), j...  5.09 us
    pallas_call x1, Pallas kernels, prepare(): pl.pallas_call(prepare_kernel, out_shape=(piece, piece, near, two, two, t...  4.87 us
  transfers between devices with their start and end apart: 23, of which 16 were waited for; matrix products, arithmetic and copies ran while one was open for 6% of the time, Pallas kernels for 3%

profile of v4, /device:TPU:32, one launch (start us, length us, event | category | flops | bytes accessed | tf_op | source)
XLA Modules:
  0.0 173.0 jit_solution(87423276063485161)
XLA Ops:
  0.6 4.9 %prepare.1 = (bf16[192,1024]{1,0:T(8,128)(2,1)}, bf16[192,1024]{1,0:T(8,128)(2,1)}, bf16[192,3072]{1,0:T(8,128)(2,1)}, bf16[2,192,1024]{2,1,0:T(8,128)(2,1)}, bf...) custom-call(s32[3]{0:T(128)} %pad_add_fusion.place, s32[4,8]{1,0:T(4,128)} %amp_mask.1, s32[4,8]{1,0:T(4,128)} %bitcast.23, ...), custom_call_target="tpu_custom_call" | custom-call | bytes 8388608 | tf_op jit(solution)/shard_map/prepare/pallas_call | solution.py:99
  5.5 1.6 collective-permute-start
  7.1 2.1 %collective-permute-start.4 = (bf16[192,1024]{1,0:T(8,128)(2,1)}, bf16[192,1024]{1,0:T(8,128)(2,1)S(1)}, u32[]{:S(2)}, u32[]{:S(2)}) collective-permute-start(bf16[192,1024]{1,0:T(8,128)(2,1)} %get-tuple-element.19.own), channel_id=1, source_target_pairs={{0,48},{1,49},{2,50},{3,51},{4,52},{5,53},{6,54},{7,55},{8,56},{9,... | collective-permute-start | bytes 1179656 | tf_op jit(solution)/shard_map/ppermute | solution.py:53
  9.2 1.6 collective-permute-start.1
  10.7 1.7 collective-permute-start.2
  12.4 2.0 %collective-permute-start.3 = (bf16[2,192,1024]{2,1,0:T(8,128)(2,1)}, bf16[2,192,1024]{2,1,0:T(8,128)(2,1)S(1)}, u32[]{:S(2)}, u32[]{:S(2)}) collective-permute-start(bf16[2,192,1024]{2,1,0:T(8,128)(2,1)} %get-tuple-element.18), channel_id=1, source_target_pairs={{0,128},{1,129},{2,130},{3,131},{4,132},{5,133},{6,134},{7,135},{8... | collective-permute-start | bytes 2359304 | tf_op jit(solution)/shard_map/ppermute | solution.py:53
  14.4 4.7 %collective-permute-done.4.after.p0 = bf16[192,1024]{1,0:T(8,128)(2,1)S(1)} collective-permute-done((bf16[192,1024]{1,0:T(8,128)(2,1)}, bf16[192,1024]{1,0:T(8,128)(2,1)S(1)}, u32[]{:S(2)}, u32[]{:S(2)}) %collective-permute-start.4) | collective-permute-done | bytes 393248 | tf_op jit(solution)/shard_map/ppermute | solution.py:53
  19.1 1.0 copy-done.14
  20.1 1.6 collective-permute-start.5
  21.7 22.4 %collective-permute-done.5.x0 = bf16[192,1024]{1,0:T(8,128)(2,1)S(1)} collective-permute-done((bf16[192,1024]{1,0:T(8,128)(2,1)S(1)}, bf16[192,1024]{1,0:T(8,128)(2,1)S(1)}, u32[]{:S(2)}, u32[]{:S(2)}) %collective-permute-start.5) | collective-permute-done | bytes 393248 | tf_op jit(solution)/shard_map/ppermute | solution.py:53
  44.1 3.3 %collective-permute-done.3.over = bf16[2,192,1024]{2,1,0:T(8,128)(2,1)S(1)} collective-permute-done((bf16[2,192,1024]{2,1,0:T(8,128)(2,1)}, bf16[2,192,1024]{2,1,0:T(8,128)(2,1)S(1)}, u32[]{:S(2)}, u32[]{:S(2)}) %collective-permute-start.3) | collective-permute-done | bytes 786464 | tf_op jit(solution)/shard_map/ppermute | solution.py:53
  47.4 1.3 copy-done.12
  48.7 1.0 copy-done.13
  49.7 1.5 gather.1
  51.1 1.8 %collective-permute-start.7 = (bf16[256,3072]{1,0:T(8,128)(2,1)S(1)}, bf16[256,3072]{1,0:T(8,128)(2,1)S(1)}, u32[]{:S(2)}, u32[]{:S(2)}) collective-permute-start(bf16[256,3072]{1,0:T(8,128)(2,1)S(1)} %get-tuple-element.21.here), channel_id=1, source_target_pairs={{0,192},{1,193},{2,194},{3,195},{4,196},{5,197},{6,198},{7,199},{8... | collective-permute-start | bytes 4718600 | tf_op jit(solution)/shard_map/ppermute | solution.py:53
  53.2 1.2 copy-done.10
  55.3 1.1 collective-permute-start.11
  56.4 2.1 %collective-permute-start.10 = (bf16[3,192,1024]{2,1,0:T(8,128)(2,1)S(1)}, bf16[3,192,1024]{2,1,0:T(8,128)(2,1)}, u32[]{:S(2)}, u32[]{:S(2)}) collective-permute-start(bf16[3,192,1024]{2,1,0:T(8,128)(2,1)S(1)} %get-tuple-element.23.own_rest), channel_id=1, source_target_pairs={{0,48},{1,49},{2,50},{3,51},{4,52},{5,53},{6,54},{7,55},{8,56},{9,... | collective-permute-start | bytes 3538952 | tf_op jit(solution)/shard_map/ppermute | solution.py:53
  58.5 27.3 %collective-permute-done.7.up = bf16[256,3072]{1,0:T(8,128)(2,1)S(1)} collective-permute-done((bf16[256,3072]{1,0:T(8,128)(2,1)S(1)}, bf16[256,3072]{1,0:T(8,128)(2,1)S(1)}, u32[]{:S(2)}, u32[]{:S(2)}) %collective-permute-start.7) | collective-permute-done | bytes 1572896 | tf_op jit(solution)/shard_map/ppermute | solution.py:53
  85.8 1.0 slice.81
  86.7 1.1 copy-done.6
  87.9 2.5 %collective-permute-start.9 = (bf16[128,3072]{1,0:T(8,128)(2,1)}, bf16[128,3072]{1,0:T(8,128)(2,1)S(1)}, u32[]{:S(2)}, u32[]{:S(2)}) collective-permute-start(bf16[128,3072]{1,0:T(8,128)(2,1)} %slice.81), channel_id=1, source_target_pairs={{0,192},{1,193},{2,194},{3,195},{4,196},{5,197},{6,198},{7,199},{8... | collective-permute-start | bytes 2359304 | tf_op jit(solution)/shard_map/ppermute | solution.py:53
  90.4 0.9 slice.80
  91.3 1.2 copy-done.8
  92.6 13.1 %collective-permute-done.11.c1 = bf16[3,192,1024]{2,1,0:T(8,128)(2,1)} collective-permute-done((bf16[3,192,1024]{2,1,0:T(8,128)(2,1)}, bf16[3,192,1024]{2,1,0:T(8,128)(2,1)}, u32[]{:S(2)}, u32[]{:S(2)}) %collective-permute-start.11) | collective-permute-done | bytes 1179680 | tf_op jit(solution)/shard_map/ppermute | solution.py:53
  105.6 1.5 collective-permute-done.10.p1
  107.1 2.7 %arrange.3 = bf16[3072,512]{1,0:T(8,128)(2,1)S(1)} custom-call(s32[3]{0:T(128)S(1)} %copy-done.15, s32[1]{0:T(128)} %bitcast.5.half, bf16[4,192,1024]{2,1,0:T(8,128)(2,1)S(1)} %get-tuple-element.22.early, bf16[3,192,1024]{2,1,0:T(8,128)(2,1)S(1)} %get-tuple-element.23.own_rest, bf16[3,192,1024]{2,1,0:T(8,128)(2,1)} %collective-permute-done.10.p1, ...), custom_call_target="tpu_custom_call" | custom-call | bytes 6291456 | tf_op jit(solution)/shard_map/arrange/pallas_call | solution.py:222
  110.3 2.1 %join.1 = bf16[1024,3072]{1,0:T(8,128)(2,1)S(1)} custom-call(s32[3]{0:T(128)S(1)} %copy-done.15, bf16[256,3072]{1,0:T(8,128)(2,1)S(1)} %copy-done.11, bf16[256,3072]{1,0:T(8,128)(2,1)S(1)} %copy-done.9, bf16[256,3072]{1,0:T(8,128)(2,1)S(1)} %copy-done.7, bf16[128,3072]{1,0:T(8,128)(2,1)} %collective-permute-done.8.far0, ...), custom_call_target="tpu_custom_call" | custom-call | bytes 6291456 | tf_op jit(solution)/shard_map/join/pallas_call | solution.py:192
  112.5 3.4 %fusion.17 = f32[1024,512]{1,0:T(8,128)S(1)} fusion(bf16[1024,3072]{1,0:T(8,128)(2,1)S(1)} %join.1, bf16[3072,512]{1,0:T(8,128)(2,1)S(1)} %arrange.3), kind=kOutput, calls=%fused_computation.29 | convolution fusion | flops 3221225472 | bytes 11534336 | tf_op jit(solution)/shard_map/dot_general | solution.py:280
  116.3 2.4 %arrange.2 = bf16[3072,512]{1,0:T(8,128)(2,1)S(1)} custom-call(s32[3]{0:T(128)S(1)} %copy-done.15, s32[1]{0:T(128)} %bitcast.4.half, bf16[4,192,1024]{2,1,0:T(8,128)(2,1)S(1)} %copy-done.3, bf16[3,192,1024]{2,1,0:T(8,128)(2,1)S(1)} %copy-done.5, bf16[3,192,1024]{2,1,0:T(8,128)(2,1)} %collective-permute-done.10.p1, ...), custom_call_target="tpu_custom_call" | custom-call | bytes 6291456 | tf_op jit(solution)/shard_map/arrange/pallas_call | solution.py:222
  118.7 1.5 collective-permute-done.13
  122.2 1.9 %collective-permute-start.14 = (f32[64,512]{1,0:T(8,128)S(1)}, f32[64,512]{1,0:T(8,128)S(1)}, u32[]{:S(2)}, u32[]{:S(2)}) collective-permute-start(f32[64,512]{1,0:T(8,128)S(1)} %get-tuple-element.25), channel_id=1, source_target_pairs={{0,2},{1,3},{2,4},{3,5},{4,6},{5,7},{6,8},{7,9},{8,10},{9,11},{10,... | collective-permute-start | bytes 393224 | tf_op jit(solution)/shard_map/ppermute | solution.py:53
  124.2 3.1 %collective-permute-done.18 = f32[64,512]{1,0:T(8,128)S(1)} collective-permute-done((f32[64,512]{1,0:T(8,128)S(1)}, f32[64,512]{1,0:T(8,128)S(1)}, u32[]{:S(2)}, u32[]{:S(2)}) %collective-permute-start.18) | collective-permute-done | bytes 131104 | tf_op jit(solution)/shard_map/ppermute | solution.py:53
  127.3 1.9 %fusion.7 = f32[128,512]{1,0:T(8,128)S(1)} fusion(bf16[3072,512]{1,0:T(8,128)(2,1)S(1)} %arrange.2, bf16[1024,3072]{1,0:T(8,128)(2,1)} %copy-done, f32[1024,512]{1,0:T(8,128)} %copy-done.16, f32[64,512]{1,0:T(8,128)S(1)} %collective-permute-done.18), kind=kOutput, calls=%fused_computation.15 | convolution fusion | flops 402784256 | bytes 4587520 | tf_op jit(solution)/shard_map/dot_general | solution.py:286
  129.2 3.4 %collective-permute-start.19 = (f32[128,512]{1,0:T(8,128)S(1)}, f32[128,512]{1,0:T(8,128)S(1)}, u32[]{:S(2)}, u32[]{:S(2)}) collective-permute-start(f32[128,512]{1,0:T(8,128)S(1)} %fusion.7), channel_id=1, source_target_pairs={{0,14},{1,15},{2,0},{3,1},{4,2},{5,3},{6,4},{7,5},{8,6},{9,7},{10,... | collective-permute-start | bytes 786440 | tf_op jit(solution)/shard_map/ppermute | solution.py:53
  132.6 1.7 fusion.4
  134.4 3.2 %collective-permute-done.19 = f32[128,512]{1,0:T(8,128)S(1)} collective-permute-done((f32[128,512]{1,0:T(8,128)S(1)}, f32[128,512]{1,0:T(8,128)S(1)}, u32[]{:S(2)}, u32[]{:S(2)}) %collective-permute-start.19) | collective-permute-done | bytes 262176 | tf_op jit(solution)/shard_map/ppermute | solution.py:53
  138.2 3.8 %collective-permute-start.20 = (f32[128,512]{1,0:T(8,128)S(1)}, f32[128,512]{1,0:T(8,128)S(1)}, u32[]{:S(2)}, u32[]{:S(2)}) collective-permute-start(f32[128,512]{1,0:T(8,128)S(1)} %fusion.6), channel_id=1, source_target_pairs={{0,14},{1,15},{2,0},{3,1},{4,2},{5,3},{6,4},{7,5},{8,6},{9,7},{10,... | collective-permute-start | bytes 786440 | tf_op jit(solution)/shard_map/ppermute | solution.py:53
  142.0 1.6 collective-permute-done.15
  144.3 2.1 %collective-permute-done.20 = f32[128,512]{1,0:T(8,128)S(1)} collective-permute-done((f32[128,512]{1,0:T(8,128)S(1)}, f32[128,512]{1,0:T(8,128)S(1)}, u32[]{:S(2)}, u32[]{:S(2)}) %collective-permute-start.20) | collective-permute-done | bytes 262176 | tf_op jit(solution)/shard_map/ppermute | solution.py:53
  146.4 1.3 fusion.5
  147.7 3.4 %collective-permute-start.21 = (f32[128,512]{1,0:T(8,128)}, f32[128,512]{1,0:T(8,128)S(1)}, u32[]{:S(2)}, u32[]{:S(2)}) collective-permute-start(f32[128,512]{1,0:T(8,128)} %fusion.5), channel_id=1, source_target_pairs={{0,14},{1,15},{2,0},{3,1},{4,2},{5,3},{6,4},{7,5},{8,6},{9,7},{10,... | collective-permute-start | bytes 786440 | tf_op jit(solution)/shard_map/ppermute | solution.py:53
  151.8 1.3 fusion.2
  154.0 1.3 collective-permute-done.21
  155.3 5.4 %collective-permute-done.17 = f32[128,512]{1,0:T(8,128)} collective-permute-done((f32[128,512]{1,0:T(8,128)}, f32[128,512]{1,0:T(8,128)}, u32[]{:S(2)}, u32[]{:S(2)}) %collective-permute-start.17) | collective-permute-done | bytes 262176 | tf_op jit(solution)/shard_map/ppermute | solution.py:53
  160.7 1.9 %fusion.1.total = f32[128,512]{1,0:T(8,128)S(1)} fusion(f32[128,512]{1,0:T(8,128)S(1)} %collective-permute-done.21, f32[128,512]{1,0:T(8,128)} %collective-permute-done.17, bf16[3072,512]{1,0:T(8,128)(2,1)S(1)} %arrange.2, bf16[1024,3072]{1,0:T(8,128)(2,1)} %copy-done, f32[1024,512]{1,0:T(8,128)} %copy-done.16), kind=kOutput, calls=%fused_computation.9 | convolution fusion | flops 402849792 | bytes 4980736 | tf_op jit(solution)/shard_map/dot_general | solution.py:286
  162.8 1.9 %collective-permute-start.22 = (bf16[512,128]{1,0:T(8,128)(2,1)S(1)}, bf16[512,128]{1,0:T(8,128)(2,1)S(1)}, u32[]{:S(2)}, u32[]{:S(2)}) collective-permute-start(bf16[512,128]{1,0:T(8,128)(2,1)S(1)} %finish.1), channel_id=1, source_target_pairs={{0,0},{1,48},{2,1},{3,49},{4,4},{5,52},{6,5},{7,53},{8,8},{9,56},{... | collective-permute-start | bytes 393224 | tf_op jit(solution)/shard_map/ppermute | solution.py:53
  164.7 7.6 %collective-permute-done.22 = bf16[512,128]{1,0:T(8,128)(2,1)S(1)} collective-permute-done((bf16[512,128]{1,0:T(8,128)(2,1)S(1)}, bf16[512,128]{1,0:T(8,128)(2,1)S(1)}, u32[]{:S(2)}, u32[]{:S(2)}) %collective-permute-start.22) | collective-permute-done | bytes 131104 | tf_op jit(solution)/shard_map/ppermute | solution.py:53
  (66 shorter events, 8.6 us)
Async XLA Ops:
  5.5 41.9 %collective-permute-start = (bf16[192,3072]{1,0:T(8,128)(2,1)}, bf16[192,3072]{1,0:T(8,128)(2,1)S(1)}, u32[]{:S(2)}, u32[]{:S(2)}) collective-permute-start(bf16[192,3072]{1,0:T(8,128)(2,1)} %get-tuple-element.15.near), channel_id=1, source_target_pairs={{0,16},{1,17},{2,18},{3,19},{4,20},{5,21},{6,22},{7,23},{8,24},{9,... | collective-permute-start | bytes 3538952 | tf_op jit(solution)/shard_map/ppermute | solution.py:53
  7.1 12.0 %collective-permute-start.4 = (bf16[192,1024]{1,0:T(8,128)(2,1)}, bf16[192,1024]{1,0:T(8,128)(2,1)S(1)}, u32[]{:S(2)}, u32[]{:S(2)}) collective-permute-start(bf16[192,1024]{1,0:T(8,128)(2,1)} %get-tuple-element.19.own), channel_id=1, source_target_pairs={{0,48},{1,49},{2,50},{3,51},{4,52},{5,53},{6,54},{7,55},{8,56},{9,... | collective-permute-start | bytes 1179656 | tf_op jit(solution)/shard_map/ppermute | solution.py:53
  9.2 35.0 %collective-permute-start.1 = (bf16[2,192,1024]{2,1,0:T(8,128)(2,1)}, bf16[2,192,1024]{2,1,0:T(8,128)(2,1)S(1)}, u32[]{:S(2)}, u32[]{:S(2)}) collective-permute-start(bf16[2,192,1024]{2,1,0:T(8,128)(2,1)} %get-tuple-element.16), channel_id=1, source_target_pairs={{0,64},{1,65},{2,66},{3,67},{4,68},{5,69},{6,70},{7,71},{8,72},{9,... | collective-permute-start | bytes 2359304 | tf_op jit(solution)/shard_map/ppermute | solution.py:53
  10.7 33.4 %collective-permute-start.2 = (bf16[2,192,1024]{2,1,0:T(8,128)(2,1)}, bf16[2,192,1024]{2,1,0:T(8,128)(2,1)S(1)}, u32[]{:S(2)}, u32[]{:S(2)}) collective-permute-start(bf16[2,192,1024]{2,1,0:T(8,128)(2,1)} %get-tuple-element.17), channel_id=1, source_target_pairs={{0,192},{1,193},{2,194},{3,195},{4,196},{5,197},{6,198},{7,199},{8... | collective-permute-start | bytes 2359304 | tf_op jit(solution)/shard_map/ppermute | solution.py:53
  12.4 35.0 %collective-permute-start.3 = (bf16[2,192,1024]{2,1,0:T(8,128)(2,1)}, bf16[2,192,1024]{2,1,0:T(8,128)(2,1)S(1)}, u32[]{:S(2)}, u32[]{:S(2)}) collective-permute-start(bf16[2,192,1024]{2,1,0:T(8,128)(2,1)} %get-tuple-element.18), channel_id=1, source_target_pairs={{0,128},{1,129},{2,130},{3,131},{4,132},{5,133},{6,134},{7,135},{8... | collective-permute-start | bytes 2359304 | tf_op jit(solution)/shard_map/ppermute | solution.py:53
  19.1 1.0 copy-start.14
  20.1 87.1 %copy-start.15 = (s32[3]{0:T(128)S(1)}, s32[3]{0:T(128)}, u32[]{:S(2)}) copy-start(s32[3]{0:T(128)} %pad_add_fusion.place) | copy-start | bytes 40
  20.1 24.0 %collective-permute-start.5 = (bf16[192,1024]{1,0:T(8,128)(2,1)S(1)}, bf16[192,1024]{1,0:T(8,128)(2,1)S(1)}, u32[]{:S(2)}, u32[]{:S(2)}) collective-permute-start(bf16[192,1024]{1,0:T(8,128)(2,1)S(1)} %follow.1), channel_id=1, source_target_pairs={{0,32},{1,33},{2,34},{3,35},{4,36},{5,37},{6,38},{7,39},{8,40},{9,... | collective-permute-start | bytes 1179656 | tf_op jit(solution)/shard_map/ppermute | solution.py:53
  47.4 1.3 copy-start.12
  48.7 1.0 copy-start.13
  51.1 58.7 %copy-start.2 = (bf16[4,192,1024]{2,1,0:T(8,128)(2,1)}, bf16[4,192,1024]{2,1,0:T(8,128)(2,1)S(1)}, u32[]{:S(2)}) copy-start(bf16[4,192,1024]{2,1,0:T(8,128)(2,1)S(1)} %get-tuple-element.22.early) | copy-start | bytes 4718596
  51.1 58.7 %copy-start.4 = (bf16[3,192,1024]{2,1,0:T(8,128)(2,1)}, bf16[3,192,1024]{2,1,0:T(8,128)(2,1)S(1)}, u32[]{:S(2)}) copy-start(bf16[3,192,1024]{2,1,0:T(8,128)(2,1)S(1)} %get-tuple-element.23.own_rest) | copy-start | bytes 3538948
  51.1 34.6 %collective-permute-start.7 = (bf16[256,3072]{1,0:T(8,128)(2,1)S(1)}, bf16[256,3072]{1,0:T(8,128)(2,1)S(1)}, u32[]{:S(2)}, u32[]{:S(2)}) collective-permute-start(bf16[256,3072]{1,0:T(8,128)(2,1)S(1)} %get-tuple-element.21.here), channel_id=1, source_target_pairs={{0,192},{1,193},{2,194},{3,195},{4,196},{5,197},{6,198},{7,199},{8... | collective-permute-start | bytes 4718600 | tf_op jit(solution)/shard_map/ppermute | solution.py:53
  52.9 37.5 %collective-permute-start.6 = (bf16[256,3072]{1,0:T(8,128)(2,1)S(1)}, bf16[256,3072]{1,0:T(8,128)(2,1)S(1)}, u32[]{:S(2)}, u32[]{:S(2)}) collective-permute-start(bf16[256,3072]{1,0:T(8,128)(2,1)S(1)} %get-tuple-element.21.here), channel_id=1, source_target_pairs={{0,64},{1,65},{2,66},{3,67},{4,68},{5,69},{6,70},{7,71},{8,72},{9,... | collective-permute-start | bytes 4718600 | tf_op jit(solution)/shard_map/ppermute | solution.py:53
  53.2 1.2 copy-start.10
  54.4 38.2 %collective-permute-start.12 = (bf16[3,192,1024]{2,1,0:T(8,128)(2,1)}, bf16[3,192,1024]{2,1,0:T(8,128)(2,1)}, u32[]{:S(2)}, u32[]{:S(2)}) collective-permute-start(bf16[3,192,1024]{2,1,0:T(8,128)(2,1)} %get-tuple-element.24), channel_id=1, source_target_pairs={{0,32},{1,33},{2,34},{3,35},{4,36},{5,37},{6,38},{7,39},{8,40},{9,... | collective-permute-start | bytes 3538952 | tf_op jit(solution)/shard_map/ppermute | solution.py:53
  55.3 50.4 %collective-permute-start.11 = (bf16[3,192,1024]{2,1,0:T(8,128)(2,1)}, bf16[3,192,1024]{2,1,0:T(8,128)(2,1)}, u32[]{:S(2)}, u32[]{:S(2)}) collective-permute-start(bf16[3,192,1024]{2,1,0:T(8,128)(2,1)} %get-tuple-element.24), channel_id=1, source_target_pairs={{0,16},{1,17},{2,18},{3,19},{4,20},{5,21},{6,22},{7,23},{8,24},{9,... | collective-permute-start | bytes 3538952 | tf_op jit(solution)/shard_map/ppermute | solution.py:53
  56.4 50.8 %collective-permute-start.10 = (bf16[3,192,1024]{2,1,0:T(8,128)(2,1)S(1)}, bf16[3,192,1024]{2,1,0:T(8,128)(2,1)}, u32[]{:S(2)}, u32[]{:S(2)}) collective-permute-start(bf16[3,192,1024]{2,1,0:T(8,128)(2,1)S(1)} %get-tuple-element.23.own_rest), channel_id=1, source_target_pairs={{0,48},{1,49},{2,50},{3,51},{4,52},{5,53},{6,54},{7,55},{8,56},{9,... | collective-permute-start | bytes 3538952 | tf_op jit(solution)/shard_map/ppermute | solution.py:53
  86.7 1.1 copy-start.6
  87.9 22.0 %collective-permute-start.9 = (bf16[128,3072]{1,0:T(8,128)(2,1)}, bf16[128,3072]{1,0:T(8,128)(2,1)S(1)}, u32[]{:S(2)}, u32[]{:S(2)}) collective-permute-start(bf16[128,3072]{1,0:T(8,128)(2,1)} %slice.81), channel_id=1, source_target_pairs={{0,192},{1,193},{2,194},{3,195},{4,196},{5,197},{6,198},{7,199},{8... | collective-permute-start | bytes 2359304 | tf_op jit(solution)/shard_map/ppermute | solution.py:53
  91.3 1.2 copy-start.8
  92.6 17.7 %collective-permute-start.8 = (bf16[128,3072]{1,0:T(8,128)(2,1)}, bf16[128,3072]{1,0:T(8,128)(2,1)}, u32[]{:S(2)}, u32[]{:S(2)}) collective-permute-start(bf16[128,3072]{1,0:T(8,128)(2,1)} %slice.80), channel_id=1, source_target_pairs={{0,64},{1,65},{2,66},{3,67},{4,68},{5,69},{6,70},{7,71},{8,72},{9,... | collective-permute-start | bytes 2359304 | tf_op jit(solution)/shard_map/ppermute | solution.py:53
  107.1 3.2 %copy-start.7 = (bf16[256,3072]{1,0:T(8,128)(2,1)S(1)}, bf16[256,3072]{1,0:T(8,128)(2,1)}, u32[]{:S(2)}) copy-start(bf16[256,3072]{1,0:T(8,128)(2,1)} %copy-done.6) | copy-start | bytes 4718596
  107.1 3.2 %copy-start.9 = (bf16[256,3072]{1,0:T(8,128)(2,1)S(1)}, bf16[256,3072]{1,0:T(8,128)(2,1)}, u32[]{:S(2)}) copy-start(bf16[256,3072]{1,0:T(8,128)(2,1)} %copy-done.8) | copy-start | bytes 4718596
  107.1 3.2 %copy-start.11 = (bf16[256,3072]{1,0:T(8,128)(2,1)S(1)}, bf16[256,3072]{1,0:T(8,128)(2,1)}, u32[]{:S(2)}) copy-start(bf16[256,3072]{1,0:T(8,128)(2,1)} %copy-done.10) | copy-start | bytes 4718596
  112.4 7.7 %copy-start = (bf16[1024,3072]{1,0:T(8,128)(2,1)}, bf16[1024,3072]{1,0:T(8,128)(2,1)S(1)}, u32[]{:S(2)}) copy-start(bf16[1024,3072]{1,0:T(8,128)(2,1)S(1)} %join.1) | copy-start | bytes 18874372
  112.4 3.5 %copy-start.3 = (bf16[4,192,1024]{2,1,0:T(8,128)(2,1)S(1)}, bf16[4,192,1024]{2,1,0:T(8,128)(2,1)}, u32[]{:S(2)}) copy-start(bf16[4,192,1024]{2,1,0:T(8,128)(2,1)} %copy-done.2) | copy-start | bytes 4718596
  112.5 3.8 %copy-start.5 = (bf16[3,192,1024]{2,1,0:T(8,128)(2,1)S(1)}, bf16[3,192,1024]{2,1,0:T(8,128)(2,1)}, u32[]{:S(2)}) copy-start(bf16[3,192,1024]{2,1,0:T(8,128)(2,1)} %copy-done.4) | copy-start | bytes 3538948
  115.9 4.2 %collective-permute-start.13 = (f32[1024,512]{1,0:T(8,128)S(1)}, f32[1024,512]{1,0:T(8,128)S(1)}, u32[]{:S(2)}, u32[]{:S(2)}) collective-permute-start(f32[1024,512]{1,0:T(8,128)S(1)} %fusion.17), channel_id=1, source_target_pairs={{0,1},{1,0},{2,3},{3,2},{4,5},{5,4},{6,7},{7,6},{8,9},{9,8},{10,11... | collective-permute-start | bytes 6291464 | tf_op jit(solution)/shard_map/ppermute | solution.py:53
  118.6 3.0 %copy-start.19 = (f32[4]{0:T(128)S(1)}, f32[4]{0:T(128)}, u32[]{:S(2)}) copy-start(f32[4]{0:T(128)} %param.12) | copy-start | bytes 52
  120.1 1.3 copy-start.16
  121.5 5.8 %collective-permute-start.18 = (f32[64,512]{1,0:T(8,128)S(1)}, f32[64,512]{1,0:T(8,128)S(1)}, u32[]{:S(2)}, u32[]{:S(2)}) collective-permute-start(f32[64,512]{1,0:T(8,128)S(1)} %get-tuple-element.26), channel_id=1, source_target_pairs={{0,14},{1,15},{2,0},{3,1},{4,2},{5,3},{6,4},{7,5},{8,6},{9,7},{10,... | collective-permute-start | bytes 393224 | tf_op jit(solution)/shard_map/ppermute | solution.py:53
  121.7 10.9 %copy-start.17 = (f32[1024,512]{1,0:T(8,128)S(1)}, f32[1024,512]{1,0:T(8,128)}, u32[]{:S(2)}) copy-start(f32[1024,512]{1,0:T(8,128)} %copy-done.16) | copy-start | bytes 6291460
  122.2 10.3 %collective-permute-start.14 = (f32[64,512]{1,0:T(8,128)S(1)}, f32[64,512]{1,0:T(8,128)S(1)}, u32[]{:S(2)}, u32[]{:S(2)}) collective-permute-start(f32[64,512]{1,0:T(8,128)S(1)} %get-tuple-element.25), channel_id=1, source_target_pairs={{0,2},{1,3},{2,4},{3,5},{4,6},{5,7},{6,8},{7,9},{8,10},{9,11},{10,... | collective-permute-start | bytes 393224 | tf_op jit(solution)/shard_map/ppermute | solution.py:53
  127.3 10.4 %copy-start.1 = (bf16[1024,3072]{1,0:T(8,128)(2,1)S(1)}, bf16[1024,3072]{1,0:T(8,128)(2,1)}, u32[]{:S(2)}) copy-start(bf16[1024,3072]{1,0:T(8,128)(2,1)} %copy-done) | copy-start | bytes 18874372
  129.2 8.4 %collective-permute-start.19 = (f32[128,512]{1,0:T(8,128)S(1)}, f32[128,512]{1,0:T(8,128)S(1)}, u32[]{:S(2)}, u32[]{:S(2)}) collective-permute-start(f32[128,512]{1,0:T(8,128)S(1)} %fusion.7), channel_id=1, source_target_pairs={{0,14},{1,15},{2,0},{3,1},{4,2},{5,3},{6,4},{7,5},{8,6},{9,7},{10,... | collective-permute-start | bytes 786440 | tf_op jit(solution)/shard_map/ppermute | solution.py:53
  134.3 9.3 %collective-permute-start.15 = (f32[128,512]{1,0:T(8,128)S(1)}, f32[128,512]{1,0:T(8,128)S(1)}, u32[]{:S(2)}, u32[]{:S(2)}) collective-permute-start(f32[128,512]{1,0:T(8,128)S(1)} %fusion.4), channel_id=1, source_target_pairs={{0,2},{1,3},{2,4},{3,5},{4,6},{5,7},{6,8},{7,9},{8,10},{9,11},{10,... | collective-permute-start | bytes 786440 | tf_op jit(solution)/shard_map/ppermute | solution.py:53
  138.2 8.1 %collective-permute-start.20 = (f32[128,512]{1,0:T(8,128)S(1)}, f32[128,512]{1,0:T(8,128)S(1)}, u32[]{:S(2)}, u32[]{:S(2)}) collective-permute-start(f32[128,512]{1,0:T(8,128)S(1)} %fusion.6), channel_id=1, source_target_pairs={{0,14},{1,15},{2,0},{3,1},{4,2},{5,3},{6,4},{7,5},{8,6},{9,7},{10,... | collective-permute-start | bytes 786440 | tf_op jit(solution)/shard_map/ppermute | solution.py:53
  144.2 7.6 %collective-permute-start.16 = (f32[128,512]{1,0:T(8,128)S(1)}, f32[128,512]{1,0:T(8,128)S(1)}, u32[]{:S(2)}, u32[]{:S(2)}) collective-permute-start(f32[128,512]{1,0:T(8,128)S(1)} %fusion.3), channel_id=1, source_target_pairs={{0,2},{1,3},{2,4},{3,5},{4,6},{5,7},{6,8},{7,9},{8,10},{9,11},{10,... | collective-permute-start | bytes 786440 | tf_op jit(solution)/shard_map/ppermute | solution.py:53
  147.7 5.4 %copy-start.18 = (f32[4,128]{1,0:T(4,128)S(1)}, f32[4,128]{1,0:T(4,128)}, u32[]{:S(2)}) copy-start(f32[4,128]{1,0:T(4,128)} %param.13) | copy-start | bytes 6148
  147.7 6.2 %copy-start.20 = (f32[16]{0:T(128)S(1)}, f32[16]{0:T(128)}, u32[]{:S(2)}) copy-start(f32[16]{0:T(128)} %param.11) | copy-start | bytes 196
  147.7 7.6 %collective-permute-start.21 = (f32[128,512]{1,0:T(8,128)}, f32[128,512]{1,0:T(8,128)S(1)}, u32[]{:S(2)}, u32[]{:S(2)}) collective-permute-start(f32[128,512]{1,0:T(8,128)} %fusion.5), channel_id=1, source_target_pairs={{0,14},{1,15},{2,0},{3,1},{4,2},{5,3},{6,4},{7,5},{8,6},{9,7},{10,... | collective-permute-start | bytes 786440 | tf_op jit(solution)/shard_map/ppermute | solution.py:53
  153.1 7.7 %collective-permute-start.17 = (f32[128,512]{1,0:T(8,128)}, f32[128,512]{1,0:T(8,128)}, u32[]{:S(2)}, u32[]{:S(2)}) collective-permute-start(f32[128,512]{1,0:T(8,128)} %fusion.2), channel_id=1, source_target_pairs={{0,2},{1,3},{2,4},{3,5},{4,6},{5,7},{6,8},{7,9},{8,10},{9,11},{10,... | collective-permute-start | bytes 786440 | tf_op jit(solution)/shard_map/ppermute | solution.py:53
  162.8 9.5 %collective-permute-start.22 = (bf16[512,128]{1,0:T(8,128)(2,1)S(1)}, bf16[512,128]{1,0:T(8,128)(2,1)S(1)}, u32[]{:S(2)}, u32[]{:S(2)}) collective-permute-start(bf16[512,128]{1,0:T(8,128)(2,1)S(1)} %finish.1), channel_id=1, source_target_pairs={{0,0},{1,48},{2,1},{3,49},{4,4},{5,52},{6,5},{7,53},{8,8},{9,56},{... | collective-permute-start | bytes 393224 | tf_op jit(solution)/shard_map/ppermute | solution.py:53

commit v5 on v4

--- a/solution.py
+++ b/solution.py
@@ -1,3 +1,5 @@
+import functools
+
 import jax
 import jax.numpy as jnp
 from jax import lax
@@ -235,19 +237,45 @@
     )(place, half, *amps)
 
 
-def finish_kernel(total, row, col, out):
-    out[...] = (total[...] / -(row[...] + col[...])).T.astype(jnp.bfloat16)
-
-
-def finish(total, row, col):
+def merge_kernel(mine, got, out, *, first):
+    if got.shape[0] == mine.shape[0]:
+        out[...] = mine[...] + got[...]
+    else:
+        rest = 64 - first
+        out[pl.ds(first, 64), :] = mine[pl.ds(first, 64), :] + got[...]
+        out[pl.ds(rest, 64), :] = mine[pl.ds(rest, 64), :]
+
+
+def merge(others, spot, got, first):
+    vmem = pl.BlockSpec(memory_space=VMEM)
+    return pl.pallas_call(
+        functools.partial(merge_kernel, first=first),
+        out_shape=jax.ShapeDtypeStruct((128, RB), jnp.float32),
+        grid=(1,),
+        in_specs=[pl.BlockSpec((128, RB), lambda i: (spot, 0)), vmem],
+        out_specs=vmem,
+        compiler_params=pltpu.CompilerParams(vmem_limit_bytes=4 << 20),
+        cost_estimate=pl.CostEstimate(flops=0, bytes_accessed=1 << 20, transcendentals=0),
+        name="merge",
+    )(others, got)
+
+
+def finish_kernel(mine, ahead, behind, row, col, out):
+    total = mine[...] + ahead[...] + behind[...]
+    out[...] = (total / -(row[...] + col[...])).T.astype(jnp.bfloat16)
+
+
+def finish(*parts):
+    vmem = pl.BlockSpec(memory_space=VMEM)
     return pl.pallas_call(
         finish_kernel,
         out_shape=jax.ShapeDtypeStruct((RB, 128), jnp.bfloat16),
-        in_specs=[pl.BlockSpec(memory_space=VMEM)] * 3,
-        out_specs=pl.BlockSpec(memory_space=VMEM),
-        compiler_params=pltpu.CompilerParams(vmem_limit_bytes=16 << 20),
+        grid=(1,),
+        in_specs=[pl.BlockSpec((128, RB), lambda i: (6, 0))] + [vmem] * 4,
+        out_specs=vmem,
+        compiler_params=pltpu.CompilerParams(vmem_limit_bytes=8 << 20),
         name="finish",
-    )(total, row, col)
+    )(*parts)
 
 
 def local(amplitudes, integrals, amp_mask, int_mask, occ_row, occ_col, vir_energy):
@@ -281,20 +309,14 @@
     taken = send(given, SWAP)
     keep = arrange(place, keep_half[None], amps)
 
-    def partial(spot):
-        rows = slice(spot * 128, spot * 128 + 128)
-        return jnp.dot(slabs[rows], keep, preferred_element_type=jnp.float32) + taken[rows]
-
-    farthest = partial(0)
+    farthest = jnp.dot(slabs[:128], keep, preferred_element_type=jnp.float32) + taken[:128]
+    others = jnp.dot(slabs[128:], keep, preferred_element_type=jnp.float32) + taken[128:]
     ahead, behind = farthest[:64], farthest[64:]
     for step in range(3):
         ahead, behind = send(ahead, AHEAD), send(behind, BEHIND)
-        if step == 0:
-            ahead = jnp.pad(ahead, ((0, 64), (0, 0)))
-            behind = jnp.pad(behind, ((64, 0), (0, 0)))
-        ahead = partial(1 + 2 * step) + ahead
-        behind = partial(2 + 2 * step) + behind
-    cycle_sum = partial(7) + send(ahead, AHEAD) + send(behind, BEHIND)
+        ahead = merge(others, 2 * step, ahead, 0)
+        behind = merge(others, 1 + 2 * step, behind, 64)
+    ahead, behind = send(ahead, AHEAD), send(behind, BEHIND)
 
     row_x = jnp.where(core == 0, x, 3 - x)
     row_occ = lax.dynamic_slice(occ_row, (4 * row_x,), (4,))
@@ -303,7 +325,7 @@
     col_y, col_x = slab_of(x, z)
     col_occ = lax.dynamic_slice(occ_col, (col_x,), (1,))
     col_energy = (lax.dynamic_slice(vir_energy, (col_y, 0), (1, 128)) - col_occ).reshape(128, 1)
-    return send(finish(cycle_sum, row_energy, col_energy), HOME)
+    return send(finish(others, ahead, behind, row_energy, col_energy), HOME)
 
 
 def solution(mesh):

time: 173 us -> 165 us (0.954)
  the two profiles are of different devices: /device:TPU:32 before, /device:TPU:96 now
where the time goes in v5:
time: 165 us
  waiting for transfers between devices  95 us (58%)
  starting transfers between devices  38.4 us (23%)
  Pallas kernels  13.9 us (8%)
  local copies, waits for them, and re-layouts  9.15 us (6%)
  matrix products  6.99 us (4%)
    ppermute x23, waiting for transfers between devices, send(): return lax.ppermute(value, AXES, where)  95 us
    ppermute x23, starting transfers between devices, send(): return lax.ppermute(value, AXES, where)  38.4 us
    unnamed x27, local copies, waits for them, and re-layouts  6.46 us
    pallas_call x2, Pallas kernels, arrange(): pl.pallas_call(arrange_kernel, out_shape=jax.ShapeDtypeStruct((KT, RB), j...  5.1 us
    pallas_call x1, Pallas kernels, prepare(): pl.pallas_call(prepare_kernel, out_shape=(piece, piece, near, two, two, t...  4.88 us
    dot_general x1, matrix products, local(): given = jnp.dot(slabs, give, preferred_element_type=jnp.float32)  3.4 us
  transfers between devices with their start and end apart: 23, of which 12 were waited for; matrix products, arithmetic and copies ran while one was open for 4% of the time, Pallas kernels for 3%

profile of v5, /device:TPU:96, one launch (start us, length us, event | category | flops | bytes accessed | tf_op | source)
XLA Modules:
  0.0 165.1 jit_solution(11443551775570190448)
XLA Ops:
  0.0 0.6 pad_add_fusion.place
  0.6 4.9 %prepare.1 = (bf16[192,1024]{1,0:T(8,128)(2,1)}, bf16[192,1024]{1,0:T(8,128)(2,1)}, bf16[192,3072]{1,0:T(8,128)(2,1)}, bf16[2,192,1024]{2,1,0:T(8,128)(2,1)}, bf...) custom-call(s32[3]{0:T(128)} %pad_add_fusion.place, s32[4,8]{1,0:T(4,128)} %amp_mask.1, s32[4,8]{1,0:T(4,128)} %bitcast.17, ...), custom_call_target="tpu_custom_call" | custom-call | bytes 8388608 | tf_op jit(solution)/shard_map/prepare/pallas_call | solution.py:101
  5.5 1.6 collective-permute-start
  7.1 1.6 collective-permute-start.1
  8.6 1.7 %collective-permute-start.2 = (bf16[2,192,1024]{2,1,0:T(8,128)(2,1)}, bf16[2,192,1024]{2,1,0:T(8,128)(2,1)S(1)}, u32[]{:S(2)}, u32[]{:S(2)}) collective-permute-start(bf16[2,192,1024]{2,1,0:T(8,128)(2,1)} %get-tuple-element.17), channel_id=1, source_target_pairs={{0,192},{1,193},{2,194},{3,195},{4,196},{5,197},{6,198},{7,199},{8... | collective-permute-start | bytes 2359304 | tf_op jit(solution)/shard_map/ppermute | solution.py:55
  10.3 2.1 %collective-permute-start.4 = (bf16[192,1024]{1,0:T(8,128)(2,1)}, bf16[192,1024]{1,0:T(8,128)(2,1)S(1)}, u32[]{:S(2)}, u32[]{:S(2)}) collective-permute-start(bf16[192,1024]{1,0:T(8,128)(2,1)} %get-tuple-element.19.own), channel_id=1, source_target_pairs={{0,48},{1,49},{2,50},{3,51},{4,52},{5,53},{6,54},{7,55},{8,56},{9,... | collective-permute-start | bytes 1179656 | tf_op jit(solution)/shard_map/ppermute | solution.py:55
  12.4 2.0 %collective-permute-start.3 = (bf16[2,192,1024]{2,1,0:T(8,128)(2,1)}, bf16[2,192,1024]{2,1,0:T(8,128)(2,1)S(1)}, u32[]{:S(2)}, u32[]{:S(2)}) collective-permute-start(bf16[2,192,1024]{2,1,0:T(8,128)(2,1)} %get-tuple-element.18), channel_id=1, source_target_pairs={{0,128},{1,129},{2,130},{3,131},{4,132},{5,133},{6,134},{7,135},{8... | collective-permute-start | bytes 2359304 | tf_op jit(solution)/shard_map/ppermute | solution.py:55
  14.4 7.4 %collective-permute-done.4.after.p0 = bf16[192,1024]{1,0:T(8,128)(2,1)S(1)} collective-permute-done((bf16[192,1024]{1,0:T(8,128)(2,1)}, bf16[192,1024]{1,0:T(8,128)(2,1)S(1)}, u32[]{:S(2)}, u32[]{:S(2)}) %collective-permute-start.4) | collective-permute-done | bytes 393248 | tf_op jit(solution)/shard_map/ppermute | solution.py:55
  21.8 1.0 copy-done.8
  22.8 1.6 collective-permute-start.5
  24.4 3.4 %collective-permute-done.1.down = bf16[2,192,1024]{2,1,0:T(8,128)(2,1)S(1)} collective-permute-done((bf16[2,192,1024]{2,1,0:T(8,128)(2,1)}, bf16[2,192,1024]{2,1,0:T(8,128)(2,1)S(1)}, u32[]{:S(2)}, u32[]{:S(2)}) %collective-permute-start.1) | collective-permute-done | bytes 786464 | tf_op jit(solution)/shard_map/ppermute | solution.py:55
  27.8 1.5 collective-permute-done.2.up
  29.3 16.2 %collective-permute-done.3.over = bf16[2,192,1024]{2,1,0:T(8,128)(2,1)S(1)} collective-permute-done((bf16[2,192,1024]{2,1,0:T(8,128)(2,1)}, bf16[2,192,1024]{2,1,0:T(8,128)(2,1)S(1)}, u32[]{:S(2)}, u32[]{:S(2)}) %collective-permute-start.3) | collective-permute-done | bytes 786464 | tf_op jit(solution)/shard_map/ppermute | solution.py:55
  45.6 1.3 copy-done.6
  46.9 1.0 copy-done.7
  47.9 1.4 gather.1
  49.3 1.1 collective-permute-start.6
  50.4 2.1 %collective-permute-start.7 = (bf16[256,3072]{1,0:T(8,128)(2,1)S(1)}, bf16[256,3072]{1,0:T(8,128)(2,1)S(1)}, u32[]{:S(2)}, u32[]{:S(2)}) collective-permute-start(bf16[256,3072]{1,0:T(8,128)(2,1)S(1)} %get-tuple-element.21.here), channel_id=1, source_target_pairs={{0,192},{1,193},{2,194},{3,195},{4,196},{5,197},{6,198},{7,199},{8... | collective-permute-start | bytes 4718600 | tf_op jit(solution)/shard_map/ppermute | solution.py:55
  52.5 2.1 %collective-permute-start.10 = (bf16[3,192,1024]{2,1,0:T(8,128)(2,1)S(1)}, bf16[3,192,1024]{2,1,0:T(8,128)(2,1)}, u32[]{:S(2)}, u32[]{:S(2)}) collective-permute-start(bf16[3,192,1024]{2,1,0:T(8,128)(2,1)S(1)} %get-tuple-element.23.own_rest), channel_id=1, source_target_pairs={{0,48},{1,49},{2,50},{3,51},{4,52},{5,53},{6,54},{7,55},{8,56},{9,... | collective-permute-start | bytes 3538952 | tf_op jit(solution)/shard_map/ppermute | solution.py:55
  54.6 0.6 collective-permute-start.11
  55.2 2.0 %collective-permute-start.12 = (bf16[3,192,1024]{2,1,0:T(8,128)(2,1)}, bf16[3,192,1024]{2,1,0:T(8,128)(2,1)}, u32[]{:S(2)}, u32[]{:S(2)}) collective-permute-start(bf16[3,192,1024]{2,1,0:T(8,128)(2,1)} %get-tuple-element.24), channel_id=1, source_target_pairs={{0,32},{1,33},{2,34},{3,35},{4,36},{5,37},{6,38},{7,39},{8,40},{9,... | collective-permute-start | bytes 3538952 | tf_op jit(solution)/shard_map/ppermute | solution.py:55
  57.2 28.2 %collective-permute-done.6.down = bf16[256,3072]{1,0:T(8,128)(2,1)S(1)} collective-permute-done((bf16[256,3072]{1,0:T(8,128)(2,1)S(1)}, bf16[256,3072]{1,0:T(8,128)(2,1)S(1)}, u32[]{:S(2)}, u32[]{:S(2)}) %collective-permute-start.6) | collective-permute-done | bytes 1572896 | tf_op jit(solution)/shard_map/ppermute | solution.py:55
  85.4 1.0 slice.32
  86.4 1.1 copy-done
  87.5 0.9 slice.33
  88.5 1.1 copy-done.2
  89.6 3.2 %collective-permute-start.9 = (bf16[128,3072]{1,0:T(8,128)(2,1)}, bf16[128,3072]{1,0:T(8,128)(2,1)}, u32[]{:S(2)}, u32[]{:S(2)}) collective-permute-start(bf16[128,3072]{1,0:T(8,128)(2,1)} %slice.33), channel_id=1, source_target_pairs={{0,192},{1,193},{2,194},{3,195},{4,196},{5,197},{6,198},{7,199},{8... | collective-permute-start | bytes 2359304 | tf_op jit(solution)/shard_map/ppermute | solution.py:55
  92.9 13.6 %collective-permute-done.12.x1 = bf16[3,192,1024]{2,1,0:T(8,128)(2,1)} collective-permute-done((bf16[3,192,1024]{2,1,0:T(8,128)(2,1)}, bf16[3,192,1024]{2,1,0:T(8,128)(2,1)}, u32[]{:S(2)}, u32[]{:S(2)}) %collective-permute-start.12) | collective-permute-done | bytes 1179680 | tf_op jit(solution)/shard_map/ppermute | solution.py:55
  106.5 2.7 %arrange.3 = bf16[3072,512]{1,0:T(8,128)(2,1)S(1)} custom-call(s32[3]{0:T(128)S(1)} %copy-done.9, s32[1]{0:T(128)} %bitcast.5.half, bf16[4,192,1024]{2,1,0:T(8,128)(2,1)S(1)} %get-tuple-element.22.early, bf16[3,192,1024]{2,1,0:T(8,128)(2,1)S(1)} %get-tuple-element.23.own_rest, bf16[3,192,1024]{2,1,0:T(8,128)(2,1)} %collective-permute-done.10.p1, ...), custom_call_target="tpu_custom_call" | custom-call | bytes 6291456 | tf_op jit(solution)/shard_map/arrange/pallas_call | solution.py:224
  109.5 2.2 %join.1 = bf16[1024,3072]{1,0:T(8,128)(2,1)S(1)} custom-call(s32[3]{0:T(128)S(1)} %copy-done.9, bf16[256,3072]{1,0:T(8,128)(2,1)S(1)} %copy-done.5, bf16[256,3072]{1,0:T(8,128)(2,1)S(1)} %copy-done.1, bf16[256,3072]{1,0:T(8,128)(2,1)S(1)} %copy-done.3, bf16[128,3072]{1,0:T(8,128)(2,1)S(1)} %collective-permute-done.8.far0, ...), custom_call_target="tpu_custom_call" | custom-call | bytes 6291456 | tf_op jit(solution)/shard_map/join/pallas_call | solution.py:194
  111.6 3.4 %fusion.6 = f32[1024,512]{1,0:T(8,128)S(1)} fusion(bf16[1024,3072]{1,0:T(8,128)(2,1)S(1)} %join.1, bf16[3072,512]{1,0:T(8,128)(2,1)S(1)} %arrange.3), kind=kOutput, calls=%fused_computation.10 | convolution fusion | flops 3221225472 | bytes 11534336 | tf_op jit(solution)/shard_map/dot_general | solution.py:308
  115.2 2.4 %arrange.2 = bf16[3072,512]{1,0:T(8,128)(2,1)S(1)} custom-call(s32[3]{0:T(128)S(1)} %copy-done.9, s32[1]{0:T(128)} %bitcast.4.half, bf16[4,192,1024]{2,1,0:T(8,128)(2,1)S(1)} %get-tuple-element.22.early, bf16[3,192,1024]{2,1,0:T(8,128)(2,1)S(1)} %get-tuple-element.23.own_rest, bf16[3,192,1024]{2,1,0:T(8,128)(2,1)} %collective-permute-done.10.p1, ...), custom_call_target="tpu_custom_call" | custom-call | bytes 6291456 | tf_op jit(solution)/shard_map/arrange/pallas_call | solution.py:224
  117.5 1.8 %collective-permute-done.13 = f32[1024,512]{1,0:T(8,128)S(1)} collective-permute-done((f32[1024,512]{1,0:T(8,128)S(1)}, f32[1024,512]{1,0:T(8,128)S(1)}, u32[]{:S(2)}, u32[]{:S(2)}) %collective-permute-start.13) | collective-permute-done | bytes 2097184 | tf_op jit(solution)/shard_map/ppermute | solution.py:55
  119.3 0.6 convolution_add_fusion
  119.9 3.2 %collective-permute-start.14 = (f32[64,512]{1,0:T(8,128)S(1)}, f32[64,512]{1,0:T(8,128)S(1)}, u32[]{:S(2)}, u32[]{:S(2)}) collective-permute-start(f32[64,512]{1,0:T(8,128)S(1)} %get-tuple-element.26), channel_id=1, source_target_pairs={{0,2},{1,3},{2,4},{3,5},{4,6},{5,7},{6,8},{7,9},{8,10},{9,11},{10,... | collective-permute-start | bytes 393224 | tf_op jit(solution)/shard_map/ppermute | solution.py:55
  123.1 3.0 %slice_add_fusion.mine = f32[896,512]{1,0:T(8,128)S(1)} fusion(f32[1024,512]{1,0:T(8,128)S(1)} %collective-permute-done.13, bf16[3072,512]{1,0:T(8,128)(2,1)S(1)} %arrange.2, bf16[1024,3072]{1,0:T(8,128)(2,1)S(1)} %join.1), kind=kOutput, calls=%fused_computation.2 | convolution fusion | flops 2819031040 | bytes 12320768 | tf_op jit(solution)/shard_map/dot_general | solution.py:313
  126.2 3.8 %collective-permute-start.15 = (f32[128,512]{1,0:T(8,128)S(1)}, f32[128,512]{1,0:T(8,128)S(1)}, u32[]{:S(2)}, u32[]{:S(2)}) collective-permute-start(f32[128,512]{1,0:T(8,128)S(1)} %merge.6), channel_id=1, source_target_pairs={{0,2},{1,3},{2,4},{3,5},{4,6},{5,7},{6,8},{7,9},{8,10},{9,11},{10,... | collective-permute-start | bytes 786440 | tf_op jit(solution)/shard_map/ppermute | solution.py:55
  130.1 4.9 %collective-permute-done.15.got = f32[128,512]{1,0:T(8,128)S(1)} collective-permute-done((f32[128,512]{1,0:T(8,128)S(1)}, f32[128,512]{1,0:T(8,128)S(1)}, u32[]{:S(2)}, u32[]{:S(2)}) %collective-permute-start.15) | collective-permute-done | bytes 262176 | tf_op jit(solution)/shard_map/ppermute | solution.py:55
  135.1 3.8 %collective-permute-start.16 = (f32[128,512]{1,0:T(8,128)S(1)}, f32[128,512]{1,0:T(8,128)S(1)}, u32[]{:S(2)}, u32[]{:S(2)}) collective-permute-start(f32[128,512]{1,0:T(8,128)S(1)} %merge.7), channel_id=1, source_target_pairs={{0,2},{1,3},{2,4},{3,5},{4,6},{5,7},{6,8},{7,9},{8,10},{9,11},{10,... | collective-permute-start | bytes 786440 | tf_op jit(solution)/shard_map/ppermute | solution.py:55
  139.0 0.6 dynamic_slice.15
  139.6 3.4 %collective-permute-done.16.got = f32[128,512]{1,0:T(8,128)S(1)} collective-permute-done((f32[128,512]{1,0:T(8,128)S(1)}, f32[128,512]{1,0:T(8,128)S(1)}, u32[]{:S(2)}, u32[]{:S(2)}) %collective-permute-start.16) | collective-permute-done | bytes 262176 | tf_op jit(solution)/shard_map/ppermute | solution.py:55
  143.0 3.8 %collective-permute-start.17 = (f32[128,512]{1,0:T(8,128)S(1)}, f32[128,512]{1,0:T(8,128)S(1)}, u32[]{:S(2)}, u32[]{:S(2)}) collective-permute-start(f32[128,512]{1,0:T(8,128)S(1)} %merge.8), channel_id=1, source_target_pairs={{0,2},{1,3},{2,4},{3,5},{4,6},{5,7},{6,8},{7,9},{8,10},{9,11},{10,... | collective-permute-start | bytes 786440 | tf_op jit(solution)/shard_map/ppermute | solution.py:55
  146.9 0.7 subtract_bitcast_fusion
  147.8 2.8 %collective-permute-done.17.ahead = f32[128,512]{1,0:T(8,128)S(1)} collective-permute-done((f32[128,512]{1,0:T(8,128)S(1)}, f32[128,512]{1,0:T(8,128)S(1)}, u32[]{:S(2)}, u32[]{:S(2)}) %collective-permute-start.17) | collective-permute-done | bytes 262176 | tf_op jit(solution)/shard_map/ppermute | solution.py:55
  150.7 3.8 %collective-permute-done.21.behind = f32[128,512]{1,0:T(8,128)S(1)} collective-permute-done((f32[128,512]{1,0:T(8,128)S(1)}, f32[128,512]{1,0:T(8,128)S(1)}, u32[]{:S(2)}, u32[]{:S(2)}) %collective-permute-start.21) | collective-permute-done | bytes 262176 | tf_op jit(solution)/shard_map/ppermute | solution.py:55
  154.6 1.9 %collective-permute-start.22 = (bf16[512,128]{1,0:T(8,128)(2,1)S(1)}, bf16[512,128]{1,0:T(8,128)(2,1)S(1)}, u32[]{:S(2)}, u32[]{:S(2)}) collective-permute-start(bf16[512,128]{1,0:T(8,128)(2,1)S(1)} %finish.1), channel_id=1, source_target_pairs={{0,0},{1,48},{2,1},{3,49},{4,4},{5,52},{6,5},{7,53},{8,8},{9,56},{... | collective-permute-start | bytes 393224 | tf_op jit(solution)/shard_map/ppermute | solution.py:55
  156.6 7.9 %collective-permute-done.22 = bf16[512,128]{1,0:T(8,128)(2,1)S(1)} collective-permute-done((bf16[512,128]{1,0:T(8,128)(2,1)S(1)}, bf16[512,128]{1,0:T(8,128)(2,1)S(1)}, u32[]{:S(2)}, u32[]{:S(2)}) %collective-permute-start.22) | collective-permute-done | bytes 131104 | tf_op jit(solution)/shard_map/ppermute | solution.py:55
  164.4 0.7 copy.10
  (50 shorter events, 1.3 us)
Async XLA Ops:
  5.5 40.1 %collective-permute-start = (bf16[192,3072]{1,0:T(8,128)(2,1)}, bf16[192,3072]{1,0:T(8,128)(2,1)S(1)}, u32[]{:S(2)}, u32[]{:S(2)}) collective-permute-start(bf16[192,3072]{1,0:T(8,128)(2,1)} %get-tuple-element.15.near), channel_id=1, source_target_pairs={{0,16},{1,17},{2,18},{3,19},{4,20},{5,21},{6,22},{7,23},{8,24},{9,... | collective-permute-start | bytes 3538952 | tf_op jit(solution)/shard_map/ppermute | solution.py:55
  7.1 20.8 %collective-permute-start.1 = (bf16[2,192,1024]{2,1,0:T(8,128)(2,1)}, bf16[2,192,1024]{2,1,0:T(8,128)(2,1)S(1)}, u32[]{:S(2)}, u32[]{:S(2)}) collective-permute-start(bf16[2,192,1024]{2,1,0:T(8,128)(2,1)} %get-tuple-element.16), channel_id=1, source_target_pairs={{0,64},{1,65},{2,66},{3,67},{4,68},{5,69},{6,70},{7,71},{8,72},{9,... | collective-permute-start | bytes 2359304 | tf_op jit(solution)/shard_map/ppermute | solution.py:55
  8.6 20.7 %collective-permute-start.2 = (bf16[2,192,1024]{2,1,0:T(8,128)(2,1)}, bf16[2,192,1024]{2,1,0:T(8,128)(2,1)S(1)}, u32[]{:S(2)}, u32[]{:S(2)}) collective-permute-start(bf16[2,192,1024]{2,1,0:T(8,128)(2,1)} %get-tuple-element.17), channel_id=1, source_target_pairs={{0,192},{1,193},{2,194},{3,195},{4,196},{5,197},{6,198},{7,199},{8... | collective-permute-start | bytes 2359304 | tf_op jit(solution)/shard_map/ppermute | solution.py:55
  10.3 11.5 %collective-permute-start.4 = (bf16[192,1024]{1,0:T(8,128)(2,1)}, bf16[192,1024]{1,0:T(8,128)(2,1)S(1)}, u32[]{:S(2)}, u32[]{:S(2)}) collective-permute-start(bf16[192,1024]{1,0:T(8,128)(2,1)} %get-tuple-element.19.own), channel_id=1, source_target_pairs={{0,48},{1,49},{2,50},{3,51},{4,52},{5,53},{6,54},{7,55},{8,56},{9,... | collective-permute-start | bytes 1179656 | tf_op jit(solution)/shard_map/ppermute | solution.py:55
  12.4 33.2 %collective-permute-start.3 = (bf16[2,192,1024]{2,1,0:T(8,128)(2,1)}, bf16[2,192,1024]{2,1,0:T(8,128)(2,1)S(1)}, u32[]{:S(2)}, u32[]{:S(2)}) collective-permute-start(bf16[2,192,1024]{2,1,0:T(8,128)(2,1)} %get-tuple-element.18), channel_id=1, source_target_pairs={{0,128},{1,129},{2,130},{3,131},{4,132},{5,133},{6,134},{7,135},{8... | collective-permute-start | bytes 2359304 | tf_op jit(solution)/shard_map/ppermute | solution.py:55
  21.8 1.0 copy-start.8
  22.8 83.7 %copy-start.9 = (s32[3]{0:T(128)S(1)}, s32[3]{0:T(128)}, u32[]{:S(2)}) copy-start(s32[3]{0:T(128)} %pad_add_fusion.place) | copy-start | bytes 40
  22.8 22.8 %collective-permute-start.5 = (bf16[192,1024]{1,0:T(8,128)(2,1)S(1)}, bf16[192,1024]{1,0:T(8,128)(2,1)S(1)}, u32[]{:S(2)}, u32[]{:S(2)}) collective-permute-start(bf16[192,1024]{1,0:T(8,128)(2,1)S(1)} %follow.1), channel_id=1, source_target_pairs={{0,32},{1,33},{2,34},{3,35},{4,36},{5,37},{6,38},{7,39},{8,40},{9,... | collective-permute-start | bytes 1179656 | tf_op jit(solution)/shard_map/ppermute | solution.py:55
  45.6 1.3 copy-start.6
  46.9 1.0 copy-start.7
  49.3 39.2 %copy-start.4 = (bf16[256,3072]{1,0:T(8,128)(2,1)}, bf16[256,3072]{1,0:T(8,128)(2,1)S(1)}, u32[]{:S(2)}) copy-start(bf16[256,3072]{1,0:T(8,128)(2,1)S(1)} %get-tuple-element.21.here) | copy-start | bytes 4718596
  49.3 36.2 %collective-permute-start.6 = (bf16[256,3072]{1,0:T(8,128)(2,1)S(1)}, bf16[256,3072]{1,0:T(8,128)(2,1)S(1)}, u32[]{:S(2)}, u32[]{:S(2)}) collective-permute-start(bf16[256,3072]{1,0:T(8,128)(2,1)S(1)} %get-tuple-element.21.here), channel_id=1, source_target_pairs={{0,64},{1,65},{2,66},{3,67},{4,68},{5,69},{6,70},{7,71},{8,72},{9,... | collective-permute-start | bytes 4718600 | tf_op jit(solution)/shard_map/ppermute | solution.py:55
  50.4 37.1 %collective-permute-start.7 = (bf16[256,3072]{1,0:T(8,128)(2,1)S(1)}, bf16[256,3072]{1,0:T(8,128)(2,1)S(1)}, u32[]{:S(2)}, u32[]{:S(2)}) collective-permute-start(bf16[256,3072]{1,0:T(8,128)(2,1)S(1)} %get-tuple-element.21.here), channel_id=1, source_target_pairs={{0,192},{1,193},{2,194},{3,195},{4,196},{5,197},{6,198},{7,199},{8... | collective-permute-start | bytes 4718600 | tf_op jit(solution)/shard_map/ppermute | solution.py:55
  52.5 40.3 %collective-permute-start.10 = (bf16[3,192,1024]{2,1,0:T(8,128)(2,1)S(1)}, bf16[3,192,1024]{2,1,0:T(8,128)(2,1)}, u32[]{:S(2)}, u32[]{:S(2)}) collective-permute-start(bf16[3,192,1024]{2,1,0:T(8,128)(2,1)S(1)} %get-tuple-element.23.own_rest), channel_id=1, source_target_pairs={{0,48},{1,49},{2,50},{3,51},{4,52},{5,53},{6,54},{7,55},{8,56},{9,... | collective-permute-start | bytes 3538952 | tf_op jit(solution)/shard_map/ppermute | solution.py:55
  54.6 38.3 %collective-permute-start.11 = (bf16[3,192,1024]{2,1,0:T(8,128)(2,1)}, bf16[3,192,1024]{2,1,0:T(8,128)(2,1)}, u32[]{:S(2)}, u32[]{:S(2)}) collective-permute-start(bf16[3,192,1024]{2,1,0:T(8,128)(2,1)} %get-tuple-element.24), channel_id=1, source_target_pairs={{0,16},{1,17},{2,18},{3,19},{4,20},{5,21},{6,22},{7,23},{8,24},{9,... | collective-permute-start | bytes 3538952 | tf_op jit(solution)/shard_map/ppermute | solution.py:55
  55.2 51.3 %collective-permute-start.12 = (bf16[3,192,1024]{2,1,0:T(8,128)(2,1)}, bf16[3,192,1024]{2,1,0:T(8,128)(2,1)}, u32[]{:S(2)}, u32[]{:S(2)}) collective-permute-start(bf16[3,192,1024]{2,1,0:T(8,128)(2,1)} %get-tuple-element.24), channel_id=1, source_target_pairs={{0,32},{1,33},{2,34},{3,35},{4,36},{5,37},{6,38},{7,39},{8,40},{9,... | collective-permute-start | bytes 3538952 | tf_op jit(solution)/shard_map/ppermute | solution.py:55
  86.4 1.1 copy-start
  87.5 21.7 %collective-permute-start.8 = (bf16[128,3072]{1,0:T(8,128)(2,1)}, bf16[128,3072]{1,0:T(8,128)(2,1)S(1)}, u32[]{:S(2)}, u32[]{:S(2)}) collective-permute-start(bf16[128,3072]{1,0:T(8,128)(2,1)} %slice.32), channel_id=1, source_target_pairs={{0,64},{1,65},{2,66},{3,67},{4,68},{5,69},{6,70},{7,71},{8,72},{9,... | collective-permute-start | bytes 2359304 | tf_op jit(solution)/shard_map/ppermute | solution.py:55
  88.5 1.1 copy-start.2
  89.6 19.6 %collective-permute-start.9 = (bf16[128,3072]{1,0:T(8,128)(2,1)}, bf16[128,3072]{1,0:T(8,128)(2,1)}, u32[]{:S(2)}, u32[]{:S(2)}) collective-permute-start(bf16[128,3072]{1,0:T(8,128)(2,1)} %slice.33), channel_id=1, source_target_pairs={{0,192},{1,193},{2,194},{3,195},{4,196},{5,197},{6,198},{7,199},{8... | collective-permute-start | bytes 2359304 | tf_op jit(solution)/shard_map/ppermute | solution.py:55
  106.5 2.8 %copy-start.1 = (bf16[256,3072]{1,0:T(8,128)(2,1)S(1)}, bf16[256,3072]{1,0:T(8,128)(2,1)}, u32[]{:S(2)}) copy-start(bf16[256,3072]{1,0:T(8,128)(2,1)} %copy-done) | copy-start | bytes 4718596
  106.5 2.8 %copy-start.3 = (bf16[256,3072]{1,0:T(8,128)(2,1)S(1)}, bf16[256,3072]{1,0:T(8,128)(2,1)}, u32[]{:S(2)}) copy-start(bf16[256,3072]{1,0:T(8,128)(2,1)} %copy-done.2) | copy-start | bytes 4718596
  106.5 3.0 %copy-start.5 = (bf16[256,3072]{1,0:T(8,128)(2,1)S(1)}, bf16[256,3072]{1,0:T(8,128)(2,1)}, u32[]{:S(2)}) copy-start(bf16[256,3072]{1,0:T(8,128)(2,1)} %copy-done.4) | copy-start | bytes 4718596
  115.1 4.2 %collective-permute-start.13 = (f32[1024,512]{1,0:T(8,128)S(1)}, f32[1024,512]{1,0:T(8,128)S(1)}, u32[]{:S(2)}, u32[]{:S(2)}) collective-permute-start(f32[1024,512]{1,0:T(8,128)S(1)} %fusion.6), channel_id=1, source_target_pairs={{0,1},{1,0},{2,3},{3,2},{4,5},{5,4},{6,7},{7,6},{8,9},{9,8},{10,11... | collective-permute-start | bytes 6291464 | tf_op jit(solution)/shard_map/ppermute | solution.py:55
  119.9 6.3 %collective-permute-start.14 = (f32[64,512]{1,0:T(8,128)S(1)}, f32[64,512]{1,0:T(8,128)S(1)}, u32[]{:S(2)}, u32[]{:S(2)}) collective-permute-start(f32[64,512]{1,0:T(8,128)S(1)} %get-tuple-element.26), channel_id=1, source_target_pairs={{0,2},{1,3},{2,4},{3,5},{4,6},{5,7},{6,8},{7,9},{8,10},{9,11},{10,... | collective-permute-start | bytes 393224 | tf_op jit(solution)/shard_map/ppermute | solution.py:55
  123.1 6.9 %collective-permute-start.18 = (f32[64,512]{1,0:T(8,128)S(1)}, f32[64,512]{1,0:T(8,128)S(1)}, u32[]{:S(2)}, u32[]{:S(2)}) collective-permute-start(f32[64,512]{1,0:T(8,128)S(1)} %get-tuple-element.25), channel_id=1, source_target_pairs={{0,14},{1,15},{2,0},{3,1},{4,2},{5,3},{6,4},{7,5},{8,6},{9,7},{10,... | collective-permute-start | bytes 393224 | tf_op jit(solution)/shard_map/ppermute | solution.py:55
  126.2 12.8 %copy-start.11 = (f32[4]{0:T(128)S(1)}, f32[4]{0:T(128)}, u32[]{:S(2)}) copy-start(f32[4]{0:T(128)} %param.12) | copy-start | bytes 52
  126.2 8.8 %collective-permute-start.15 = (f32[128,512]{1,0:T(8,128)S(1)}, f32[128,512]{1,0:T(8,128)S(1)}, u32[]{:S(2)}, u32[]{:S(2)}) collective-permute-start(f32[128,512]{1,0:T(8,128)S(1)} %merge.6), channel_id=1, source_target_pairs={{0,2},{1,3},{2,4},{3,5},{4,6},{5,7},{6,8},{7,9},{8,10},{9,11},{10,... | collective-permute-start | bytes 786440 | tf_op jit(solution)/shard_map/ppermute | solution.py:55
  130.0 8.8 %collective-permute-start.19 = (f32[128,512]{1,0:T(8,128)S(1)}, f32[128,512]{1,0:T(8,128)S(1)}, u32[]{:S(2)}, u32[]{:S(2)}) collective-permute-start(f32[128,512]{1,0:T(8,128)S(1)} %merge.9), channel_id=1, source_target_pairs={{0,14},{1,15},{2,0},{3,1},{4,2},{5,3},{6,4},{7,5},{8,6},{9,7},{10,... | collective-permute-start | bytes 786440 | tf_op jit(solution)/shard_map/ppermute | solution.py:55
  135.1 11.8 %copy-start.10 = (f32[4,128]{1,0:T(4,128)S(1)}, f32[4,128]{1,0:T(4,128)}, u32[]{:S(2)}) copy-start(f32[4,128]{1,0:T(4,128)} %param.13) | copy-start | bytes 6148
  135.1 12.6 %copy-start.12 = (f32[16]{0:T(128)S(1)}, f32[16]{0:T(128)}, u32[]{:S(2)}) copy-start(f32[16]{0:T(128)} %param.11) | copy-start | bytes 196
  135.1 7.9 %collective-permute-start.16 = (f32[128,512]{1,0:T(8,128)S(1)}, f32[128,512]{1,0:T(8,128)S(1)}, u32[]{:S(2)}, u32[]{:S(2)}) collective-permute-start(f32[128,512]{1,0:T(8,128)S(1)} %merge.7), channel_id=1, source_target_pairs={{0,2},{1,3},{2,4},{3,5},{4,6},{5,7},{6,8},{7,9},{8,10},{9,11},{10,... | collective-permute-start | bytes 786440 | tf_op jit(solution)/shard_map/ppermute | solution.py:55
  138.9 7.9 %collective-permute-start.20 = (f32[128,512]{1,0:T(8,128)S(1)}, f32[128,512]{1,0:T(8,128)S(1)}, u32[]{:S(2)}, u32[]{:S(2)}) collective-permute-start(f32[128,512]{1,0:T(8,128)S(1)} %merge.10), channel_id=1, source_target_pairs={{0,14},{1,15},{2,0},{3,1},{4,2},{5,3},{6,4},{7,5},{8,6},{9,7},{10,... | collective-permute-start | bytes 786440 | tf_op jit(solution)/shard_map/ppermute | solution.py:55
  143.0 7.7 %collective-permute-start.17 = (f32[128,512]{1,0:T(8,128)S(1)}, f32[128,512]{1,0:T(8,128)S(1)}, u32[]{:S(2)}, u32[]{:S(2)}) collective-permute-start(f32[128,512]{1,0:T(8,128)S(1)} %merge.8), channel_id=1, source_target_pairs={{0,2},{1,3},{2,4},{3,5},{4,6},{5,7},{6,8},{7,9},{8,10},{9,11},{10,... | collective-permute-start | bytes 786440 | tf_op jit(solution)/shard_map/ppermute | solution.py:55
  146.8 7.7 %collective-permute-start.21 = (f32[128,512]{1,0:T(8,128)S(1)}, f32[128,512]{1,0:T(8,128)S(1)}, u32[]{:S(2)}, u32[]{:S(2)}) collective-permute-start(f32[128,512]{1,0:T(8,128)S(1)} %merge.11), channel_id=1, source_target_pairs={{0,14},{1,15},{2,0},{3,1},{4,2},{5,3},{6,4},{7,5},{8,6},{9,7},{10,... | collective-permute-start | bytes 786440 | tf_op jit(solution)/shard_map/ppermute | solution.py:55
  154.6 9.8 %collective-permute-start.22 = (bf16[512,128]{1,0:T(8,128)(2,1)S(1)}, bf16[512,128]{1,0:T(8,128)(2,1)S(1)}, u32[]{:S(2)}, u32[]{:S(2)}) collective-permute-start(bf16[512,128]{1,0:T(8,128)(2,1)S(1)} %finish.1), channel_id=1, source_target_pairs={{0,0},{1,48},{2,1},{3,49},{4,4},{5,52},{6,5},{7,53},{8,8},{9,56},{... | collective-permute-start | bytes 393224 | tf_op jit(solution)/shard_map/ppermute | solution.py:55

commit v6 on v5

--- a/solution.py
+++ b/solution.py
@@ -56,9 +56,9 @@
 
 
 def prepare_kernel(
-    place, amp_mask, int_mask, a_any, b_any, own, oth, near, up, down, over, a, b, scratch, sems
+    amp_mask, int_mask, a_any, b_any, own, oth, near, up, down, over, a, b, scratch, sems
 ):
-    y, x = place[0], place[1]
+    y, x = lax.axis_index("y"), lax.axis_index("x")
     block_q = 2 * y + x // 2
     low = jnp.minimum(x, 3 - x)
     turns = (y, lax.rem(y + 1, 4), lax.rem(y + 3, 4), lax.rem(y + 2, 4))
@@ -92,7 +92,7 @@
                         near[pl.ds(128, 64), pl.ds((2 * k + half) * RB, RB)] = value
 
 
-def prepare(place, amp_mask, int_mask, a, b):
+def prepare(amp_mask, int_mask, a, b):
     piece = jax.ShapeDtypeStruct((KD, 2 * RB), jnp.bfloat16)
     two = jax.ShapeDtypeStruct((2, KD, 2 * RB), jnp.bfloat16)
     near = jax.ShapeDtypeStruct((KD, KT), jnp.bfloat16)
@@ -102,7 +102,7 @@
         prepare_kernel,
         out_shape=(piece, piece, near, two, two, two),
         grid_spec=pltpu.PrefetchScalarGridSpec(
-            num_scalar_prefetch=3,
+            num_scalar_prefetch=2,
             grid=(1,),
             in_specs=[anywhere, anywhere],
             out_specs=(vmem,) * 6,
@@ -116,7 +116,7 @@
         compiler_params=pltpu.CompilerParams(vmem_limit_bytes=55 << 20),
         cost_estimate=pl.CostEstimate(flops=0, bytes_accessed=8 << 20, transcendentals=0),
         name="prepare",
-    )(place, amp_mask, int_mask.T, a, b)
+    )(amp_mask, int_mask.T, a, b)
 
 
 def follow_kernel(value, after, out):
@@ -281,7 +281,7 @@
 def local(amplitudes, integrals, amp_mask, int_mask, occ_row, occ_col, vir_energy):
     y, x, z, core = (lax.axis_index(name) for name in AXES)
     place = jnp.stack([y, x, z]).astype(jnp.int32)
-    own, oth, near, up, down, over = prepare(place, amp_mask, int_mask, amplitudes, integrals)
+    own, oth, near, up, down, over = prepare(amp_mask, int_mask, amplitudes, integrals)
 
     from_down = send(up, UP)
     from_up = send(down, DOWN)
@@ -305,12 +305,12 @@
     amps = (early, own_rest, p1, c1, x1)
     keep_half = jnp.bitwise_xor(x // 2, core).astype(jnp.int32)
     give = arrange(place, (1 - keep_half)[None], amps)
-    given = jnp.dot(slabs, give, preferred_element_type=jnp.float32)
-    taken = send(given, SWAP)
+    first_taken = send(jnp.dot(slabs[:128], give, preferred_element_type=jnp.float32), SWAP)
+    taken = send(jnp.dot(slabs[128:], give, preferred_element_type=jnp.float32), SWAP)
     keep = arrange(place, keep_half[None], amps)
 
-    farthest = jnp.dot(slabs[:128], keep, preferred_element_type=jnp.float32) + taken[:128]
-    others = jnp.dot(slabs[128:], keep, preferred_element_type=jnp.float32) + taken[128:]
+    farthest = jnp.dot(slabs[:128], keep, preferred_element_type=jnp.float32) + first_taken
+    others = jnp.dot(slabs[128:], keep, preferred_element_type=jnp.float32) + taken
     ahead, behind = farthest[:64], farthest[64:]
     for step in range(3):
         ahead, behind = send(ahead, AHEAD), send(behind, BEHIND)

time: 165 us -> 164 us (level)
  the two profiles are of different devices: /device:TPU:96 before, /device:TPU:32 now
where the time goes in v6:
time: 164 us; the launch traced here: 163 us
  waiting for transfers between devices  98.9 us (60%)
  starting transfers between devices  33.4 us (20%)
  Pallas kernels  13.9 us (8%)
  local copies, waits for them, and re-layouts  8.93 us (5%)
  matrix products  7.25 us (4%)
    ppermute x24, waiting for transfers between devices, send(): return lax.ppermute(value, AXES, where)  98.9 us
    ppermute x24, starting transfers between devices, send(): return lax.ppermute(value, AXES, where)  33.4 us
    unnamed x25, local copies, waits for them, and re-layouts  6.24 us
    pallas_call x2, Pallas kernels, arrange(): pl.pallas_call(arrange_kernel, out_shape=jax.ShapeDtypeStruct((KT, RB), j...  5.09 us
    pallas_call x1, Pallas kernels, prepare(): pl.pallas_call(prepare_kernel, out_shape=(piece, piece, near, two, two, t...  4.87 us
  transfers between devices with their start and end apart: 24, of which 13 were waited for; matrix products, arithmetic and copies ran while one was open for 5% of the time, Pallas kernels for 3%

profile of v6, /device:TPU:32, one launch (start us, length us, event | category | flops | bytes accessed | tf_op | source)
XLA Modules:
  0.0 163.4 jit_solution(14161463845010292891)
XLA Ops:
  0.0 4.9 %prepare.1 = (bf16[192,1024]{1,0:T(8,128)(2,1)}, bf16[192,1024]{1,0:T(8,128)(2,1)}, bf16[192,3072]{1,0:T(8,128)(2,1)}, bf16[2,192,1024]{2,1,0:T(8,128)(2,1)}, bf...) custom-call(s32[4,8]{1,0:T(4,128)} %amp_mask.1, s32[4,8]{1,0:T(4,128)} %bitcast.17, ...), custom_call_target="tpu_custom_call" | custom-call | bytes 8388608 | tf_op jit(solution)/shard_map/prepare/pallas_call | solution.py:101
  4.9 1.6 collective-permute-start
  6.5 2.1 %collective-permute-start.4 = (bf16[192,1024]{1,0:T(8,128)(2,1)}, bf16[192,1024]{1,0:T(8,128)(2,1)S(1)}, u32[]{:S(2)}, u32[]{:S(2)}) collective-permute-start(bf16[192,1024]{1,0:T(8,128)(2,1)} %get-tuple-element.19.own), channel_id=1, source_target_pairs={{0,48},{1,49},{2,50},{3,51},{4,52},{5,53},{6,54},{7,55},{8,56},{9,... | collective-permute-start | bytes 1179656 | tf_op jit(solution)/shard_map/ppermute | solution.py:55
  8.6 1.6 collective-permute-start.1
  10.1 1.7 %collective-permute-start.2 = (bf16[2,192,1024]{2,1,0:T(8,128)(2,1)}, bf16[2,192,1024]{2,1,0:T(8,128)(2,1)S(1)}, u32[]{:S(2)}, u32[]{:S(2)}) collective-permute-start(bf16[2,192,1024]{2,1,0:T(8,128)(2,1)} %get-tuple-element.17), channel_id=1, source_target_pairs={{0,192},{1,193},{2,194},{3,195},{4,196},{5,197},{6,198},{7,199},{8... | collective-permute-start | bytes 2359304 | tf_op jit(solution)/shard_map/ppermute | solution.py:55
  11.8 2.0 %collective-permute-start.3 = (bf16[2,192,1024]{2,1,0:T(8,128)(2,1)}, bf16[2,192,1024]{2,1,0:T(8,128)(2,1)S(1)}, u32[]{:S(2)}, u32[]{:S(2)}) collective-permute-start(bf16[2,192,1024]{2,1,0:T(8,128)(2,1)} %get-tuple-element.18), channel_id=1, source_target_pairs={{0,128},{1,129},{2,130},{3,131},{4,132},{5,133},{6,134},{7,135},{8... | collective-permute-start | bytes 2359304 | tf_op jit(solution)/shard_map/ppermute | solution.py:55
  13.8 4.7 %collective-permute-done.4.after.p0 = bf16[192,1024]{1,0:T(8,128)(2,1)S(1)} collective-permute-done((bf16[192,1024]{1,0:T(8,128)(2,1)}, bf16[192,1024]{1,0:T(8,128)(2,1)S(1)}, u32[]{:S(2)}, u32[]{:S(2)}) %collective-permute-start.4) | collective-permute-done | bytes 393248 | tf_op jit(solution)/shard_map/ppermute | solution.py:55
  18.5 1.0 copy-done.8
  19.5 1.6 collective-permute-start.5
  21.1 22.4 %collective-permute-done.5.x0 = bf16[192,1024]{1,0:T(8,128)(2,1)S(1)} collective-permute-done((bf16[192,1024]{1,0:T(8,128)(2,1)S(1)}, bf16[192,1024]{1,0:T(8,128)(2,1)S(1)}, u32[]{:S(2)}, u32[]{:S(2)}) %collective-permute-start.5) | collective-permute-done | bytes 393248 | tf_op jit(solution)/shard_map/ppermute | solution.py:55
  43.5 3.3 %collective-permute-done.3.over = bf16[2,192,1024]{2,1,0:T(8,128)(2,1)S(1)} collective-permute-done((bf16[2,192,1024]{2,1,0:T(8,128)(2,1)}, bf16[2,192,1024]{2,1,0:T(8,128)(2,1)S(1)}, u32[]{:S(2)}, u32[]{:S(2)}) %collective-permute-start.3) | collective-permute-done | bytes 786464 | tf_op jit(solution)/shard_map/ppermute | solution.py:55
  46.8 1.3 copy-done.6
  48.1 1.0 copy-done.7
  49.1 1.4 gather.1
  50.5 1.8 %collective-permute-start.7 = (bf16[256,3072]{1,0:T(8,128)(2,1)S(1)}, bf16[256,3072]{1,0:T(8,128)(2,1)S(1)}, u32[]{:S(2)}, u32[]{:S(2)}) collective-permute-start(bf16[256,3072]{1,0:T(8,128)(2,1)S(1)} %get-tuple-element.21.here), channel_id=1, source_target_pairs={{0,192},{1,193},{2,194},{3,195},{4,196},{5,197},{6,198},{7,199},{8... | collective-permute-start | bytes 4718600 | tf_op jit(solution)/shard_map/ppermute | solution.py:55
  52.5 0.9 collective-permute-start.12
  53.4 1.1 collective-permute-start.11
  54.5 2.1 %collective-permute-start.10 = (bf16[3,192,1024]{2,1,0:T(8,128)(2,1)S(1)}, bf16[3,192,1024]{2,1,0:T(8,128)(2,1)}, u32[]{:S(2)}, u32[]{:S(2)}) collective-permute-start(bf16[3,192,1024]{2,1,0:T(8,128)(2,1)S(1)} %get-tuple-element.23.own_rest), channel_id=1, source_target_pairs={{0,48},{1,49},{2,50},{3,51},{4,52},{5,53},{6,54},{7,55},{8,56},{9,... | collective-permute-start | bytes 3538952 | tf_op jit(solution)/shard_map/ppermute | solution.py:55
  56.6 28.5 %collective-permute-done.7.up = bf16[256,3072]{1,0:T(8,128)(2,1)S(1)} collective-permute-done((bf16[256,3072]{1,0:T(8,128)(2,1)S(1)}, bf16[256,3072]{1,0:T(8,128)(2,1)S(1)}, u32[]{:S(2)}, u32[]{:S(2)}) %collective-permute-start.7) | collective-permute-done | bytes 1572896 | tf_op jit(solution)/shard_map/ppermute | solution.py:55
  85.1 1.0 slice.27
  86.1 1.1 copy-done
  87.2 2.5 %collective-permute-start.9 = (bf16[128,3072]{1,0:T(8,128)(2,1)}, bf16[128,3072]{1,0:T(8,128)(2,1)S(1)}, u32[]{:S(2)}, u32[]{:S(2)}) collective-permute-start(bf16[128,3072]{1,0:T(8,128)(2,1)} %slice.27), channel_id=1, source_target_pairs={{0,192},{1,193},{2,194},{3,195},{4,196},{5,197},{6,198},{7,199},{8... | collective-permute-start | bytes 2359304 | tf_op jit(solution)/shard_map/ppermute | solution.py:55
  89.7 0.9 slice.26
  90.7 1.1 copy-done.2
  91.9 11.9 %collective-permute-done.11.c1 = bf16[3,192,1024]{2,1,0:T(8,128)(2,1)} collective-permute-done((bf16[3,192,1024]{2,1,0:T(8,128)(2,1)}, bf16[3,192,1024]{2,1,0:T(8,128)(2,1)}, u32[]{:S(2)}, u32[]{:S(2)}) %collective-permute-start.11) | collective-permute-done | bytes 1179680 | tf_op jit(solution)/shard_map/ppermute | solution.py:55
  103.8 1.5 collective-permute-done.10.p1
  105.3 2.7 %arrange.3 = bf16[3072,512]{1,0:T(8,128)(2,1)S(1)} custom-call(s32[3]{0:T(128)S(1)} %pad_add_fusion.place, s32[1]{0:T(128)} %bitcast.5.half, bf16[4,192,1024]{2,1,0:T(8,128)(2,1)S(1)} %get-tuple-element.22.early, bf16[3,192,1024]{2,1,0:T(8,128)(2,1)S(1)} %get-tuple-element.23.own_rest, bf16[3,192,1024]{2,1,0:T(8,128)(2,1)} %collective-permute-done.10.p1, ...), custom_call_target="tpu_custom_call" | custom-call | bytes 6291456 | tf_op jit(solution)/shard_map/arrange/pallas_call | solution.py:224
  108.0 1.5 collective-permute-done.8.far0
  109.6 2.1 %join.1 = bf16[1024,3072]{1,0:T(8,128)(2,1)S(1)} custom-call(s32[3]{0:T(128)S(1)} %pad_add_fusion.place, bf16[256,3072]{1,0:T(8,128)(2,1)S(1)} %copy-done.5, bf16[256,3072]{1,0:T(8,128)(2,1)S(1)} %copy-done.3, bf16[256,3072]{1,0:T(8,128)(2,1)S(1)} %copy-done.1, bf16[128,3072]{1,0:T(8,128)(2,1)} %collective-permute-done.8.far0, ...), custom_call_target="tpu_custom_call" | custom-call | bytes 6291456 | tf_op jit(solution)/shard_map/join/pallas_call | solution.py:194
  111.7 3.0 %fusion = f32[896,512]{1,0:T(8,128)S(1)} fusion(bf16[3072,512]{1,0:T(8,128)(2,1)S(1)} %arrange.3, bf16[1024,3072]{1,0:T(8,128)(2,1)S(1)} %join.1), kind=kOutput, calls=%fused_computation | convolution fusion | flops 2818572288 | bytes 10485760 | tf_op jit(solution)/shard_map/dot_general | solution.py:309
  115.0 0.6 fusion.7
  116.1 2.4 %arrange.2 = bf16[3072,512]{1,0:T(8,128)(2,1)S(1)} custom-call(s32[3]{0:T(128)S(1)} %pad_add_fusion.place, s32[1]{0:T(128)} %bitcast.4.half, bf16[4,192,1024]{2,1,0:T(8,128)(2,1)S(1)} %get-tuple-element.22.early, bf16[3,192,1024]{2,1,0:T(8,128)(2,1)S(1)} %get-tuple-element.23.own_rest, bf16[3,192,1024]{2,1,0:T(8,128)(2,1)} %collective-permute-done.10.p1, ...), custom_call_target="tpu_custom_call" | custom-call | bytes 6291456 | tf_op jit(solution)/shard_map/arrange/pallas_call | solution.py:224
  118.5 0.6 collective-permute-done.14
  119.1 0.6 convolution_add_fusion
  120.0 1.9 %collective-permute-start.15 = (f32[64,512]{1,0:T(8,128)S(1)}, f32[64,512]{1,0:T(8,128)S(1)}, u32[]{:S(2)}, u32[]{:S(2)}) collective-permute-start(f32[64,512]{1,0:T(8,128)S(1)} %get-tuple-element.26), channel_id=1, source_target_pairs={{0,2},{1,3},{2,4},{3,5},{4,6},{5,7},{6,8},{7,9},{8,10},{9,11},{10,... | collective-permute-start | bytes 393224 | tf_op jit(solution)/shard_map/ppermute | solution.py:55
  121.9 3.0 %fusion.4.mine = f32[896,512]{1,0:T(8,128)S(1)} fusion(f32[896,512]{1,0:T(8,128)S(1)} %collective-permute-done.13, bf16[3072,512]{1,0:T(8,128)(2,1)S(1)} %arrange.2, bf16[1024,3072]{1,0:T(8,128)(2,1)S(1)} %join.1), kind=kOutput, calls=%fused_computation.4 | convolution fusion | flops 2819031040 | bytes 12320768 | tf_op jit(solution)/shard_map/dot_general | solution.py:313
  124.9 4.4 %collective-permute-done.15.got = f32[64,512]{1,0:T(8,128)S(1)} collective-permute-done((f32[64,512]{1,0:T(8,128)S(1)}, f32[64,512]{1,0:T(8,128)S(1)}, u32[]{:S(2)}, u32[]{:S(2)}) %collective-permute-start.15) | collective-permute-done | bytes 131104 | tf_op jit(solution)/shard_map/ppermute | solution.py:55
  129.5 3.0 %collective-permute-start.20 = (f32[128,512]{1,0:T(8,128)S(1)}, f32[128,512]{1,0:T(8,128)S(1)}, u32[]{:S(2)}, u32[]{:S(2)}) collective-permute-start(f32[128,512]{1,0:T(8,128)S(1)} %merge.9), channel_id=1, source_target_pairs={{0,14},{1,15},{2,0},{3,1},{4,2},{5,3},{6,4},{7,5},{8,6},{9,7},{10,... | collective-permute-start | bytes 786440 | tf_op jit(solution)/shard_map/ppermute | solution.py:55
  132.5 5.3 %collective-permute-done.16.got = f32[128,512]{1,0:T(8,128)S(1)} collective-permute-done((f32[128,512]{1,0:T(8,128)S(1)}, f32[128,512]{1,0:T(8,128)S(1)}, u32[]{:S(2)}, u32[]{:S(2)}) %collective-permute-start.16) | collective-permute-done | bytes 262176 | tf_op jit(solution)/shard_map/ppermute | solution.py:55
  138.1 3.0 %collective-permute-start.21 = (f32[128,512]{1,0:T(8,128)S(1)}, f32[128,512]{1,0:T(8,128)S(1)}, u32[]{:S(2)}, u32[]{:S(2)}) collective-permute-start(f32[128,512]{1,0:T(8,128)S(1)} %merge.10), channel_id=1, source_target_pairs={{0,14},{1,15},{2,0},{3,1},{4,2},{5,3},{6,4},{7,5},{8,6},{9,7},{10,... | collective-permute-start | bytes 786440 | tf_op jit(solution)/shard_map/ppermute | solution.py:55
  141.1 0.6 dynamic_slice.15
  141.7 3.8 %collective-permute-done.17.got = f32[128,512]{1,0:T(8,128)S(1)} collective-permute-done((f32[128,512]{1,0:T(8,128)S(1)}, f32[128,512]{1,0:T(8,128)S(1)}, u32[]{:S(2)}, u32[]{:S(2)}) %collective-permute-start.17) | collective-permute-done | bytes 262176 | tf_op jit(solution)/shard_map/ppermute | solution.py:55
  145.7 3.1 %collective-permute-start.22 = (f32[128,512]{1,0:T(8,128)S(1)}, f32[128,512]{1,0:T(8,128)S(1)}, u32[]{:S(2)}, u32[]{:S(2)}) collective-permute-start(f32[128,512]{1,0:T(8,128)S(1)} %merge.11), channel_id=1, source_target_pairs={{0,14},{1,15},{2,0},{3,1},{4,2},{5,3},{6,4},{7,5},{8,6},{9,7},{10,... | collective-permute-start | bytes 786440 | tf_op jit(solution)/shard_map/ppermute | solution.py:55
  148.8 0.7 subtract_bitcast_fusion
  149.7 3.3 %collective-permute-done.18.ahead = f32[128,512]{1,0:T(8,128)S(1)} collective-permute-done((f32[128,512]{1,0:T(8,128)S(1)}, f32[128,512]{1,0:T(8,128)S(1)}, u32[]{:S(2)}, u32[]{:S(2)}) %collective-permute-start.18) | collective-permute-done | bytes 262176 | tf_op jit(solution)/shard_map/ppermute | solution.py:55
  153.2 1.9 %collective-permute-start.23 = (bf16[512,128]{1,0:T(8,128)(2,1)S(1)}, bf16[512,128]{1,0:T(8,128)(2,1)S(1)}, u32[]{:S(2)}, u32[]{:S(2)}) collective-permute-start(bf16[512,128]{1,0:T(8,128)(2,1)S(1)} %finish.1), channel_id=1, source_target_pairs={{0,0},{1,48},{2,1},{3,49},{4,4},{5,52},{6,5},{7,53},{8,8},{9,56},{... | collective-permute-start | bytes 393224 | tf_op jit(solution)/shard_map/ppermute | solution.py:55
  155.1 7.6 %collective-permute-done.23 = bf16[512,128]{1,0:T(8,128)(2,1)S(1)} collective-permute-done((bf16[512,128]{1,0:T(8,128)(2,1)S(1)}, bf16[512,128]{1,0:T(8,128)(2,1)S(1)}, u32[]{:S(2)}, u32[]{:S(2)}) %collective-permute-start.23) | collective-permute-done | bytes 131104 | tf_op jit(solution)/shard_map/ppermute | solution.py:55
  162.7 0.7 copy.10
  (51 shorter events, 2.3 us)
Async XLA Ops:
  4.9 41.9 %collective-permute-start = (bf16[192,3072]{1,0:T(8,128)(2,1)}, bf16[192,3072]{1,0:T(8,128)(2,1)S(1)}, u32[]{:S(2)}, u32[]{:S(2)}) collective-permute-start(bf16[192,3072]{1,0:T(8,128)(2,1)} %get-tuple-element.15.near), channel_id=1, source_target_pairs={{0,16},{1,17},{2,18},{3,19},{4,20},{5,21},{6,22},{7,23},{8,24},{9,... | collective-permute-start | bytes 3538952 | tf_op jit(solution)/shard_map/ppermute | solution.py:55
  6.5 12.0 %collective-permute-start.4 = (bf16[192,1024]{1,0:T(8,128)(2,1)}, bf16[192,1024]{1,0:T(8,128)(2,1)S(1)}, u32[]{:S(2)}, u32[]{:S(2)}) collective-permute-start(bf16[192,1024]{1,0:T(8,128)(2,1)} %get-tuple-element.19.own), channel_id=1, source_target_pairs={{0,48},{1,49},{2,50},{3,51},{4,52},{5,53},{6,54},{7,55},{8,56},{9,... | collective-permute-start | bytes 1179656 | tf_op jit(solution)/shard_map/ppermute | solution.py:55
  8.6 35.0 %collective-permute-start.1 = (bf16[2,192,1024]{2,1,0:T(8,128)(2,1)}, bf16[2,192,1024]{2,1,0:T(8,128)(2,1)S(1)}, u32[]{:S(2)}, u32[]{:S(2)}) collective-permute-start(bf16[2,192,1024]{2,1,0:T(8,128)(2,1)} %get-tuple-element.16), channel_id=1, source_target_pairs={{0,64},{1,65},{2,66},{3,67},{4,68},{5,69},{6,70},{7,71},{8,72},{9,... | collective-permute-start | bytes 2359304 | tf_op jit(solution)/shard_map/ppermute | solution.py:55
  10.1 33.4 %collective-permute-start.2 = (bf16[2,192,1024]{2,1,0:T(8,128)(2,1)}, bf16[2,192,1024]{2,1,0:T(8,128)(2,1)S(1)}, u32[]{:S(2)}, u32[]{:S(2)}) collective-permute-start(bf16[2,192,1024]{2,1,0:T(8,128)(2,1)} %get-tuple-element.17), channel_id=1, source_target_pairs={{0,192},{1,193},{2,194},{3,195},{4,196},{5,197},{6,198},{7,199},{8... | collective-permute-start | bytes 2359304 | tf_op jit(solution)/shard_map/ppermute | solution.py:55
  11.8 35.0 %collective-permute-start.3 = (bf16[2,192,1024]{2,1,0:T(8,128)(2,1)}, bf16[2,192,1024]{2,1,0:T(8,128)(2,1)S(1)}, u32[]{:S(2)}, u32[]{:S(2)}) collective-permute-start(bf16[2,192,1024]{2,1,0:T(8,128)(2,1)} %get-tuple-element.18), channel_id=1, source_target_pairs={{0,128},{1,129},{2,130},{3,131},{4,132},{5,133},{6,134},{7,135},{8... | collective-permute-start | bytes 2359304 | tf_op jit(solution)/shard_map/ppermute | solution.py:55
  18.5 1.0 copy-start.8
  19.5 24.0 %collective-permute-start.5 = (bf16[192,1024]{1,0:T(8,128)(2,1)S(1)}, bf16[192,1024]{1,0:T(8,128)(2,1)S(1)}, u32[]{:S(2)}, u32[]{:S(2)}) collective-permute-start(bf16[192,1024]{1,0:T(8,128)(2,1)S(1)} %follow.1), channel_id=1, source_target_pairs={{0,32},{1,33},{2,34},{3,35},{4,36},{5,37},{6,38},{7,39},{8,40},{9,... | collective-permute-start | bytes 1179656 | tf_op jit(solution)/shard_map/ppermute | solution.py:55
  46.8 1.3 copy-start.6
  48.1 1.0 copy-start.7
  50.5 40.2 %copy-start.4 = (bf16[256,3072]{1,0:T(8,128)(2,1)}, bf16[256,3072]{1,0:T(8,128)(2,1)S(1)}, u32[]{:S(2)}) copy-start(bf16[256,3072]{1,0:T(8,128)(2,1)S(1)} %get-tuple-element.21.here) | copy-start | bytes 4718596
  50.5 34.6 %collective-permute-start.7 = (bf16[256,3072]{1,0:T(8,128)(2,1)S(1)}, bf16[256,3072]{1,0:T(8,128)(2,1)S(1)}, u32[]{:S(2)}, u32[]{:S(2)}) collective-permute-start(bf16[256,3072]{1,0:T(8,128)(2,1)S(1)} %get-tuple-element.21.here), channel_id=1, source_target_pairs={{0,192},{1,193},{2,194},{3,195},{4,196},{5,197},{6,198},{7,199},{8... | collective-permute-start | bytes 4718600 | tf_op jit(solution)/shard_map/ppermute | solution.py:55
  52.3 37.5 %collective-permute-start.6 = (bf16[256,3072]{1,0:T(8,128)(2,1)S(1)}, bf16[256,3072]{1,0:T(8,128)(2,1)S(1)}, u32[]{:S(2)}, u32[]{:S(2)}) collective-permute-start(bf16[256,3072]{1,0:T(8,128)(2,1)S(1)} %get-tuple-element.21.here), channel_id=1, source_target_pairs={{0,64},{1,65},{2,66},{3,67},{4,68},{5,69},{6,70},{7,71},{8,72},{9,... | collective-permute-start | bytes 4718600 | tf_op jit(solution)/shard_map/ppermute | solution.py:55
  52.5 39.4 %collective-permute-start.12 = (bf16[3,192,1024]{2,1,0:T(8,128)(2,1)}, bf16[3,192,1024]{2,1,0:T(8,128)(2,1)}, u32[]{:S(2)}, u32[]{:S(2)}) collective-permute-start(bf16[3,192,1024]{2,1,0:T(8,128)(2,1)} %get-tuple-element.24), channel_id=1, source_target_pairs={{0,32},{1,33},{2,34},{3,35},{4,36},{5,37},{6,38},{7,39},{8,40},{9,... | collective-permute-start | bytes 3538952 | tf_op jit(solution)/shard_map/ppermute | solution.py:55
  53.4 50.4 %collective-permute-start.11 = (bf16[3,192,1024]{2,1,0:T(8,128)(2,1)}, bf16[3,192,1024]{2,1,0:T(8,128)(2,1)}, u32[]{:S(2)}, u32[]{:S(2)}) collective-permute-start(bf16[3,192,1024]{2,1,0:T(8,128)(2,1)} %get-tuple-element.24), channel_id=1, source_target_pairs={{0,16},{1,17},{2,18},{3,19},{4,20},{5,21},{6,22},{7,23},{8,24},{9,... | collective-permute-start | bytes 3538952 | tf_op jit(solution)/shard_map/ppermute | solution.py:55
  54.5 50.8 %collective-permute-start.10 = (bf16[3,192,1024]{2,1,0:T(8,128)(2,1)S(1)}, bf16[3,192,1024]{2,1,0:T(8,128)(2,1)}, u32[]{:S(2)}, u32[]{:S(2)}) collective-permute-start(bf16[3,192,1024]{2,1,0:T(8,128)(2,1)S(1)} %get-tuple-element.23.own_rest), channel_id=1, source_target_pairs={{0,48},{1,49},{2,50},{3,51},{4,52},{5,53},{6,54},{7,55},{8,56},{9,... | collective-permute-start | bytes 3538952 | tf_op jit(solution)/shard_map/ppermute | solution.py:55
  86.1 1.1 copy-start
  87.2 20.8 %collective-permute-start.9 = (bf16[128,3072]{1,0:T(8,128)(2,1)}, bf16[128,3072]{1,0:T(8,128)(2,1)S(1)}, u32[]{:S(2)}, u32[]{:S(2)}) collective-permute-start(bf16[128,3072]{1,0:T(8,128)(2,1)} %slice.27), channel_id=1, source_target_pairs={{0,192},{1,193},{2,194},{3,195},{4,196},{5,197},{6,198},{7,199},{8... | collective-permute-start | bytes 2359304 | tf_op jit(solution)/shard_map/ppermute | solution.py:55
  90.7 1.1 copy-start.2
  91.8 17.7 %collective-permute-start.8 = (bf16[128,3072]{1,0:T(8,128)(2,1)}, bf16[128,3072]{1,0:T(8,128)(2,1)}, u32[]{:S(2)}, u32[]{:S(2)}) collective-permute-start(bf16[128,3072]{1,0:T(8,128)(2,1)} %slice.26), channel_id=1, source_target_pairs={{0,64},{1,65},{2,66},{3,67},{4,68},{5,69},{6,70},{7,71},{8,72},{9,... | collective-permute-start | bytes 2359304 | tf_op jit(solution)/shard_map/ppermute | solution.py:55
  105.3 4.3 %copy-start.1 = (bf16[256,3072]{1,0:T(8,128)(2,1)S(1)}, bf16[256,3072]{1,0:T(8,128)(2,1)}, u32[]{:S(2)}) copy-start(bf16[256,3072]{1,0:T(8,128)(2,1)} %copy-done) | copy-start | bytes 4718596
  105.3 4.3 %copy-start.3 = (bf16[256,3072]{1,0:T(8,128)(2,1)S(1)}, bf16[256,3072]{1,0:T(8,128)(2,1)}, u32[]{:S(2)}) copy-start(bf16[256,3072]{1,0:T(8,128)(2,1)} %copy-done.2) | copy-start | bytes 4718596
  105.3 4.3 %copy-start.5 = (bf16[256,3072]{1,0:T(8,128)(2,1)S(1)}, bf16[256,3072]{1,0:T(8,128)(2,1)}, u32[]{:S(2)}) copy-start(bf16[256,3072]{1,0:T(8,128)(2,1)} %copy-done.4) | copy-start | bytes 4718596
  114.7 7.2 %collective-permute-start.13 = (f32[896,512]{1,0:T(8,128)S(1)}, f32[896,512]{1,0:T(8,128)S(1)}, u32[]{:S(2)}, u32[]{:S(2)}) collective-permute-start(f32[896,512]{1,0:T(8,128)S(1)} %fusion), channel_id=1, source_target_pairs={{0,1},{1,0},{2,3},{3,2},{4,5},{5,4},{6,7},{7,6},{8,9},{9,8},{10,11... | collective-permute-start | bytes 5505032 | tf_op jit(solution)/shard_map/ppermute | solution.py:55
  115.6 3.6 %collective-permute-start.14 = (f32[128,512]{1,0:T(8,128)S(1)}, f32[128,512]{1,0:T(8,128)S(1)}, u32[]{:S(2)}, u32[]{:S(2)}) collective-permute-start(f32[128,512]{1,0:T(8,128)S(1)} %fusion.7), channel_id=1, source_target_pairs={{0,1},{1,0},{2,3},{3,2},{4,5},{5,4},{6,7},{7,6},{8,9},{9,8},{10,11... | collective-permute-start | bytes 786440 | tf_op jit(solution)/shard_map/ppermute | solution.py:55
  119.8 9.7 %collective-permute-start.19 = (f32[64,512]{1,0:T(8,128)S(1)}, f32[64,512]{1,0:T(8,128)S(1)}, u32[]{:S(2)}, u32[]{:S(2)}) collective-permute-start(f32[64,512]{1,0:T(8,128)S(1)} %get-tuple-element.25), channel_id=1, source_target_pairs={{0,14},{1,15},{2,0},{3,1},{4,2},{5,3},{6,4},{7,5},{8,6},{9,7},{10,... | collective-permute-start | bytes 393224 | tf_op jit(solution)/shard_map/ppermute | solution.py:55
  120.0 9.4 %collective-permute-start.15 = (f32[64,512]{1,0:T(8,128)S(1)}, f32[64,512]{1,0:T(8,128)S(1)}, u32[]{:S(2)}, u32[]{:S(2)}) collective-permute-start(f32[64,512]{1,0:T(8,128)S(1)} %get-tuple-element.26), channel_id=1, source_target_pairs={{0,2},{1,3},{2,4},{3,5},{4,6},{5,7},{6,8},{7,9},{8,10},{9,11},{10,... | collective-permute-start | bytes 393224 | tf_op jit(solution)/shard_map/ppermute | solution.py:55
  129.4 11.7 %copy-start.10 = (f32[4]{0:T(128)S(1)}, f32[4]{0:T(128)}, u32[]{:S(2)}) copy-start(f32[4]{0:T(128)} %param.12) | copy-start | bytes 52
  129.4 8.5 %collective-permute-start.16 = (f32[128,512]{1,0:T(8,128)S(1)}, f32[128,512]{1,0:T(8,128)S(1)}, u32[]{:S(2)}, u32[]{:S(2)}) collective-permute-start(f32[128,512]{1,0:T(8,128)S(1)} %merge.6), channel_id=1, source_target_pairs={{0,2},{1,3},{2,4},{3,5},{4,6},{5,7},{6,8},{7,9},{8,10},{9,11},{10,... | collective-permute-start | bytes 786440 | tf_op jit(solution)/shard_map/ppermute | solution.py:55
  129.5 8.5 %collective-permute-start.20 = (f32[128,512]{1,0:T(8,128)S(1)}, f32[128,512]{1,0:T(8,128)S(1)}, u32[]{:S(2)}, u32[]{:S(2)}) collective-permute-start(f32[128,512]{1,0:T(8,128)S(1)} %merge.9), channel_id=1, source_target_pairs={{0,14},{1,15},{2,0},{3,1},{4,2},{5,3},{6,4},{7,5},{8,6},{9,7},{10,... | collective-permute-start | bytes 786440 | tf_op jit(solution)/shard_map/ppermute | solution.py:55
  137.9 10.9 %copy-start.9 = (f32[4,128]{1,0:T(4,128)S(1)}, f32[4,128]{1,0:T(4,128)}, u32[]{:S(2)}) copy-start(f32[4,128]{1,0:T(4,128)} %param.13) | copy-start | bytes 6148
  137.9 11.7 %copy-start.11 = (f32[16]{0:T(128)S(1)}, f32[16]{0:T(128)}, u32[]{:S(2)}) copy-start(f32[16]{0:T(128)} %param.11) | copy-start | bytes 196
  137.9 7.6 %collective-permute-start.17 = (f32[128,512]{1,0:T(8,128)S(1)}, f32[128,512]{1,0:T(8,128)S(1)}, u32[]{:S(2)}, u32[]{:S(2)}) collective-permute-start(f32[128,512]{1,0:T(8,128)S(1)} %merge.7), channel_id=1, source_target_pairs={{0,2},{1,3},{2,4},{3,5},{4,6},{5,7},{6,8},{7,9},{8,10},{9,11},{10,... | collective-permute-start | bytes 786440 | tf_op jit(solution)/shard_map/ppermute | solution.py:55
  138.1 7.6 %collective-permute-start.21 = (f32[128,512]{1,0:T(8,128)S(1)}, f32[128,512]{1,0:T(8,128)S(1)}, u32[]{:S(2)}, u32[]{:S(2)}) collective-permute-start(f32[128,512]{1,0:T(8,128)S(1)} %merge.10), channel_id=1, source_target_pairs={{0,14},{1,15},{2,0},{3,1},{4,2},{5,3},{6,4},{7,5},{8,6},{9,7},{10,... | collective-permute-start | bytes 786440 | tf_op jit(solution)/shard_map/ppermute | solution.py:55
  145.5 7.5 %collective-permute-start.18 = (f32[128,512]{1,0:T(8,128)S(1)}, f32[128,512]{1,0:T(8,128)S(1)}, u32[]{:S(2)}, u32[]{:S(2)}) collective-permute-start(f32[128,512]{1,0:T(8,128)S(1)} %merge.8), channel_id=1, source_target_pairs={{0,2},{1,3},{2,4},{3,5},{4,6},{5,7},{6,8},{7,9},{8,10},{9,11},{10,... | collective-permute-start | bytes 786440 | tf_op jit(solution)/shard_map/ppermute | solution.py:55
  145.7 7.3 %collective-permute-start.22 = (f32[128,512]{1,0:T(8,128)S(1)}, f32[128,512]{1,0:T(8,128)S(1)}, u32[]{:S(2)}, u32[]{:S(2)}) collective-permute-start(f32[128,512]{1,0:T(8,128)S(1)} %merge.11), channel_id=1, source_target_pairs={{0,14},{1,15},{2,0},{3,1},{4,2},{5,3},{6,4},{7,5},{8,6},{9,7},{10,... | collective-permute-start | bytes 786440 | tf_op jit(solution)/shard_map/ppermute | solution.py:55
  153.2 9.5 %collective-permute-start.23 = (bf16[512,128]{1,0:T(8,128)(2,1)S(1)}, bf16[512,128]{1,0:T(8,128)(2,1)S(1)}, u32[]{:S(2)}, u32[]{:S(2)}) collective-permute-start(bf16[512,128]{1,0:T(8,128)(2,1)S(1)} %finish.1), channel_id=1, source_target_pairs={{0,0},{1,48},{2,1},{3,49},{4,4},{5,52},{6,5},{7,53},{8,8},{9,56},{... | collective-permute-start | bytes 393224 | tf_op jit(solution)/shard_map/ppermute | solution.py:55

commit v7 on v6

--- a/solution.py
+++ b/solution.py
@@ -190,6 +190,26 @@
     run(moves, sems)
 
 
+def tails_kernel(down, up, far0, far1):
+    far0[...] = down[...]
+    far1[...] = up[...]
+
+
+def tails(down, up):
+    slab = jax.ShapeDtypeStruct((128, KT), jnp.bfloat16)
+    top = pl.BlockSpec((128, KT), lambda i: (0, 0))
+    return pl.pallas_call(
+        tails_kernel,
+        out_shape=(slab, slab),
+        grid=(1,),
+        in_specs=[top, pl.BlockSpec((128, KT), lambda i: (1, 0))],
+        out_specs=(top, top),
+        compiler_params=pltpu.CompilerParams(vmem_limit_bytes=10 << 20),
+        cost_estimate=pl.CostEstimate(flops=0, bytes_accessed=3 << 20, transcendentals=0),
+        name="tails",
+    )(down, up)
+
+
 def join(place, *parts):
     return pl.pallas_call(
         join_kernel,
@@ -298,8 +318,9 @@
     p1 = send(own_rest, PARTNER)
     c1 = send(oth_rest, CROSS)
     x1 = send(oth_rest, ACROSS)
-    b_far0 = send(b_down[:128], UP)
-    b_far1 = send(b_up[128:], DOWN)
+    far0, far1 = tails(b_down, b_up)
+    b_far0 = send(far0, UP)
+    b_far1 = send(far1, DOWN)
     slabs = join(place, b_here, b_down, b_up, b_far0, b_far1)
 
     amps = (early, own_rest, p1, c1, x1)

time: 164 us -> 164 us (level)
  local copies, waits for them, and re-layouts: 8.93 us -> 5.89 us
  Pallas kernels: 13.9 us -> 15.9 us
    slice x2 -> x0, local copies, waits for them, and re-layouts: 1.89 us -> none  [the longest x1 0.96 us: local(): b_far1 = send(b_up[128:], DOWN)]
    unnamed x25 -> x21, local copies, waits for them, and re-layouts: 6.24 us -> 5.1 us
  transfers between devices with their start and end apart: 24 -> 24, of which waited for: 13 -> 13; matrix products, arithmetic and copies ran while one was open for 5% -> 4% of each run, Pallas kernels for 3% -> 4%
where the time goes in v7:
time: 164 us; the launch traced here: 163 us
  waiting for transfers between devices  98.3 us (60%)
  starting transfers between devices  34.2 us (21%)
  Pallas kernels  15.9 us (10%)
  matrix products  7.23 us (4%)
  local copies, waits for them, and re-layouts  5.89 us (4%)
    ppermute x24, waiting for transfers between devices, send(): return lax.ppermute(value, AXES, where)  98.3 us
    ppermute x24, starting transfers between devices, send(): return lax.ppermute(value, AXES, where)  34.2 us
    pallas_call x2, Pallas kernels, arrange(): pl.pallas_call(arrange_kernel, out_shape=jax.ShapeDtypeStruct((KT, RB), j...  5.16 us
    unnamed x21, local copies, waits for them, and re-layouts  5.1 us
    pallas_call x1, Pallas kernels, prepare(): pl.pallas_call(prepare_kernel, out_shape=(piece, piece, near, two, two, t...  4.86 us
  transfers between devices with their start and end apart: 24, of which 13 were waited for; matrix products, arithmetic and copies ran while one was open for 4% of the time, Pallas kernels for 4%

profile of v7, /device:TPU:32, one launch (start us, length us, event | category | flops | bytes accessed | tf_op | source)
XLA Modules:
  0.0 162.6 jit_solution(10205777892243224394)
XLA Ops:
  0.0 4.9 %prepare.1 = (bf16[192,1024]{1,0:T(8,128)(2,1)}, bf16[192,1024]{1,0:T(8,128)(2,1)}, bf16[192,3072]{1,0:T(8,128)(2,1)}, bf16[2,192,1024]{2,1,0:T(8,128)(2,1)}, bf...) custom-call(s32[4,8]{1,0:T(4,128)} %amp_mask.1, s32[4,8]{1,0:T(4,128)} %bitcast.17, ...), custom_call_target="tpu_custom_call" | custom-call | bytes 8388608 | tf_op jit(solution)/shard_map/prepare/pallas_call | solution.py:101
  4.9 1.6 collective-permute-start
  6.4 2.1 %collective-permute-start.4 = (bf16[192,1024]{1,0:T(8,128)(2,1)}, bf16[192,1024]{1,0:T(8,128)(2,1)S(1)}, u32[]{:S(2)}, u32[]{:S(2)}) collective-permute-start(bf16[192,1024]{1,0:T(8,128)(2,1)} %get-tuple-element.21.own), channel_id=1, source_target_pairs={{0,48},{1,49},{2,50},{3,51},{4,52},{5,53},{6,54},{7,55},{8,56},{9,... | collective-permute-start | bytes 1179656 | tf_op jit(solution)/shard_map/ppermute | solution.py:55
  8.5 1.6 collective-permute-start.1
  10.1 1.7 %collective-permute-start.2 = (bf16[2,192,1024]{2,1,0:T(8,128)(2,1)}, bf16[2,192,1024]{2,1,0:T(8,128)(2,1)S(1)}, u32[]{:S(2)}, u32[]{:S(2)}) collective-permute-start(bf16[2,192,1024]{2,1,0:T(8,128)(2,1)} %get-tuple-element.19), channel_id=1, source_target_pairs={{0,192},{1,193},{2,194},{3,195},{4,196},{5,197},{6,198},{7,199},{8... | collective-permute-start | bytes 2359304 | tf_op jit(solution)/shard_map/ppermute | solution.py:55
  11.8 2.0 %collective-permute-start.3 = (bf16[2,192,1024]{2,1,0:T(8,128)(2,1)}, bf16[2,192,1024]{2,1,0:T(8,128)(2,1)S(1)}, u32[]{:S(2)}, u32[]{:S(2)}) collective-permute-start(bf16[2,192,1024]{2,1,0:T(8,128)(2,1)} %get-tuple-element.20), channel_id=1, source_target_pairs={{0,128},{1,129},{2,130},{3,131},{4,132},{5,133},{6,134},{7,135},{8... | collective-permute-start | bytes 2359304 | tf_op jit(solution)/shard_map/ppermute | solution.py:55
  13.8 4.7 %collective-permute-done.4.after.p0 = bf16[192,1024]{1,0:T(8,128)(2,1)S(1)} collective-permute-done((bf16[192,1024]{1,0:T(8,128)(2,1)}, bf16[192,1024]{1,0:T(8,128)(2,1)S(1)}, u32[]{:S(2)}, u32[]{:S(2)}) %collective-permute-start.4) | collective-permute-done | bytes 393248 | tf_op jit(solution)/shard_map/ppermute | solution.py:55
  18.4 1.0 copy-done.6
  19.5 1.6 collective-permute-start.5
  21.1 22.4 %collective-permute-done.5.x0 = bf16[192,1024]{1,0:T(8,128)(2,1)S(1)} collective-permute-done((bf16[192,1024]{1,0:T(8,128)(2,1)S(1)}, bf16[192,1024]{1,0:T(8,128)(2,1)S(1)}, u32[]{:S(2)}, u32[]{:S(2)}) %collective-permute-start.5) | collective-permute-done | bytes 393248 | tf_op jit(solution)/shard_map/ppermute | solution.py:55
  43.5 3.3 %collective-permute-done.3.over = bf16[2,192,1024]{2,1,0:T(8,128)(2,1)S(1)} collective-permute-done((bf16[2,192,1024]{2,1,0:T(8,128)(2,1)}, bf16[2,192,1024]{2,1,0:T(8,128)(2,1)S(1)}, u32[]{:S(2)}, u32[]{:S(2)}) %collective-permute-start.3) | collective-permute-done | bytes 786464 | tf_op jit(solution)/shard_map/ppermute | solution.py:55
  46.8 1.3 copy-done.4
  48.1 1.0 copy-done.5
  49.0 1.9 %gather.1 = (bf16[3,192,1024]{2,1,0:T(8,128)(2,1)}, bf16[3,192,1024]{2,1,0:T(8,128)(2,1)}, bf16[256,3072]{1,0:T(8,128)(2,1)S(1)}, bf16[4,192,1024]{2,1,0:T(8,128)(2,1)S(1)}) custom-call(bf16[192,3072]{1,0:T(8,128)(2,1)S(1)} %copy-done.4, bf16[192,3072]{1,0:T(8,128)(2,1)S(1)} %collective-permute-done.from_near, ...), custom_call_target="tpu_custom_call" | custom-call | bytes 10485760 | tf_op jit(solution)/shard_map/gather/pallas_call | solution.py:159
  50.9 1.8 %collective-permute-start.7 = (bf16[256,3072]{1,0:T(8,128)(2,1)S(1)}, bf16[256,3072]{1,0:T(8,128)(2,1)S(1)}, u32[]{:S(2)}, u32[]{:S(2)}) collective-permute-start(bf16[256,3072]{1,0:T(8,128)(2,1)S(1)} %get-tuple-element.23.here), channel_id=1, source_target_pairs={{0,192},{1,193},{2,194},{3,195},{4,196},{5,197},{6,198},{7,199},{8... | collective-permute-start | bytes 4718600 | tf_op jit(solution)/shard_map/ppermute | solution.py:55
  53.0 0.9 collective-permute-start.12
  53.9 1.1 collective-permute-start.11
  55.0 2.1 %collective-permute-start.10 = (bf16[3,192,1024]{2,1,0:T(8,128)(2,1)}, bf16[3,192,1024]{2,1,0:T(8,128)(2,1)}, u32[]{:S(2)}, u32[]{:S(2)}) collective-permute-start(bf16[3,192,1024]{2,1,0:T(8,128)(2,1)} %get-tuple-element.27.own_rest), channel_id=1, source_target_pairs={{0,48},{1,49},{2,50},{3,51},{4,52},{5,53},{6,54},{7,55},{8,56},{9,... | collective-permute-start | bytes 3538952 | tf_op jit(solution)/shard_map/ppermute | solution.py:55
  57.0 28.5 %collective-permute-done.7.up = bf16[256,3072]{1,0:T(8,128)(2,1)S(1)} collective-permute-done((bf16[256,3072]{1,0:T(8,128)(2,1)S(1)}, bf16[256,3072]{1,0:T(8,128)(2,1)S(1)}, u32[]{:S(2)}, u32[]{:S(2)}) %collective-permute-start.7) | collective-permute-done | bytes 1572896 | tf_op jit(solution)/shard_map/ppermute | solution.py:55
  85.6 2.2 %collective-permute-done.6.down = bf16[256,3072]{1,0:T(8,128)(2,1)S(1)} collective-permute-done((bf16[256,3072]{1,0:T(8,128)(2,1)S(1)}, bf16[256,3072]{1,0:T(8,128)(2,1)S(1)}, u32[]{:S(2)}, u32[]{:S(2)}) %collective-permute-start.6) | collective-permute-done | bytes 1572896 | tf_op jit(solution)/shard_map/ppermute | solution.py:55
  87.8 1.3 tails.1
  89.1 1.1 copy-done
  90.2 3.2 %collective-permute-start.9 = (bf16[128,3072]{1,0:T(8,128)(2,1)}, bf16[128,3072]{1,0:T(8,128)(2,1)}, u32[]{:S(2)}, u32[]{:S(2)}) collective-permute-start(bf16[128,3072]{1,0:T(8,128)(2,1)} %get-tuple-element.25), channel_id=1, source_target_pairs={{0,192},{1,193},{2,194},{3,195},{4,196},{5,197},{6,198},{7,199},{8... | collective-permute-start | bytes 2359304 | tf_op jit(solution)/shard_map/ppermute | solution.py:55
  93.5 10.7 %collective-permute-done.11.c1 = bf16[3,192,1024]{2,1,0:T(8,128)(2,1)} collective-permute-done((bf16[3,192,1024]{2,1,0:T(8,128)(2,1)}, bf16[3,192,1024]{2,1,0:T(8,128)(2,1)}, u32[]{:S(2)}, u32[]{:S(2)}) %collective-permute-start.11) | collective-permute-done | bytes 1179680 | tf_op jit(solution)/shard_map/ppermute | solution.py:55
  104.2 1.5 collective-permute-done.10.p1
  105.7 2.7 %arrange.3 = bf16[3072,512]{1,0:T(8,128)(2,1)S(1)} custom-call(s32[3]{0:T(128)S(1)} %pad_add_fusion.place, s32[1]{0:T(128)} %bitcast.5.half, bf16[4,192,1024]{2,1,0:T(8,128)(2,1)S(1)} %get-tuple-element.26.early, bf16[3,192,1024]{2,1,0:T(8,128)(2,1)} %get-tuple-element.27.own_rest, bf16[3,192,1024]{2,1,0:T(8,128)(2,1)} %collective-permute-done.10.p1, ...), custom_call_target="tpu_custom_call" | custom-call | bytes 6291456 | tf_op jit(solution)/shard_map/arrange/pallas_call | solution.py:244
  108.5 2.4 %join.1 = bf16[1024,3072]{1,0:T(8,128)(2,1)S(1)} custom-call(s32[3]{0:T(128)S(1)} %pad_add_fusion.place, bf16[256,3072]{1,0:T(8,128)(2,1)S(1)} %copy-done.3, bf16[256,3072]{1,0:T(8,128)(2,1)S(1)} %copy-done.1, bf16[256,3072]{1,0:T(8,128)(2,1)S(1)} %collective-permute-done.7.up, bf16[128,3072]{1,0:T(8,128)(2,1)} %collective-permute-done.8.far0, ...), custom_call_target="tpu_custom_call" | custom-call | bytes 6291456 | tf_op jit(solution)/shard_map/join/pallas_call | solution.py:214
  110.9 3.0 %fusion = f32[896,512]{1,0:T(8,128)S(1)} fusion(bf16[3072,512]{1,0:T(8,128)(2,1)S(1)} %arrange.3, bf16[1024,3072]{1,0:T(8,128)(2,1)S(1)} %join.1), kind=kOutput, calls=%fused_computation | convolution fusion | flops 2818572288 | bytes 10485760 | tf_op jit(solution)/shard_map/dot_general | solution.py:330
  113.9 0.3 collective-permute-start.13
  114.1 0.6 fusion.7
  114.7 0.6 collective-permute-start.14
  115.3 2.5 %arrange.2 = bf16[3072,512]{1,0:T(8,128)(2,1)S(1)} custom-call(s32[3]{0:T(128)S(1)} %pad_add_fusion.place, s32[1]{0:T(128)} %bitcast.4.half, bf16[4,192,1024]{2,1,0:T(8,128)(2,1)S(1)} %get-tuple-element.26.early, bf16[3,192,1024]{2,1,0:T(8,128)(2,1)} %get-tuple-element.27.own_rest, bf16[3,192,1024]{2,1,0:T(8,128)(2,1)} %collective-permute-done.10.p1, ...), custom_call_target="tpu_custom_call" | custom-call | bytes 6291456 | tf_op jit(solution)/shard_map/arrange/pallas_call | solution.py:244
  117.8 0.5 collective-permute-done.14
  118.3 0.6 convolution_add_fusion
  119.1 1.9 %collective-permute-start.15 = (f32[64,512]{1,0:T(8,128)S(1)}, f32[64,512]{1,0:T(8,128)S(1)}, u32[]{:S(2)}, u32[]{:S(2)}) collective-permute-start(f32[64,512]{1,0:T(8,128)S(1)} %get-tuple-element.30), channel_id=1, source_target_pairs={{0,2},{1,3},{2,4},{3,5},{4,6},{5,7},{6,8},{7,9},{8,10},{9,11},{10,... | collective-permute-start | bytes 393224 | tf_op jit(solution)/shard_map/ppermute | solution.py:55
  121.0 3.0 %fusion.4.mine = f32[896,512]{1,0:T(8,128)S(1)} fusion(f32[896,512]{1,0:T(8,128)S(1)} %collective-permute-done.13, bf16[3072,512]{1,0:T(8,128)(2,1)S(1)} %arrange.2, bf16[1024,3072]{1,0:T(8,128)(2,1)S(1)} %join.1), kind=kOutput, calls=%fused_computation.4 | convolution fusion | flops 2819031040 | bytes 12320768 | tf_op jit(solution)/shard_map/dot_general | solution.py:334
  124.1 4.4 %collective-permute-done.15.got = f32[64,512]{1,0:T(8,128)S(1)} collective-permute-done((f32[64,512]{1,0:T(8,128)S(1)}, f32[64,512]{1,0:T(8,128)S(1)}, u32[]{:S(2)}, u32[]{:S(2)}) %collective-permute-start.15) | collective-permute-done | bytes 131104 | tf_op jit(solution)/shard_map/ppermute | solution.py:55
  128.7 3.0 %collective-permute-start.20 = (f32[128,512]{1,0:T(8,128)S(1)}, f32[128,512]{1,0:T(8,128)S(1)}, u32[]{:S(2)}, u32[]{:S(2)}) collective-permute-start(f32[128,512]{1,0:T(8,128)S(1)} %merge.9), channel_id=1, source_target_pairs={{0,14},{1,15},{2,0},{3,1},{4,2},{5,3},{6,4},{7,5},{8,6},{9,7},{10,... | collective-permute-start | bytes 786440 | tf_op jit(solution)/shard_map/ppermute | solution.py:55
  131.7 5.3 %collective-permute-done.16.got = f32[128,512]{1,0:T(8,128)S(1)} collective-permute-done((f32[128,512]{1,0:T(8,128)S(1)}, f32[128,512]{1,0:T(8,128)S(1)}, u32[]{:S(2)}, u32[]{:S(2)}) %collective-permute-start.16) | collective-permute-done | bytes 262176 | tf_op jit(solution)/shard_map/ppermute | solution.py:55
  137.2 3.0 %collective-permute-start.21 = (f32[128,512]{1,0:T(8,128)S(1)}, f32[128,512]{1,0:T(8,128)S(1)}, u32[]{:S(2)}, u32[]{:S(2)}) collective-permute-start(f32[128,512]{1,0:T(8,128)S(1)} %merge.10), channel_id=1, source_target_pairs={{0,14},{1,15},{2,0},{3,1},{4,2},{5,3},{6,4},{7,5},{8,6},{9,7},{10,... | collective-permute-start | bytes 786440 | tf_op jit(solution)/shard_map/ppermute | solution.py:55
  140.3 0.6 dynamic_slice.15
  140.9 3.8 %collective-permute-done.17.got = f32[128,512]{1,0:T(8,128)S(1)} collective-permute-done((f32[128,512]{1,0:T(8,128)S(1)}, f32[128,512]{1,0:T(8,128)S(1)}, u32[]{:S(2)}, u32[]{:S(2)}) %collective-permute-start.17) | collective-permute-done | bytes 262176 | tf_op jit(solution)/shard_map/ppermute | solution.py:55
  144.8 3.1 %collective-permute-start.22 = (f32[128,512]{1,0:T(8,128)S(1)}, f32[128,512]{1,0:T(8,128)S(1)}, u32[]{:S(2)}, u32[]{:S(2)}) collective-permute-start(f32[128,512]{1,0:T(8,128)S(1)} %merge.11), channel_id=1, source_target_pairs={{0,14},{1,15},{2,0},{3,1},{4,2},{5,3},{6,4},{7,5},{8,6},{9,7},{10,... | collective-permute-start | bytes 786440 | tf_op jit(solution)/shard_map/ppermute | solution.py:55
  148.0 0.7 subtract_bitcast_fusion
  148.9 3.3 %collective-permute-done.18.ahead = f32[128,512]{1,0:T(8,128)S(1)} collective-permute-done((f32[128,512]{1,0:T(8,128)S(1)}, f32[128,512]{1,0:T(8,128)S(1)}, u32[]{:S(2)}, u32[]{:S(2)}) %collective-permute-start.18) | collective-permute-done | bytes 262176 | tf_op jit(solution)/shard_map/ppermute | solution.py:55
  152.4 1.9 %collective-permute-start.23 = (bf16[512,128]{1,0:T(8,128)(2,1)S(1)}, bf16[512,128]{1,0:T(8,128)(2,1)S(1)}, u32[]{:S(2)}, u32[]{:S(2)}) collective-permute-start(bf16[512,128]{1,0:T(8,128)(2,1)S(1)} %finish.1), channel_id=1, source_target_pairs={{0,0},{1,48},{2,1},{3,49},{4,4},{5,52},{6,5},{7,53},{8,8},{9,56},{... | collective-permute-start | bytes 393224 | tf_op jit(solution)/shard_map/ppermute | solution.py:55
  154.3 7.6 %collective-permute-done.23 = bf16[512,128]{1,0:T(8,128)(2,1)S(1)} collective-permute-done((bf16[512,128]{1,0:T(8,128)(2,1)S(1)}, bf16[512,128]{1,0:T(8,128)(2,1)S(1)}, u32[]{:S(2)}, u32[]{:S(2)}) %collective-permute-start.23) | collective-permute-done | bytes 131104 | tf_op jit(solution)/shard_map/ppermute | solution.py:55
  161.9 0.7 copy.10
  (46 shorter events, 1.5 us)
Async XLA Ops:
  4.9 41.9 %collective-permute-start = (bf16[192,3072]{1,0:T(8,128)(2,1)}, bf16[192,3072]{1,0:T(8,128)(2,1)S(1)}, u32[]{:S(2)}, u32[]{:S(2)}) collective-permute-start(bf16[192,3072]{1,0:T(8,128)(2,1)} %get-tuple-element.17.near), channel_id=1, source_target_pairs={{0,16},{1,17},{2,18},{3,19},{4,20},{5,21},{6,22},{7,23},{8,24},{9,... | collective-permute-start | bytes 3538952 | tf_op jit(solution)/shard_map/ppermute | solution.py:55
  6.4 12.0 %collective-permute-start.4 = (bf16[192,1024]{1,0:T(8,128)(2,1)}, bf16[192,1024]{1,0:T(8,128)(2,1)S(1)}, u32[]{:S(2)}, u32[]{:S(2)}) collective-permute-start(bf16[192,1024]{1,0:T(8,128)(2,1)} %get-tuple-element.21.own), channel_id=1, source_target_pairs={{0,48},{1,49},{2,50},{3,51},{4,52},{5,53},{6,54},{7,55},{8,56},{9,... | collective-permute-start | bytes 1179656 | tf_op jit(solution)/shard_map/ppermute | solution.py:55
  8.5 35.0 %collective-permute-start.1 = (bf16[2,192,1024]{2,1,0:T(8,128)(2,1)}, bf16[2,192,1024]{2,1,0:T(8,128)(2,1)S(1)}, u32[]{:S(2)}, u32[]{:S(2)}) collective-permute-start(bf16[2,192,1024]{2,1,0:T(8,128)(2,1)} %get-tuple-element.18), channel_id=1, source_target_pairs={{0,64},{1,65},{2,66},{3,67},{4,68},{5,69},{6,70},{7,71},{8,72},{9,... | collective-permute-start | bytes 2359304 | tf_op jit(solution)/shard_map/ppermute | solution.py:55
  10.1 33.4 %collective-permute-start.2 = (bf16[2,192,1024]{2,1,0:T(8,128)(2,1)}, bf16[2,192,1024]{2,1,0:T(8,128)(2,1)S(1)}, u32[]{:S(2)}, u32[]{:S(2)}) collective-permute-start(bf16[2,192,1024]{2,1,0:T(8,128)(2,1)} %get-tuple-element.19), channel_id=1, source_target_pairs={{0,192},{1,193},{2,194},{3,195},{4,196},{5,197},{6,198},{7,199},{8... | collective-permute-start | bytes 2359304 | tf_op jit(solution)/shard_map/ppermute | solution.py:55
  11.8 35.0 %collective-permute-start.3 = (bf16[2,192,1024]{2,1,0:T(8,128)(2,1)}, bf16[2,192,1024]{2,1,0:T(8,128)(2,1)S(1)}, u32[]{:S(2)}, u32[]{:S(2)}) collective-permute-start(bf16[2,192,1024]{2,1,0:T(8,128)(2,1)} %get-tuple-element.20), channel_id=1, source_target_pairs={{0,128},{1,129},{2,130},{3,131},{4,132},{5,133},{6,134},{7,135},{8... | collective-permute-start | bytes 2359304 | tf_op jit(solution)/shard_map/ppermute | solution.py:55
  18.4 1.0 copy-start.6
  19.5 24.0 %collective-permute-start.5 = (bf16[192,1024]{1,0:T(8,128)(2,1)S(1)}, bf16[192,1024]{1,0:T(8,128)(2,1)S(1)}, u32[]{:S(2)}, u32[]{:S(2)}) collective-permute-start(bf16[192,1024]{1,0:T(8,128)(2,1)S(1)} %follow.1), channel_id=1, source_target_pairs={{0,32},{1,33},{2,34},{3,35},{4,36},{5,37},{6,38},{7,39},{8,40},{9,... | collective-permute-start | bytes 1179656 | tf_op jit(solution)/shard_map/ppermute | solution.py:55
  46.8 1.3 copy-start.4
  48.1 1.0 copy-start.5
  50.9 38.1 %copy-start.2 = (bf16[256,3072]{1,0:T(8,128)(2,1)}, bf16[256,3072]{1,0:T(8,128)(2,1)S(1)}, u32[]{:S(2)}) copy-start(bf16[256,3072]{1,0:T(8,128)(2,1)S(1)} %get-tuple-element.23.here) | copy-start | bytes 4718596
  50.9 34.6 %collective-permute-start.7 = (bf16[256,3072]{1,0:T(8,128)(2,1)S(1)}, bf16[256,3072]{1,0:T(8,128)(2,1)S(1)}, u32[]{:S(2)}, u32[]{:S(2)}) collective-permute-start(bf16[256,3072]{1,0:T(8,128)(2,1)S(1)} %get-tuple-element.23.here), channel_id=1, source_target_pairs={{0,192},{1,193},{2,194},{3,195},{4,196},{5,197},{6,198},{7,199},{8... | collective-permute-start | bytes 4718600 | tf_op jit(solution)/shard_map/ppermute | solution.py:55
  52.7 35.1 %collective-permute-start.6 = (bf16[256,3072]{1,0:T(8,128)(2,1)S(1)}, bf16[256,3072]{1,0:T(8,128)(2,1)S(1)}, u32[]{:S(2)}, u32[]{:S(2)}) collective-permute-start(bf16[256,3072]{1,0:T(8,128)(2,1)S(1)} %get-tuple-element.23.here), channel_id=1, source_target_pairs={{0,64},{1,65},{2,66},{3,67},{4,68},{5,69},{6,70},{7,71},{8,72},{9,... | collective-permute-start | bytes 4718600 | tf_op jit(solution)/shard_map/ppermute | solution.py:55
  53.0 40.6 %collective-permute-start.12 = (bf16[3,192,1024]{2,1,0:T(8,128)(2,1)}, bf16[3,192,1024]{2,1,0:T(8,128)(2,1)}, u32[]{:S(2)}, u32[]{:S(2)}) collective-permute-start(bf16[3,192,1024]{2,1,0:T(8,128)(2,1)} %get-tuple-element.28), channel_id=1, source_target_pairs={{0,32},{1,33},{2,34},{3,35},{4,36},{5,37},{6,38},{7,39},{8,40},{9,... | collective-permute-start | bytes 3538952 | tf_op jit(solution)/shard_map/ppermute | solution.py:55
  53.9 50.4 %collective-permute-start.11 = (bf16[3,192,1024]{2,1,0:T(8,128)(2,1)}, bf16[3,192,1024]{2,1,0:T(8,128)(2,1)}, u32[]{:S(2)}, u32[]{:S(2)}) collective-permute-start(bf16[3,192,1024]{2,1,0:T(8,128)(2,1)} %get-tuple-element.28), channel_id=1, source_target_pairs={{0,16},{1,17},{2,18},{3,19},{4,20},{5,21},{6,22},{7,23},{8,24},{9,... | collective-permute-start | bytes 3538952 | tf_op jit(solution)/shard_map/ppermute | solution.py:55
  55.0 50.8 %collective-permute-start.10 = (bf16[3,192,1024]{2,1,0:T(8,128)(2,1)}, bf16[3,192,1024]{2,1,0:T(8,128)(2,1)}, u32[]{:S(2)}, u32[]{:S(2)}) collective-permute-start(bf16[3,192,1024]{2,1,0:T(8,128)(2,1)} %get-tuple-element.27.own_rest), channel_id=1, source_target_pairs={{0,48},{1,49},{2,50},{3,51},{4,52},{5,53},{6,54},{7,55},{8,56},{9,... | collective-permute-start | bytes 3538952 | tf_op jit(solution)/shard_map/ppermute | solution.py:55
  89.1 1.2 copy-start
  90.2 18.2 %collective-permute-start.8 = (bf16[128,3072]{1,0:T(8,128)(2,1)}, bf16[128,3072]{1,0:T(8,128)(2,1)}, u32[]{:S(2)}, u32[]{:S(2)}) collective-permute-start(bf16[128,3072]{1,0:T(8,128)(2,1)} %get-tuple-element.24), channel_id=1, source_target_pairs={{0,64},{1,65},{2,66},{3,67},{4,68},{5,69},{6,70},{7,71},{8,72},{9,... | collective-permute-start | bytes 2359304 | tf_op jit(solution)/shard_map/ppermute | solution.py:55
  90.2 18.2 %collective-permute-start.9 = (bf16[128,3072]{1,0:T(8,128)(2,1)}, bf16[128,3072]{1,0:T(8,128)(2,1)}, u32[]{:S(2)}, u32[]{:S(2)}) collective-permute-start(bf16[128,3072]{1,0:T(8,128)(2,1)} %get-tuple-element.25), channel_id=1, source_target_pairs={{0,192},{1,193},{2,194},{3,195},{4,196},{5,197},{6,198},{7,199},{8... | collective-permute-start | bytes 2359304 | tf_op jit(solution)/shard_map/ppermute | solution.py:55
  105.7 2.7 %copy-start.1 = (bf16[256,3072]{1,0:T(8,128)(2,1)S(1)}, bf16[256,3072]{1,0:T(8,128)(2,1)}, u32[]{:S(2)}) copy-start(bf16[256,3072]{1,0:T(8,128)(2,1)} %copy-done) | copy-start | bytes 4718596
  105.7 2.8 %copy-start.3 = (bf16[256,3072]{1,0:T(8,128)(2,1)S(1)}, bf16[256,3072]{1,0:T(8,128)(2,1)}, u32[]{:S(2)}) copy-start(bf16[256,3072]{1,0:T(8,128)(2,1)} %copy-done.2) | copy-start | bytes 4718596
  113.9 7.2 %collective-permute-start.13 = (f32[896,512]{1,0:T(8,128)S(1)}, f32[896,512]{1,0:T(8,128)S(1)}, u32[]{:S(2)}, u32[]{:S(2)}) collective-permute-start(f32[896,512]{1,0:T(8,128)S(1)} %fusion), channel_id=1, source_target_pairs={{0,1},{1,0},{2,3},{3,2},{4,5},{5,4},{6,7},{7,6},{8,9},{9,8},{10,11... | collective-permute-start | bytes 5505032 | tf_op jit(solution)/shard_map/ppermute | solution.py:55
  114.7 3.6 %collective-permute-start.14 = (f32[128,512]{1,0:T(8,128)S(1)}, f32[128,512]{1,0:T(8,128)S(1)}, u32[]{:S(2)}, u32[]{:S(2)}) collective-permute-start(f32[128,512]{1,0:T(8,128)S(1)} %fusion.7), channel_id=1, source_target_pairs={{0,1},{1,0},{2,3},{3,2},{4,5},{5,4},{6,7},{7,6},{8,9},{9,8},{10,11... | collective-permute-start | bytes 786440 | tf_op jit(solution)/shard_map/ppermute | solution.py:55
  118.9 9.7 %collective-permute-start.19 = (f32[64,512]{1,0:T(8,128)S(1)}, f32[64,512]{1,0:T(8,128)S(1)}, u32[]{:S(2)}, u32[]{:S(2)}) collective-permute-start(f32[64,512]{1,0:T(8,128)S(1)} %get-tuple-element.29), channel_id=1, source_target_pairs={{0,14},{1,15},{2,0},{3,1},{4,2},{5,3},{6,4},{7,5},{8,6},{9,7},{10,... | collective-permute-start | bytes 393224 | tf_op jit(solution)/shard_map/ppermute | solution.py:55
  119.1 9.4 %collective-permute-start.15 = (f32[64,512]{1,0:T(8,128)S(1)}, f32[64,512]{1,0:T(8,128)S(1)}, u32[]{:S(2)}, u32[]{:S(2)}) collective-permute-start(f32[64,512]{1,0:T(8,128)S(1)} %get-tuple-element.30), channel_id=1, source_target_pairs={{0,2},{1,3},{2,4},{3,5},{4,6},{5,7},{6,8},{7,9},{8,10},{9,11},{10,... | collective-permute-start | bytes 393224 | tf_op jit(solution)/shard_map/ppermute | solution.py:55
  128.5 11.7 %copy-start.8 = (f32[4]{0:T(128)S(1)}, f32[4]{0:T(128)}, u32[]{:S(2)}) copy-start(f32[4]{0:T(128)} %param.12) | copy-start | bytes 52
  128.5 8.5 %collective-permute-start.16 = (f32[128,512]{1,0:T(8,128)S(1)}, f32[128,512]{1,0:T(8,128)S(1)}, u32[]{:S(2)}, u32[]{:S(2)}) collective-permute-start(f32[128,512]{1,0:T(8,128)S(1)} %merge.6), channel_id=1, source_target_pairs={{0,2},{1,3},{2,4},{3,5},{4,6},{5,7},{6,8},{7,9},{8,10},{9,11},{10,... | collective-permute-start | bytes 786440 | tf_op jit(solution)/shard_map/ppermute | solution.py:55
  128.7 8.5 %collective-permute-start.20 = (f32[128,512]{1,0:T(8,128)S(1)}, f32[128,512]{1,0:T(8,128)S(1)}, u32[]{:S(2)}, u32[]{:S(2)}) collective-permute-start(f32[128,512]{1,0:T(8,128)S(1)} %merge.9), channel_id=1, source_target_pairs={{0,14},{1,15},{2,0},{3,1},{4,2},{5,3},{6,4},{7,5},{8,6},{9,7},{10,... | collective-permute-start | bytes 786440 | tf_op jit(solution)/shard_map/ppermute | solution.py:55
  137.1 10.9 %copy-start.7 = (f32[4,128]{1,0:T(4,128)S(1)}, f32[4,128]{1,0:T(4,128)}, u32[]{:S(2)}) copy-start(f32[4,128]{1,0:T(4,128)} %param.13) | copy-start | bytes 6148
  137.1 11.7 %copy-start.9 = (f32[16]{0:T(128)S(1)}, f32[16]{0:T(128)}, u32[]{:S(2)}) copy-start(f32[16]{0:T(128)} %param.11) | copy-start | bytes 196
  137.1 7.6 %collective-permute-start.17 = (f32[128,512]{1,0:T(8,128)S(1)}, f32[128,512]{1,0:T(8,128)S(1)}, u32[]{:S(2)}, u32[]{:S(2)}) collective-permute-start(f32[128,512]{1,0:T(8,128)S(1)} %merge.7), channel_id=1, source_target_pairs={{0,2},{1,3},{2,4},{3,5},{4,6},{5,7},{6,8},{7,9},{8,10},{9,11},{10,... | collective-permute-start | bytes 786440 | tf_op jit(solution)/shard_map/ppermute | solution.py:55
  137.2 7.6 %collective-permute-start.21 = (f32[128,512]{1,0:T(8,128)S(1)}, f32[128,512]{1,0:T(8,128)S(1)}, u32[]{:S(2)}, u32[]{:S(2)}) collective-permute-start(f32[128,512]{1,0:T(8,128)S(1)} %merge.10), channel_id=1, source_target_pairs={{0,14},{1,15},{2,0},{3,1},{4,2},{5,3},{6,4},{7,5},{8,6},{9,7},{10,... | collective-permute-start | bytes 786440 | tf_op jit(solution)/shard_map/ppermute | solution.py:55
  144.7 7.5 %collective-permute-start.18 = (f32[128,512]{1,0:T(8,128)S(1)}, f32[128,512]{1,0:T(8,128)S(1)}, u32[]{:S(2)}, u32[]{:S(2)}) collective-permute-start(f32[128,512]{1,0:T(8,128)S(1)} %merge.8), channel_id=1, source_target_pairs={{0,2},{1,3},{2,4},{3,5},{4,6},{5,7},{6,8},{7,9},{8,10},{9,11},{10,... | collective-permute-start | bytes 786440 | tf_op jit(solution)/shard_map/ppermute | solution.py:55
  144.8 7.3 %collective-permute-start.22 = (f32[128,512]{1,0:T(8,128)S(1)}, f32[128,512]{1,0:T(8,128)S(1)}, u32[]{:S(2)}, u32[]{:S(2)}) collective-permute-start(f32[128,512]{1,0:T(8,128)S(1)} %merge.11), channel_id=1, source_target_pairs={{0,14},{1,15},{2,0},{3,1},{4,2},{5,3},{6,4},{7,5},{8,6},{9,7},{10,... | collective-permute-start | bytes 786440 | tf_op jit(solution)/shard_map/ppermute | solution.py:55
  152.4 9.5 %collective-permute-start.23 = (bf16[512,128]{1,0:T(8,128)(2,1)S(1)}, bf16[512,128]{1,0:T(8,128)(2,1)S(1)}, u32[]{:S(2)}, u32[]{:S(2)}) collective-permute-start(bf16[512,128]{1,0:T(8,128)(2,1)S(1)} %finish.1), channel_id=1, source_target_pairs={{0,0},{1,48},{2,1},{3,49},{4,4},{5,52},{6,5},{7,53},{8,8},{9,56},{... | collective-permute-start | bytes 393224 | tf_op jit(solution)/shard_map/ppermute | solution.py:55
